TPU v7x, 32 devices: a whole 2x2x4 slice. The times are simulated.
32 devices in a mesh: wide: 8 (over z, core), narrow: 4 (over y, x).
Axes of the slice: x: 2, y: 2, z: 4, core: 2. Of those that a mesh axis runs over, the one named last changes fastest.
Arguments:
- series: bfloat16 [12288, 3600], P(('wide', 'narrow')), may hold values from -6 to 6
- padding: int32 [12288], P('wide'), may hold values from 0 to 1800, as said below
- coarse_first: bfloat16 [512, 900], P(('wide', 'narrow')), may hold values from -0.1875 to 0.1875
- coarse_first_bias: float32 [512], replicated, may hold values from -3 to 3
- coarse_second: bfloat16 [512, 512], P(('wide', 'narrow')), may hold values from -0.25 to 0.25
- coarse_second_bias: float32 [512], replicated, may hold values from -3 to 3
- coarse_third: bfloat16 [512, 512], P(('wide', 'narrow')), may hold values from -0.25 to 0.25
- coarse_third_bias: float32 [512], replicated, may hold values from -3 to 3
- coarse_basis: bfloat16 [512, 360], P(('wide', 'narrow')), may hold values from -0.25 to 0.25
- coarse_basis_bias: float32 [360], replicated, may hold values from -3 to 3
- fine_first: bfloat16 [512, 3600], P('wide', 'narrow'), may hold values from -0.09375 to 0.09375
- fine_first_bias: float32 [512], replicated, may hold values from -3 to 3
- fine_second: bfloat16 [512, 512], P(('wide', 'narrow')), may hold values from -0.25 to 0.25
- fine_second_bias: float32 [512], replicated, may hold values from -3 to 3
- fine_third: bfloat16 [512, 512], P(('wide', 'narrow')), may hold values from -0.25 to 0.25
- fine_third_bias: float32 [512], replicated, may hold values from -3 to 3
- fine_back: bfloat16 [512, 3600], P('wide', 'narrow'), may hold values from -0.25 to 0.25
- fine_back_bias: float32 [3600], replicated, may hold values from -3 to 3
- fine_fore: bfloat16 [512, 720], P('wide', 'narrow'), may hold values from -0.25 to 0.25
- detailed_predict_offset: float32 [720], replicated, may hold values from -3 to 3
- grad_resid: bfloat16 [12288, 3600], P('wide', 'narrow'), may hold values from -6 to 6
- future_cotangent_array: bfloat16 [12288, 720], P('wide', 'narrow'), may hold values from -6 to 6
Outputs:
- leftover_signal: bfloat16 [12288, 3600], P('wide', 'narrow')
- predicted_future: float32 [12288, 720], P('wide', 'narrow')
- temporal_input_derivative: bfloat16 [12288, 3600], P(('wide', 'narrow'))
- grad_coarse_first: float32 [512, 900], P(('wide', 'narrow'))
- grad_coarse_first_bias: float32 [512], replicated
- grad_coarse_second: float32 [512, 512], P(('wide', 'narrow'))
- grad_coarse_second_bias: float32 [512], replicated
- grad_coarse_third: float32 [512, 512], P(('wide', 'narrow'))
- grad_coarse_third_bias: float32 [512], replicated
- grad_coarse_basis: float32 [512, 360], P(('wide', 'narrow'))
- grad_coarse_basis_bias: float32 [360], replicated
- grad_fine_first: float32 [512, 3600], P('wide', 'narrow')
- grad_fine_first_bias: float32 [512], replicated
- grad_fine_second: float32 [512, 512], P(('wide', 'narrow'))
- grad_fine_second_bias: float32 [512], replicated
- grad_fine_third: float32 [512, 512], P(('wide', 'narrow'))
- grad_fine_third_bias: float32 [512], replicated
- grad_fine_back: float32 [512, 3600], P('wide', 'narrow')
- grad_fine_back_bias: float32 [3600], replicated
- grad_fine_fore: float32 [512, 720], P('wide', 'narrow')
- grad_fine_fore_bias: float32 [720], replicated
Inputs may be any that keep to these rules, and one draw needn't show every extreme that they name: padding[r] counts the leading padded steps of window r: its mask is 1 at steps t >= padding[r] and 0 before.
All inputs are finite; a program needn't handle non-finite values.
Results may differ from a plain program's by a relative error of at most 0.017.
Values may be sent and summed in bfloat16 or wider, within the bound.
A program may use at most 192 MiB of HBM per device.

v0:
```python
import jax
import jax.numpy as jnp
from jax import lax
from jax.sharding import PartitionSpec as P

L = 3600
AHEAD_TIMES = 720
POOL = 4
KB = 300
MINIBATCHES = 4


def upsample(coef, length):
    coef_count = coef.shape[1]
    stride = length // coef_count
    halfway = stride // 2
    padded = jnp.concatenate([coef[:, :1], coef, coef[:, -1:]], axis=1)
    preceding = jnp.repeat(padded[:, :coef_count], stride, axis=1)
    central = jnp.repeat(padded[:, 1 : coef_count + 1], stride, axis=1)
    following = jnp.repeat(padded[:, 2:], stride, axis=1)
    offsets = jnp.arange(length, dtype=jnp.int32) % stride
    in_front = offsets < halfway
    fraction = (
        jnp.where(in_front, offsets + halfway, offsets - halfway).astype(jnp.float32) + 0.5
    ) / stride
    lower_val = jnp.where(in_front[None, :], preceding, central)
    upper_val = jnp.where(in_front[None, :], central, following)
    return lower_val * (1.0 - fraction) + upper_val * fraction


def silu_slope(value):
    sigma = jax.nn.sigmoid(value)
    return sigma * (1.0 + value * (1.0 - sigma))


def project_rows(rows_in, matrix):
    return lax.dot_general(
        rows_in, matrix, (((1,), (1,)), ((), ())), preferred_element_type=jnp.float32
    )


def apply_rows(rows_in, matrix):
    return jnp.dot(rows_in, matrix, preferred_element_type=jnp.float32)


def column_outer(first_rows, second_rows):
    return lax.dot_general(
        first_rows, second_rows, (((0,), (0,)), ((), ())), preferred_element_type=jnp.float32
    )


def own_slice(values, begin, amount):
    return lax.dynamic_slice_in_dim(values, begin, amount, 0)


def column_sums(values):
    return jnp.sum(values.astype(jnp.float32), axis=0)


def on_device(
    series,
    padding,
    coarse_first,
    coarse_first_bias,
    coarse_second,
    coarse_second_bias,
    coarse_third,
    coarse_third_bias,
    coarse_basis,
    coarse_basis_bias,
    fine_first,
    fine_first_bias,
    fine_second,
    fine_second_bias,
    fine_third,
    fine_third_bias,
    fine_back,
    fine_back_bias,
    fine_fore,
    detailed_predict_offset,
    grad_resid,
    future_cotangent_array,
):
    slim_breadth = lax.axis_size("narrow")
    slim_position = lax.axis_index("narrow")
    onsite_tally = series.shape[0]
    sample_group = onsite_tally // MINIBATCHES
    piece = L // slim_breadth
    predicted_portion = AHEAD_TIMES // slim_breadth
    group_pads = padding.reshape(slim_breadth, onsite_tally)
    own_pads = lax.dynamic_slice_in_dim(group_pads, slim_position, 1, 0)[0]
    steps_all = jnp.arange(L, dtype=jnp.int32)
    time_start = slim_position * piece
    predict_onset = slim_position * predicted_portion
    steps_piece = time_start + jnp.arange(piece, dtype=jnp.int32)
    back_bias = lax.dynamic_slice_in_dim(fine_back_bias, time_start, piece, 0)
    predict_offset = lax.dynamic_slice_in_dim(
        detailed_predict_offset, predict_onset, predicted_portion, 0
    )
    resid_grid = grad_resid.reshape(slim_breadth, MINIBATCHES, sample_group, piece)
    predict_mesh = future_cotangent_array.reshape(
        slim_breadth, MINIBATCHES, sample_group, predicted_portion
    )
    own_start = slim_position * sample_group
    coarse_local = (
        coarse_first,
        coarse_second,
        coarse_third,
        coarse_basis,
        fine_second,
        fine_third,
    )
    fine_local = (fine_first, fine_back, fine_fore)
    totals = tuple((jnp.zeros(w.shape, jnp.float32) for w in coarse_local))
    fine_totals = tuple((jnp.zeros(w.shape, jnp.float32) for w in fine_local))
    bias_totals = tuple(
        (
            jnp.zeros(b.shape, jnp.float32)
            for b in (
                coarse_first_bias,
                coarse_second_bias,
                coarse_third_bias,
                coarse_basis_bias,
                fine_first_bias,
                fine_second_bias,
                fine_third_bias,
                fine_back_bias,
                detailed_predict_offset,
            )
        )
    )
    residual_parts = []
    predicted_portions = []
    grad_parts = []
    for iteration_index in range(MINIBATCHES):
        shared = (
            lax.all_gather(coarse_first, ("wide", "narrow"), axis=0, tiled=True),
            lax.all_gather(coarse_second, ("wide", "narrow"), axis=0, tiled=True),
            lax.all_gather(coarse_third, ("wide", "narrow"), axis=0, tiled=True),
            lax.all_gather(coarse_basis, ("wide", "narrow"), axis=0, tiled=True),
            lax.all_gather(fine_second, ("wide", "narrow"), axis=0, tiled=True),
            lax.all_gather(fine_third, ("wide", "narrow"), axis=0, tiled=True),
        )
        pieces = (
            lax.all_gather(fine_first, "wide", axis=0, tiled=True),
            lax.all_gather(fine_back, "wide", axis=0, tiled=True),
            lax.all_gather(fine_fore, "wide", axis=0, tiled=True),
        )
        weight_one, weight_two, weight_three, weight_basis, inner_two, inner_three = shared
        inner_one, inner_back, inner_fore = pieces
        lower = iteration_index * sample_group
        mask = (steps_all[None, :] >= own_pads[lower : lower + sample_group, None]).astype(
            jnp.float32
        )
        started = series[lower : lower + sample_group].astype(jnp.float32) * mask
        pooled = jnp.mean(started.reshape(sample_group, L // POOL, POOL), axis=2).astype(
            jnp.bfloat16
        )
        linear_one = project_rows(pooled, weight_one) + coarse_first_bias
        hidden_one = jax.nn.silu(linear_one).astype(jnp.bfloat16)
        linear_two = project_rows(hidden_one, weight_two) + coarse_second_bias
        hidden_two = jax.nn.silu(linear_two).astype(jnp.bfloat16)
        linear_three = project_rows(hidden_two, weight_three) + coarse_third_bias
        hidden_three = jax.nn.silu(linear_three).astype(jnp.bfloat16)
        theta = apply_rows(hidden_three, weight_basis) + coarse_basis_bias
        backcast = upsample(theta[:, :KB], L)
        coarse_fore = upsample(theta[:, KB:], AHEAD_TIMES)
        residual_here = (started - backcast) * mask
        sent_resid, sent_fore = (
            lax.all_to_all(
                residual_here.astype(jnp.bfloat16),
                "narrow",
                split_axis=1,
                concat_axis=0,
                tiled=True,
            ),
            lax.all_to_all(
                coarse_fore.astype(jnp.bfloat16), "narrow", split_axis=1, concat_axis=0, tiled=True
            ),
        )
        pads_here = group_pads[:, lower : lower + sample_group].reshape(-1)
        piece_mask = (steps_piece[None, :] >= pads_here[:, None]).astype(jnp.float32)
        first_partial = project_rows(sent_resid, inner_one)
        lift_one = lax.psum(first_partial, "narrow") + fine_first_bias
        fine_one = jax.nn.silu(lift_one).astype(jnp.bfloat16)
        lift_two = project_rows(fine_one, inner_two) + fine_second_bias
        fine_two = jax.nn.silu(lift_two).astype(jnp.bfloat16)
        lift_three = project_rows(fine_two, inner_three) + fine_third_bias
        fine_three = jax.nn.silu(lift_three).astype(jnp.bfloat16)
        coef_back = apply_rows(fine_three, inner_back) + back_bias
        coef_fore = apply_rows(fine_three, inner_fore) + predict_offset
        residual_parts.append(
            ((sent_resid.astype(jnp.float32) - coef_back) * piece_mask)
            .astype(jnp.bfloat16)
            .reshape(slim_breadth, sample_group, piece)
        )
        predicted_portions.append(
            (sent_fore.astype(jnp.float32) + coef_fore).reshape(
                slim_breadth, sample_group, predicted_portion
            )
        )
        out_grad = (
            resid_grid[:, iteration_index]
            .reshape(slim_breadth * sample_group, piece)
            .astype(jnp.float32)
        )
        predict_cotan = predict_mesh[:, iteration_index].reshape(
            slim_breadth * sample_group, predicted_portion
        )
        back_grad = (-out_grad * piece_mask).astype(jnp.bfloat16)
        coef_partial = project_rows(back_grad, inner_back) + project_rows(predict_cotan, inner_fore)
        three_grad = lax.psum(coef_partial, "narrow")
        lift_three_grad = (three_grad * silu_slope(lift_three)).astype(jnp.bfloat16)
        lift_two_grad = (apply_rows(lift_three_grad, inner_three) * silu_slope(lift_two)).astype(
            jnp.bfloat16
        )
        lift_one_grad = (apply_rows(lift_two_grad, inner_two) * silu_slope(lift_one)).astype(
            jnp.bfloat16
        )
        own_one_grad = own_slice(lift_one_grad, own_start, sample_group)
        own_two_grad = own_slice(lift_two_grad, own_start, sample_group)
        own_three_grad = own_slice(lift_three_grad, own_start, sample_group)
        own_fine_one = own_slice(fine_one, own_start, sample_group)
        own_fine_two = own_slice(fine_two, own_start, sample_group)
        sent_grad = (out_grad * piece_mask + apply_rows(lift_one_grad, inner_one)).astype(
            jnp.bfloat16
        )
        resid_back, fore_back = (
            lax.all_to_all(sent_grad, "narrow", split_axis=0, concat_axis=1, tiled=True),
            lax.all_to_all(predict_cotan, "narrow", split_axis=0, concat_axis=1, tiled=True),
        )
        grad_inner_one = column_outer(lift_one_grad, sent_resid)
        grad_inner_back = column_outer(fine_three, back_grad)
        grad_inner_fore = column_outer(fine_three, predict_cotan)
        grad_inner_two = column_outer(own_two_grad, own_fine_one)
        grad_inner_three = column_outer(own_three_grad, own_fine_two)
        resid_grad = resid_back.astype(jnp.float32)
        back_pull = jax.vjp(lambda coef: upsample(coef, L), theta[:, :KB])[1]
        fore_pull = jax.vjp(lambda coef: upsample(coef, AHEAD_TIMES), theta[:, KB:])[1]
        back_coef_grad = back_pull(-resid_grad * mask)[0]
        fore_coef_grad = fore_pull(fore_back.astype(jnp.float32))[0]
        theta_grad = jnp.concatenate([back_coef_grad, fore_coef_grad], axis=1).astype(jnp.bfloat16)
        coarse_three_grad = (
            project_rows(theta_grad, weight_basis) * silu_slope(linear_three)
        ).astype(jnp.bfloat16)
        coarse_two_grad = (
            apply_rows(coarse_three_grad, weight_three) * silu_slope(linear_two)
        ).astype(jnp.bfloat16)
        coarse_one_grad = (apply_rows(coarse_two_grad, weight_two) * silu_slope(linear_one)).astype(
            jnp.bfloat16
        )
        pooled_grad = apply_rows(coarse_one_grad, weight_one)
        start_grad = resid_grad * mask + jnp.repeat(pooled_grad, POOL, axis=1) / POOL
        grad_parts.append((start_grad * mask).astype(jnp.bfloat16))
        grad_weight_one = column_outer(coarse_one_grad, pooled)
        grad_weight_two = column_outer(coarse_two_grad, hidden_one)
        grad_weight_three = column_outer(coarse_three_grad, hidden_two)
        grad_weight_basis = column_outer(hidden_three, theta_grad)
        bias_terms = (
            column_sums(coarse_one_grad),
            column_sums(coarse_two_grad),
            column_sums(coarse_three_grad),
            column_sums(theta_grad),
            column_sums(own_one_grad),
            column_sums(own_two_grad),
            column_sums(own_three_grad),
            lax.dynamic_update_slice_in_dim(
                jnp.zeros((L,), jnp.float32), column_sums(back_grad), time_start, 0
            ),
            lax.dynamic_update_slice_in_dim(
                jnp.zeros((AHEAD_TIMES,), jnp.float32), column_sums(predict_cotan), predict_onset, 0
            ),
        )
        bias_totals = tuple((total + term for total, term in zip(bias_totals, bias_terms)))
        scattered = (
            lax.psum_scatter(grad_weight_one, ("wide", "narrow"), scatter_dimension=0, tiled=True),
            lax.psum_scatter(grad_weight_two, ("wide", "narrow"), scatter_dimension=0, tiled=True),
            lax.psum_scatter(
                grad_weight_three, ("wide", "narrow"), scatter_dimension=0, tiled=True
            ),
            lax.psum_scatter(
                grad_weight_basis, ("wide", "narrow"), scatter_dimension=0, tiled=True
            ),
            lax.psum_scatter(grad_inner_two, ("wide", "narrow"), scatter_dimension=0, tiled=True),
            lax.psum_scatter(grad_inner_three, ("wide", "narrow"), scatter_dimension=0, tiled=True),
        )
        spread = (
            lax.psum_scatter(
                grad_inner_one.astype(jnp.bfloat16), "wide", scatter_dimension=0, tiled=True
            ).astype(jnp.float32),
            lax.psum_scatter(
                grad_inner_back.astype(jnp.bfloat16), "wide", scatter_dimension=0, tiled=True
            ).astype(jnp.float32),
            lax.psum_scatter(
                grad_inner_fore.astype(jnp.bfloat16), "wide", scatter_dimension=0, tiled=True
            ).astype(jnp.float32),
        )
        totals = tuple((total + term for total, term in zip(totals, scattered)))
        fine_totals = tuple((total + term for total, term in zip(fine_totals, spread)))
    bias_sums = lax.psum(
        (
            bias_totals[0],
            bias_totals[1],
            bias_totals[2],
            bias_totals[3],
            bias_totals[4],
            bias_totals[5],
            bias_totals[6],
            bias_totals[7],
            bias_totals[8],
        ),
        ("wide", "narrow"),
    )
    leftover_signal = jnp.stack(residual_parts, axis=1).reshape(slim_breadth * onsite_tally, piece)
    predicted_future = jnp.stack(predicted_portions, axis=1).reshape(
        slim_breadth * onsite_tally, predicted_portion
    )
    temporal_input_derivative = jnp.concatenate(grad_parts, axis=0)
    return (
        leftover_signal,
        predicted_future,
        temporal_input_derivative,
        totals[0],
        bias_sums[0],
        totals[1],
        bias_sums[1],
        totals[2],
        bias_sums[2],
        totals[3],
        bias_sums[3],
        fine_totals[0],
        bias_sums[4],
        totals[4],
        bias_sums[5],
        totals[5],
        bias_sums[6],
        fine_totals[1],
        bias_sums[7],
        fine_totals[2],
        bias_sums[8],
    )


def solution(mesh):
    in_specs = (
        P(("wide", "narrow"), None),
        P("wide"),
        P(("wide", "narrow"), None),
        P(),
        P(("wide", "narrow"), None),
        P(),
        P(("wide", "narrow"), None),
        P(),
        P(("wide", "narrow"), None),
        P(),
        P("wide", "narrow"),
        P(),
        P(("wide", "narrow"), None),
        P(),
        P(("wide", "narrow"), None),
        P(),
        P("wide", "narrow"),
        P(),
        P("wide", "narrow"),
        P(),
        P("wide", "narrow"),
        P("wide", "narrow"),
    )
    out_specs = (
        P("wide", "narrow"),
        P("wide", "narrow"),
        P(("wide", "narrow"), None),
        P(("wide", "narrow"), None),
        P(),
        P(("wide", "narrow"), None),
        P(),
        P(("wide", "narrow"), None),
        P(),
        P(("wide", "narrow"), None),
        P(),
        P("wide", "narrow"),
        P(),
        P(("wide", "narrow"), None),
        P(),
        P(("wide", "narrow"), None),
        P(),
        P("wide", "narrow"),
        P(),
        P("wide", "narrow"),
        P(),
    )
    return jax.shard_map(
        on_device, mesh=mesh, in_specs=in_specs, out_specs=out_specs, check_vma=False
    )
```

profile of v0, /device:TPU:0, one launch (start us, length us, event | category | flops | bytes accessed | tf_op | source)
XLA Modules:
  0.0 1949.6 jit_solution(8421166244802407479)
XLA Ops:
  8.6 5.0 fusion.130
  20.4 75.6 %all_gather.18 = bf16[512,900]{1,0:T(8,128)(2,1)S(1)} all-gather(bf16[16,900]{1,0:T(8,128)(2,1)S(1)} %copy-done.190), channel_id=1, replica_groups=mesh['wide'=8,'narrow'=4] {'wide','narrow'}, dimensions={0}, use_global_device_ids=true | all-gather | bytes 950400 | tf_op jit(solution)/shard_map/all_gather | solution.py:137
  96.0 66.3 %all_gather.19 = bf16[512,512]{1,0:T(8,128)(2,1)S(1)} all-gather(bf16[16,512]{1,0:T(8,128)(2,1)S(1)} %copy-done.217), channel_id=1, replica_groups=mesh['wide'=8,'narrow'=4] {'wide','narrow'}, dimensions={0}, use_global_device_ids=true | all-gather | bytes 540672 | tf_op jit(solution)/shard_map/all_gather | solution.py:138
  162.3 68.8 %all_gather.20 = bf16[512,512]{1,0:T(8,128)(2,1)S(1)} all-gather(bf16[16,512]{1,0:T(8,128)(2,1)S(1)} %copy-done.218), channel_id=1, replica_groups=mesh['wide'=8,'narrow'=4] {'wide','narrow'}, dimensions={0}, use_global_device_ids=true | all-gather | bytes 540672 | tf_op jit(solution)/shard_map/all_gather | solution.py:139
  231.1 65.5 %all_gather.21 = bf16[512,360]{1,0:T(8,128)(2,1)S(1)} all-gather(bf16[16,360]{1,0:T(8,128)(2,1)S(1)} %copy-done.235), channel_id=1, replica_groups=mesh['wide'=8,'narrow'=4] {'wide','narrow'}, dimensions={0}, use_global_device_ids=true | all-gather | bytes 380160 | tf_op jit(solution)/shard_map/all_gather | solution.py:140
  396.9 7.0 select_convert_fusion.11
  451.3 6.7 slice_reduce_fusion.3
  458.2 14.2 all_gather.26
  472.5 17.3 all_gather.25
  489.8 4.6 copy.484
  494.4 4.8 slice_convert_fusion.1
  526.0 4.3 all-to-all-start.2
  545.0 17.2 all_gather.22
  562.2 4.4 all-to-all-start.3
  571.6 7.2 all-to-all-done.3
  578.8 4.2 all-to-all-start.1
  588.3 5.8 all-to-all-done.1
  630.5 74.2 %all_gather.23 = bf16[512,512]{1,0:T(8,128)(2,1)} all-gather(bf16[16,512]{1,0:T(8,128)(2,1)S(1)} %copy-done.219), channel_id=1, replica_groups=mesh['wide'=8,'narrow'=4] {'wide','narrow'}, dimensions={0}, use_global_device_ids=true | all-gather | bytes 540672 | tf_op jit(solution)/shard_map/all_gather | solution.py:141
  704.7 72.3 %all_gather.24 = bf16[512,512]{1,0:T(8,128)(2,1)} all-gather(bf16[16,512]{1,0:T(8,128)(2,1)S(1)} %copy-done.220), channel_id=1, replica_groups=mesh['wide'=8,'narrow'=4] {'wide','narrow'}, dimensions={0}, use_global_device_ids=true | all-gather | bytes 540672 | tf_op jit(solution)/shard_map/all_gather | solution.py:142
  841.4 5.8 convert_reduce_fusion.4
  1022.2 4.2 all-to-all-start.10
  1033.4 4.5 all-to-all-done.10
  1080.3 12.7 select_reduce_fusion.1
  1131.6 4.6 copy.517
  1233.1 4.4 pad_maximum_fusion.1
  1237.7 4.5 copy.518
  1242.8 39.6 %all-reduce.32 = (f32[512]{0:T(512)}, f32[512]{0:T(512)}, f32[512]{0:T(512)}, f32[360]{0:T(512)}, f32[512]{0:T(512)}, /*index=5*/f32[512]{0:T(512)}, f32[512]{0:T(512)}, f32[3600]{0:T(1024)}, f32[720]{0:T(1024)}) all-reduce(f32[512]{0:T(512)S(1)} %add_add_fusion.7, ...), channel_id=1, replica_groups=mesh['wide'=8,'narrow'=4] {'wide','narrow'}, use_global_device_ids=true, to_apply=%region_44.45 | all-reduce | flops 7752 | bytes 62016 | tf_op jit(solution)/shard_map/psum | solution.py:300
  1286.1 119.5 %reduce-scatter.53.cloned.1.call-done = f32[16,512]{1,0:T(8,128)} async-done(((f32[512,512]{1,0:T(8,128)}), f32[16,512]{1,0:T(8,128)}) %reduce-scatter.53.cloned.1.call-update) | async-done | bytes 32784 | tf_op jit(solution)/shard_map/reduce_scatter | solution.py:285
  1405.7 133.9 %reduce-scatter.51.cloned.1.call-done = f32[16,512]{1,0:T(8,128)} async-done(((f32[512,512]{1,0:T(8,128)}), f32[16,512]{1,0:T(8,128)}) %reduce-scatter.51.cloned.1.call-update) | async-done | bytes 32784 | tf_op jit(solution)/shard_map/reduce_scatter | solution.py:284
  1539.5 133.7 %reduce-scatter.47.cloned.1.call-done = f32[16,512]{1,0:T(8,128)} async-done(((f32[512,512]{1,0:T(8,128)}), f32[16,512]{1,0:T(8,128)}) %reduce-scatter.47.cloned.1.call-update) | async-done | bytes 32784 | tf_op jit(solution)/shard_map/reduce_scatter | solution.py:278
  1673.3 133.8 %reduce-scatter.45.cloned.1.call-done = f32[16,512]{1,0:T(8,128)} async-done(((f32[512,512]{1,0:T(8,128)}), f32[16,512]{1,0:T(8,128)}) %reduce-scatter.45.cloned.1.call-update) | async-done | bytes 32784 | tf_op jit(solution)/shard_map/reduce_scatter | solution.py:277
  1807.0 135.8 %reduce-scatter.43.cloned.1.call-done = f32[16,900]{1,0:T(8,128)} async-done(((f32[512,900]{1,0:T(8,128)}), f32[16,900]{1,0:T(8,128)}) %reduce-scatter.43.cloned.1.call-update) | async-done | bytes 57616 | tf_op jit(solution)/shard_map/reduce_scatter | solution.py:276
  (1018 shorter events, 669.9 us)
Async XLA Ops:
  407.9 118.1 %all-to-all-start = ((bf16[96,4,900]{2,0,1:T(8,128)(2,1)}), bf16[96,4,900]{2,0,1:T(8,128)(2,1)S(1)}, u32[]{:S(2)}, u32[]{:S(2)}) async-start(bf16[96,4,900]{2,0,1:T(8,128)(2,1)} %copy.424), calls=%async_computation | async-start | bytes 1572864 | tf_op jit(solution)/shard_map/all_to_all | solution.py:170
  526.0 36.2 %all-to-all-start.2 = ((bf16[96,4,900]{2,0,1:T(8,128)(2,1)}), bf16[96,4,900]{2,0,1:T(8,128)(2,1)}, u32[]{:S(2)}, u32[]{:S(2)}) async-start(bf16[96,4,900]{2,0,1:T(8,128)(2,1)} %copy.450), calls=%async_computation.2 | async-start | bytes 1572864 | tf_op jit(solution)/shard_map/all_to_all | solution.py:170
  562.2 16.6 all-to-all-start.3
  578.8 15.3 all-to-all-start.1
  583.0 194.0 %all-reduce.36.cloned.1.call-start = ((), (), s32[]{:S(2)}) async-start(), calls=%async_computation.52 | async-start | bytes 12582912 | tf_op jit(solution)/shard_map/psum | solution.py:184
  598.4 270.6 %all-to-all-start.9 = ((bf16[4,96,180]{1,2,0:T(8,128)(2,1)}), bf16[4,96,180]{1,2,0:T(8,128)(2,1)}, u32[]{:S(2)}, u32[]{:S(2)}) async-start(bf16[4,96,180]{1,2,0:T(8,128)(2,1)} %bitcast.368), calls=%async_computation.9 | async-start | bytes 376832 | tf_op jit(solution)/shard_map/all_to_all | solution.py:230
  602.4 559.1 %reduce-scatter.35.cloned.1.call-start = ((), (), s32[]{:S(2)}) async-start(), calls=%async_computation.42 | async-start | bytes 294912 | tf_op jit(solution)/shard_map/reduce_scatter | solution.py:294
  785.5 376.1 %reduce-scatter.37.cloned.1.call-start = ((), (), s32[]{:S(2)}) async-start(), calls=%async_computation.43 | async-start | bytes 294912 | tf_op jit(solution)/shard_map/reduce_scatter | solution.py:294
  794.0 367.6 %reduce-scatter.39.cloned.1.call-start = ((), (), s32[]{:S(2)}) async-start(), calls=%async_computation.44 | async-start | bytes 294912 | tf_op jit(solution)/shard_map/reduce_scatter | solution.py:294
  801.4 360.2 %reduce-scatter.41.cloned.1.call-start = ((), (), s32[]{:S(2)}) async-start(), calls=%async_computation.45 | async-start | bytes 294912 | tf_op jit(solution)/shard_map/reduce_scatter | solution.py:294
  806.2 476.2 %reduce-scatter.27.cloned.1.call-start = ((), (), s32[]{:S(2)}) async-start(), calls=%async_computation.38 | async-start | bytes 1179648 | tf_op jit(solution)/shard_map/reduce_scatter | solution.py:291
  818.2 464.1 %reduce-scatter.29.cloned.1.call-start = ((), (), s32[]{:S(2)}) async-start(), calls=%async_computation.39 | async-start | bytes 1179648 | tf_op jit(solution)/shard_map/reduce_scatter | solution.py:291
  854.5 427.9 %reduce-scatter.31.cloned.1.call-start = ((), (), s32[]{:S(2)}) async-start(), calls=%async_computation.40 | async-start | bytes 1179648 | tf_op jit(solution)/shard_map/reduce_scatter | solution.py:291
  887.5 9.6 all-to-all-start.15
  897.1 9.5 all-to-all-start.4
  910.7 371.7 %reduce-scatter.33.cloned.1.call-start = ((), (), s32[]{:S(2)}) async-start(), calls=%async_computation.41 | async-start | bytes 1179648 | tf_op jit(solution)/shard_map/reduce_scatter | solution.py:291
  915.9 9.3 all-to-all-start.6
  925.2 24.4 %all-to-all-start.7 = ((bf16[96,4,180]{0,2,1:T(8,128)(2,1)}), bf16[96,4,180]{0,2,1:T(8,128)(2,1)}, u32[]{:S(2)}, u32[]{:S(2)}) async-start(bf16[96,4,180]{0,2,1:T(8,128)(2,1)} %get-tuple-element.254), calls=%async_computation.7 | async-start | bytes 376832 | tf_op jit(solution)/shard_map/all_to_all | solution.py:177
  929.2 355.0 %reduce-scatter.21.cloned.1.call-start = ((), (), s32[]{:S(2)}) async-start(), calls=%async_computation.35 | async-start | bytes 1179648 | tf_op jit(solution)/shard_map/reduce_scatter | solution.py:288
  963.3 320.9 %reduce-scatter.23.cloned.1.call-start = ((), (), s32[]{:S(2)}) async-start(), calls=%async_computation.36 | async-start | bytes 1179648 | tf_op jit(solution)/shard_map/reduce_scatter | solution.py:288
  989.5 32.7 %all-to-all-start.12 = ((bf16[4,96,900]{2,1,0:T(8,128)(2,1)}), bf16[4,96,900]{2,1,0:T(8,128)(2,1)}, u32[]{:S(2)}, u32[]{:S(2)}) async-start(bf16[4,96,900]{2,1,0:T(8,128)(2,1)} %bitcast.358), calls=%async_computation.12 | async-start | bytes 1572864 | tf_op jit(solution)/shard_map/all_to_all | solution.py:229
  993.7 290.5 %reduce-scatter.19.cloned.1.call-start = ((), (), s32[]{:S(2)}) async-start(), calls=%async_computation.34 | async-start | bytes 1179648 | tf_op jit(solution)/shard_map/reduce_scatter | solution.py:288
  1022.2 15.7 all-to-all-start.10
  1026.5 257.8 %reduce-scatter.25.cloned.1.call-start = ((), (), s32[]{:S(2)}) async-start(), calls=%async_computation.37 | async-start | bytes 1179648 | tf_op jit(solution)/shard_map/reduce_scatter | solution.py:288
  1037.9 15.0 all-to-all-start.8
  1053.0 20.4 %all-to-all-start.14 = ((bf16[4,96,900]{2,1,0:T(8,128)(2,1)}), bf16[4,96,900]{2,1,0:T(8,128)(2,1)S(1)}, u32[]{:S(2)}, u32[]{:S(2)}) async-start(bf16[4,96,900]{2,1,0:T(8,128)(2,1)} %bitcast.356), calls=%async_computation.14 | async-start | bytes 1572864 | tf_op jit(solution)/shard_map/all_to_all | solution.py:229
  1057.1 229.0 %reduce-scatter.49.cloned.1.call-start = ((), (), s32[]{:S(2)}) async-start(), calls=%async_computation.49 | async-start | bytes 811008 | tf_op jit(solution)/shard_map/reduce_scatter | solution.py:281
  1096.8 308.8 %reduce-scatter.53.cloned.1.call-start = ((), (), s32[]{:S(2)}) async-start(), calls=%async_computation.51 | async-start | bytes 1081344 | tf_op jit(solution)/shard_map/reduce_scatter | solution.py:285
  1112.2 427.4 %reduce-scatter.51.cloned.1.call-start = ((), (), s32[]{:S(2)}) async-start(), calls=%async_computation.50 | async-start | bytes 1081344 | tf_op jit(solution)/shard_map/reduce_scatter | solution.py:284
  1157.4 515.8 %reduce-scatter.47.cloned.1.call-start = ((), (), s32[]{:S(2)}) async-start(), calls=%async_computation.48 | async-start | bytes 1081344 | tf_op jit(solution)/shard_map/reduce_scatter | solution.py:278
  1196.3 610.7 %reduce-scatter.45.cloned.1.call-start = ((), (), s32[]{:S(2)}) async-start(), calls=%async_computation.47 | async-start | bytes 1081344 | tf_op jit(solution)/shard_map/reduce_scatter | solution.py:277
  1206.7 736.1 %reduce-scatter.43.cloned.1.call-start = ((), (), s32[]{:S(2)}) async-start(), calls=%async_computation.46 | async-start | bytes 2162688 | tf_op jit(solution)/shard_map/reduce_scatter | solution.py:276
  (271 other events, 3048.2 us)
Sparse Core Ops, SparseCore 0:
  596.9 153.9 all-reduce.35
  785.6 28.2 reduce-scatter.34
  816.2 28.4 reduce-scatter.36
  847.4 28.6 reduce-scatter.38
  878.8 28.4 reduce-scatter.40
  909.5 30.3 reduce-scatter.26
  942.2 30.5 reduce-scatter.28
  975.0 30.5 reduce-scatter.30
  1007.9 30.5 reduce-scatter.32
  1040.7 30.6 reduce-scatter.20
  1073.6 30.3 reduce-scatter.22
  1106.2 30.5 reduce-scatter.18
  1139.0 30.6 reduce-scatter.24
  1175.2 93.7 reduce-scatter.48
  1271.7 133.9 reduce-scatter.52
  1408.4 131.0 reduce-scatter.50
  1542.2 131.0 reduce-scatter.46
  1676.0 130.9 reduce-scatter.44
  1809.9 132.9 reduce-scatter.42
where the time goes:
time: 1960 us; the launch traced here: 1950 us
  waiting for transfers between devices  693 us (35%)
  blocking collectives  511 us (26%)
  local copies, waits for them, and re-layouts  373 us (19%)
  other arithmetic  145 us (7%)
  matrix products  142 us (7%)
  starting transfers between devices  67.9 us (3%)
    reduce_scatter x1, waiting for transfers between devices, on_device(): lax.psum_scatter(grad_weight_one, ('wide', 'narrow'), scatter_dimension=0...  136 us
    reduce_scatter x1, waiting for transfers between devices, on_device(): lax.psum_scatter(grad_inner_two, ('wide', 'narrow'), scatter_dimension=0,...  134 us
    reduce_scatter x1, waiting for transfers between devices, on_device(): lax.psum_scatter(grad_weight_two, ('wide', 'narrow'), scatter_dimension=0...  134 us
    reduce_scatter x1, waiting for transfers between devices, on_device(): lax.psum_scatter(grad_weight_three, ('wide', 'narrow'), scatter_dimension...  134 us
    reduce_scatter x1, waiting for transfers between devices, on_device(): lax.psum_scatter(grad_inner_three, ('wide', 'narrow'), scatter_dimension=...  120 us
    all_gather x1, blocking collectives, on_device(): lax.all_gather(coarse_first, ('wide', 'narrow'), axis=0, tiled=True)  75.6 us
    all_gather x1, blocking collectives, on_device(): lax.all_gather(fine_second, ('wide', 'narrow'), axis=0, tiled=True)  74.2 us
    all_gather x1, blocking collectives, on_device(): lax.all_gather(fine_third, ('wide', 'narrow'), axis=0, tiled=True)  72.3 us
  transfers between devices with their start and end apart: 35, of which 14 were waited for; matrix products, arithmetic and copies ran while one was open for 26% of the time, Pallas kernels for 0%

commit v1 on v0

--- a/solution.py
+++ b/solution.py
@@ -1,13 +1,527 @@
+import functools
+
 import jax
 import jax.numpy as jnp
+import numpy as np
 from jax import lax
+from jax.experimental import pallas as pl
+from jax.experimental.pallas import tpu as pltpu
 from jax.sharding import PartitionSpec as P
 
-L = 3600
-AHEAD_TIMES = 720
+MESH = pl.DeviceIdType.MESH
 POOL = 4
 KB = 300
-MINIBATCHES = 4
+PASSES = 1
+LANE = 128
+F32 = jnp.float32
+BF16 = jnp.bfloat16
+
+
+def up(value, unit):
+    return -(-value // unit) * unit
+
+
+def interp_table(count, length):
+    stride = length // count
+    table = np.zeros((count, length), np.float32)
+    for t in range(length):
+        doubled = 2 * t + 1 - stride
+        low = doubled // (2 * stride)
+        part = doubled - low * 2 * stride
+        table[min(max(low, 0), count - 1), t] += 2 * stride - part
+        table[min(max(low + 1, 0), count - 1), t] += part
+    return table
+
+
+def window_tables(nn, length, ahead, back_count, fore_count):
+    back, fore = interp_table(back_count, length), interp_table(fore_count, ahead)
+    piece, part = length // nn, ahead // nn
+    spans = []
+    for n in range(nn):
+        rows_b = np.nonzero(back[:, n * piece : (n + 1) * piece].any(1))[0]
+        rows_f = np.nonzero(fore[:, n * part : (n + 1) * part].any(1))[0]
+        spans.append((rows_b, rows_f))
+    wide_b = max(len(b) for b, _ in spans)
+    wide_f = max(len(f) for _, f in spans)
+    width = up(wide_b + wide_f, LANE)
+    bw, fw = up(back_count, LANE), up(fore_count, LANE)
+    pick = np.zeros((nn, bw + fw, width), np.float32)
+    mix_b = np.zeros((nn, width, piece), np.float32)
+    mix_f = np.zeros((nn, width, part), np.float32)
+    all_f = np.zeros((nn, fw, part), np.float32)
+    for n, (rows_b, rows_f) in enumerate(spans):
+        all_f[n, :fore_count] = fore[:, n * part : (n + 1) * part]
+        for slot, row in enumerate(rows_b):
+            pick[n, row, slot] = 1
+            mix_b[n, slot] = back[row, n * piece : (n + 1) * piece]
+        for slot, row in enumerate(rows_f):
+            pick[n, bw + row, wide_b + slot] = 1
+            mix_f[n, wide_b + slot] = fore[row, n * part : (n + 1) * part]
+    return tuple(t.astype(BF16) for t in (pick, mix_b, mix_f, all_f))
+
+
+class Net:
+    def __init__(self, sizes, sends, recvs):
+        self.nn, self.nc = sizes
+        self.sends, self.recvs = sends, recvs
+        self.count = 0
+        self.w, self.n = lax.axis_index("wide"), lax.axis_index("narrow")
+        self.chip, self.core = self.w // 2, self.w % 2
+
+    def at(self, d=0, e=0, c=0):
+        return ((self.chip ^ e) * 2 + (self.core ^ c), self.n ^ d)
+
+    def partners(self):
+        return (
+            [self.at(d=d) for d in range(1, self.nn)]
+            + [self.at(e=e) for e in range(1, self.nc)]
+            + [self.at(c=1)]
+        )
+
+    def greet(self):
+        barrier = pltpu.get_barrier_semaphore()
+        others = self.partners()
+        for other in others:
+            pl.semaphore_signal(barrier, 1, device_id=other, device_id_type=MESH)
+        pl.semaphore_wait(barrier, len(others))
+
+    def send(self, src, dst, to):
+        k = self.count
+        self.count += 1
+        copy = pltpu.make_async_remote_copy(
+            src_ref=src,
+            dst_ref=dst,
+            send_sem=self.sends.at[k],
+            recv_sem=self.recvs.at[k],
+            device_id=to,
+            device_id_type=MESH,
+        )
+        copy.start()
+        return copy
+
+
+def in_kernel(sizes, series, grad, mid, fsh, fb, land_s, land_g, wmid, wf, wfb, sends, recvs, own):
+    net = Net(sizes, sends, recvs)
+    nn, nc = sizes
+    rows = series.shape[1]
+    hs = mid.shape[0]
+    hw = fsh.shape[0]
+    n, w, chip, core = net.n, net.w, net.chip, net.core
+
+    def mrows(wi, ni):
+        return pl.ds(pl.multiple_of((wi * nn + ni) * hs, hs), hs)
+
+    def wrows(wi):
+        return pl.ds(pl.multiple_of(wi * hw, hw), hw)
+
+    def grows(ni):
+        return pl.ds(pl.multiple_of(ni * rows, rows), rows)
+
+    locals_ = [
+        pltpu.make_async_copy(mid, wmid.at[mrows(w, n)], own.at[0]),
+        pltpu.make_async_copy(fsh, wf.at[n, wrows(w)], own.at[1]),
+        pltpu.make_async_copy(fb, wfb.at[wrows(w)], own.at[2]),
+        pltpu.make_async_copy(series.at[n], land_s.at[n], own.at[3]),
+        pltpu.make_async_copy(grad.at[grows(n)], land_g.at[n], own.at[4]),
+    ]
+    for c in locals_:
+        c.start()
+    net.greet()
+    done = []
+    zm = [net.send(mid, wmid.at[mrows(w, n)], net.at(e=e)) for e in range(1, nc)]
+    fn = [net.send(fsh, wf.at[n, wrows(w)], net.at(d=d)) for d in range(1, nn)]
+    zb = [net.send(fb, wfb.at[wrows(w)], net.at(e=e)) for e in range(1, nc)]
+    locals_[0].wait()
+    locals_[1].wait()
+    locals_[2].wait()
+    nm = {}
+    for e in range(nc):
+        if e:
+            zm[e - 1].wait_recv()
+        r = mrows((chip ^ e) * 2 + core, n)
+        nm[e] = [net.send(wmid.at[r], wmid.at[r], net.at(d=d)) for d in range(1, nn)]
+    for c in fn:
+        c.wait_recv()
+    zf = [net.send(wf.at[:, wrows(w)], wf.at[:, wrows(w)], net.at(e=e)) for e in range(1, nc)]
+    last = []
+    for e in range(nc):
+        for c in nm[e]:
+            c.wait_recv()
+        r = wrows((chip ^ e) * 2 + core)
+        last.append(net.send(wmid.at[r], wmid.at[r], net.at(c=1)))
+    ga = [net.send(grad.at[grows(n ^ d)], land_g.at[n], net.at(d=d)) for d in range(1, nn)]
+    sa = [net.send(series.at[n ^ d], land_s.at[n], net.at(d=d)) for d in range(1, nn)]
+    for e in range(nc):
+        if e:
+            zb[e - 1].wait_recv()
+        r = wrows((chip ^ e) * 2 + core)
+        last.append(net.send(wfb.at[r], wfb.at[r], net.at(c=1)))
+    for e in range(nc):
+        if e:
+            zf[e - 1].wait_recv()
+        r = wrows((chip ^ e) * 2 + core)
+        last.append(net.send(wf.at[:, r], wf.at[:, r], net.at(c=1)))
+    for c in last + ga + sa:
+        c.wait()
+    for c in zm + fn + zb + zf + [c for e in range(nc) for c in nm[e]]:
+        c.wait_send()
+    locals_[3].wait()
+    locals_[4].wait()
+
+
+def partial_kernel(sizes, part, out, land, sends, recvs):
+    net = Net(sizes, sends, recvs)
+    nn, nc = sizes
+    net.greet()
+    cs = [net.send(part.at[net.n ^ d], land.at[d], net.at(d=d)) for d in range(1, nn)]
+    for c in cs:
+        c.wait()
+    total = part[net.n].astype(F32)
+    for d in range(1, nn):
+        total += land[d].astype(F32)
+    out[...] = total
+
+
+def share_kernel(sizes, f3, tw, out_f3, out_tw, sends, recvs, own):
+    net = Net(sizes, sends, recvs)
+    nn, nc = sizes
+    n = net.n
+    a = pltpu.make_async_copy(f3, out_f3.at[n], own.at[0])
+    b = pltpu.make_async_copy(tw.at[n], out_tw.at[n], own.at[1])
+    a.start()
+    b.start()
+    net.greet()
+    cs = []
+    for d in range(1, nn):
+        cs.append(net.send(tw.at[n ^ d], out_tw.at[n], net.at(d=d)))
+        cs.append(net.send(f3, out_f3.at[n], net.at(d=d)))
+    for c in cs:
+        c.wait()
+    a.wait()
+    b.wait()
+
+
+def out_kernel(
+    sizes, gm, gf, gb, bias, om, of, ob, obias,
+    cm, cf, cb, m1, f1, b1, zm, nf, zb, m2, f2, nm, zf, bl, bt, sends, recvs,
+):
+    net = Net(sizes, sends, recvs)
+    nn, nc = sizes
+    n, chip, core = net.n, net.chip, net.core
+    net.greet()
+    other = net.at(c=1)
+    keep = []
+
+    def go(*a):
+        c = net.send(*a)
+        keep.append(c)
+        return c
+
+    s_b = go(gb.at[:, 1 - core], cb, other)
+    s_f = go(gf.at[:, :, 1 - core], cf, other)
+    s_m = go(gm.at[:, 1 - core], cm, other)
+    s_v = go(bias, bl.at[0], other)
+    s_b.wait_recv()
+    for z in range(nc):
+        b1[z] = (gb[z, core].astype(F32) + cb[z].astype(F32)).astype(BF16)
+    r_b = [go(b1.at[chip ^ e], zb.at[e], net.at(e=e)) for e in range(1, nc)]
+    s_f.wait_recv()
+
+    def add_f(i, carry):
+        for z in range(nc):
+            f1[i, z] = (gf[i, z, core].astype(F32) + cf[i, z].astype(F32)).astype(BF16)
+        return carry
+
+    lax.fori_loop(0, nn, add_f, 0)
+    r_f = [go(f1.at[n ^ d], nf.at[d], net.at(d=d)) for d in range(1, nn)]
+    s_m.wait_recv()
+    for z in range(nc):
+        m1[z] = (gm[z, core].astype(F32) + cm[z].astype(F32)).astype(BF16)
+    hs = om.shape[0]
+    r_m = [go(m1.at[chip ^ e], zm.at[e], net.at(e=e)) for e in range(1, nc)]
+    s_v.wait_recv()
+    bt[0] = bias[...] + bl[0]
+    r_v = [go(bt.at[0], bl.at[e], net.at(e=e)) for e in range(1, nc)]
+    for c in r_f:
+        c.wait_recv()
+    for z in range(nc):
+        total = f1[n, z].astype(F32)
+        for d in range(1, nn):
+            total += nf[d, z].astype(F32)
+        f2[z] = total.astype(BF16)
+    q_f = [go(f2.at[chip ^ e], zf.at[e], net.at(e=e)) for e in range(1, nc)]
+    for c in r_m:
+        c.wait_recv()
+    total = m1[chip].astype(F32)
+    for e in range(1, nc):
+        total += zm[e].astype(F32)
+    m2[...] = total.astype(BF16)
+
+    def block(i):
+        return m2.at[pl.ds(pl.multiple_of(i * hs, hs), hs)]
+
+    q_m = [go(block(n ^ d), nm.at[d], net.at(d=d)) for d in range(1, nn)]
+    for c in r_v:
+        c.wait_recv()
+    total = bt[0]
+    for e in range(1, nc):
+        total += bl[e]
+    bt[1] = total
+    q_v = [go(bt.at[1], bl.at[nc - 1 + d], net.at(d=d)) for d in range(1, nn)]
+    for c in r_b:
+        c.wait_recv()
+    total = b1[chip].astype(F32)
+    for e in range(1, nc):
+        total += zb[e].astype(F32)
+    ob[...] = total
+    for c in q_m:
+        c.wait_recv()
+    total = block(n)[...].astype(F32)
+    for d in range(1, nn):
+        total += nm[d].astype(F32)
+    om[...] = total
+    for c in q_v:
+        c.wait_recv()
+    total = bt[1]
+    for d in range(1, nn):
+        total += bl[nc - 1 + d]
+    obias[...] = total
+    for c in q_f:
+        c.wait_recv()
+    total = f2[chip].astype(F32)
+    for e in range(1, nc):
+        total += zf[e].astype(F32)
+    of[...] = total
+    for c in keep:
+        c.wait_send()
+
+
+def params(cid):
+    return pltpu.CompilerParams(
+        collective_id=cid, has_side_effects=True, vmem_limit_bytes=56 << 20
+    )
+
+
+def dot_nt(a, b):
+    return lax.dot_general(a, b, (((1,), (1,)), ((), ())), preferred_element_type=F32)
+
+
+def dot_nn(a, b):
+    return lax.dot_general(a, b, (((1,), (0,)), ((), ())), preferred_element_type=F32)
+
+
+def dot_tn(a, b):
+    return lax.dot_general(a, b, (((0,), (0,)), ((), ())), preferred_element_type=F32)
+
+
+def slope(v):
+    s = jax.nn.sigmoid(v)
+    return s * (1.0 + v * (1.0 - s))
+
+
+def pad_to(x, width):
+    return jnp.pad(x, ((0, 0), (0, width - x.shape[1])))
+
+
+def spread_basis(x, back_count, bw, fw):
+    return jnp.concatenate([pad_to(x[:, :back_count], bw), pad_to(x[:, back_count:], fw)], axis=1)
+
+
+def fast(nn, nw, series, padding, *rest):
+    (cf, cfb, cs, csb, ct, ctb, cb, cbb, ff, ffb, fs, fsb, ft, ftb, fk, fkb, fo, fob, grad, fut) = rest
+    nc = nw // 2
+    sizes = (nn, nc)
+    rows, length = series.shape
+    piece, part = grad.shape[1], fut.shape[1]
+    ahead = part * nn
+    hid = cfb.shape[0]
+    hs, hw = hid // (nn * nw), hid // nw
+    back_count, fore_count = KB, cbb.shape[0] - KB
+    bw, fw = up(back_count, LANE), up(fore_count, LANE)
+    pick, mix_b, mix_f, all_f = window_tables(nn, length, ahead, back_count, fore_count)
+    width = pick.shape[2]
+    scale = 1.0 / (2 * (length // back_count))
+    scale_f = 1.0 / (2 * (ahead // fore_count))
+    n = lax.axis_index("narrow")
+    mids = (cf, cs, ct, spread_basis(cb, back_count, bw, fw), fs, ft)
+    mwid = [up(m.shape[1], LANE) for m in mids]
+    moff = np.concatenate([[0], np.cumsum(mwid)]).tolist()
+    mid = jnp.concatenate([pad_to(m, c) for m, c in zip(mids, mwid)], axis=1)
+    pw, qw = up(piece, LANE), up(part, LANE)
+    fsh = pad_to(ff, pw)
+    fbo = jnp.concatenate([pad_to(fk, pw), pad_to(fo, qw)], axis=1)
+    chunks = jnp.transpose(series.reshape(rows, nn, piece), (1, 0, 2))
+    anyspec = pl.BlockSpec(memory_space=pl.ANY)
+    vspec = pl.BlockSpec(memory_space=pltpu.VMEM)
+    ncopies = 16 + 3 * (nn + nc) + 2 * nn * nc
+    sems = [pltpu.SemaphoreType.DMA((ncopies,)), pltpu.SemaphoreType.DMA((ncopies,))]
+    S = jax.ShapeDtypeStruct
+    land_s, land_g, wmid, wf, wfb = pl.pallas_call(
+        functools.partial(in_kernel, sizes),
+        out_shape=(
+            S((nn, rows, piece), BF16),
+            S((nn, rows, piece), BF16),
+            S((hid, moff[-1]), BF16),
+            S((nn, hid, pw), BF16),
+            S((hid, pw + qw), BF16),
+        ),
+        in_specs=[anyspec] * 5,
+        out_specs=[anyspec] * 5,
+        scratch_shapes=sems + [pltpu.SemaphoreType.DMA((5,))],
+        compiler_params=params(0),
+    )(chunks, grad, mid, fsh, fbo)
+    w1, w2, w3, wb, v2, v3 = (wmid[:, moff[i] : moff[i + 1]] for i in range(6))
+    w1 = w1[:, : cf.shape[1]]
+    fkw, fow = wfb[:, :piece], wfb[:, pw : pw + part]
+    wf = wf[:, :, :piece]
+    pads = padding.reshape(nn, rows)
+    steps = n * piece + jnp.arange(piece, dtype=jnp.int32)
+    gmask = (steps[None, None, :] >= pads[:, :, None]).reshape(nn * rows, piece)
+    back_grad = jnp.where(gmask, -grad, 0)
+    my_b, my_f, my_all = jnp.asarray(mix_b)[n], jnp.asarray(mix_f)[n], jnp.asarray(all_f)[n]
+    part3 = dot_nt(back_grad, fkw) + dot_nt(fut, fow)
+    partf = dot_nt(fut, my_all) * scale_f
+    part3 = jnp.concatenate([part3, partf], axis=1).astype(BF16).reshape(nn, rows, hid + fw)
+    sum3 = pl.pallas_call(
+        functools.partial(partial_kernel, sizes),
+        out_shape=S((rows, hid + fw), F32),
+        in_specs=[vspec],
+        out_specs=vspec,
+        scratch_shapes=[pltpu.VMEM((nn, rows, hid + fw), BF16)] + sems,
+        compiler_params=params(1),
+    )(part3)
+    own_pads = lax.dynamic_slice_in_dim(pads, n, 1, 0)[0]
+    omask = jnp.arange(length, dtype=jnp.int32).reshape(nn, 1, piece) >= own_pads[None, :, None]
+    start = jnp.where(omask, chunks, 0)
+    flat = jnp.transpose(start, (1, 0, 2)).reshape(rows, length).astype(F32)
+    pooled = jnp.mean(flat.reshape(rows, length // POOL, POOL), axis=2).astype(BF16)
+    l1 = dot_nt(pooled, w1) + cfb
+    h1 = jax.nn.silu(l1).astype(BF16)
+    l2 = dot_nt(h1, w2) + csb
+    h2 = jax.nn.silu(l2).astype(BF16)
+    l3 = dot_nt(h2, w3) + ctb
+    h3 = jax.nn.silu(l3).astype(BF16)
+    theta = (dot_nn(h3, wb) + spread_basis(cbb[None], back_count, bw, fw)).astype(BF16)
+    tw = [dot_nn(theta, pick[j]).astype(BF16) for j in range(nn)]
+    resid = [
+        jnp.where(omask[j], start[j].astype(F32) - dot_nn(tw[j], mix_b[j]) * scale, 0).astype(BF16)
+        for j in range(nn)
+    ]
+    g1 = sum(dot_nt(resid[j], wf[j]) for j in range(nn)) + ffb
+    f1 = jax.nn.silu(g1).astype(BF16)
+    g2 = dot_nt(f1, v2) + fsb
+    f2 = jax.nn.silu(g2).astype(BF16)
+    g3 = dot_nt(f2, v3) + ftb
+    f3 = jax.nn.silu(g3).astype(BF16)
+    all3, allw = pl.pallas_call(
+        functools.partial(share_kernel, sizes),
+        out_shape=(S((nn, rows, hid), BF16), S((nn, rows, width), BF16)),
+        in_specs=[anyspec] * 2,
+        out_specs=[anyspec] * 2,
+        scratch_shapes=sems + [pltpu.SemaphoreType.DMA((2,))],
+        compiler_params=params(2),
+    )(f3, jnp.stack(tw))
+    d3 = (sum3[:, :hid] * slope(g3)).astype(BF16)
+    d2 = (dot_nn(d3, v3) * slope(g2)).astype(BF16)
+    d1 = (dot_nn(d2, v2) * slope(g1)).astype(BF16)
+    sent = [
+        (jnp.where(omask[j], land_g[j], 0).astype(F32) + dot_nn(d1, wf[j])).astype(BF16)
+        for j in range(nn)
+    ]
+    back_pull = 0
+    for j in range(nn):
+        pull = dot_nt(jnp.where(omask[j], -sent[j], 0), mix_b[j]) * scale
+        back_pull += dot_nt(pull.astype(BF16), pick[j, :bw])
+    dth = jnp.concatenate([back_pull, sum3[:, hid:]], axis=1).astype(BF16)
+    c3 = (dot_nt(dth, wb) * slope(l3)).astype(BF16)
+    c2 = (dot_nn(c3, w3) * slope(l2)).astype(BF16)
+    c1 = (dot_nn(c2, w2) * slope(l1)).astype(BF16)
+    dpool = jnp.repeat(dot_nn(c1, w1), POOL, axis=1) / POOL
+    dsent = jnp.transpose(jnp.stack(sent), (1, 0, 2)).reshape(rows, length)
+    rmask = jnp.arange(length, dtype=jnp.int32)[None] >= own_pads[:, None]
+    tid = jnp.where(rmask, dsent.astype(F32) + dpool, 0).astype(BF16)
+    f3a = all3.reshape(nn * rows, hid)
+    twa = allw.reshape(nn * rows, width)
+    back_bias = lax.dynamic_slice_in_dim(fkb, n * piece, piece, 0)
+    fore_bias = lax.dynamic_slice_in_dim(fob, n * part, part, 0)
+    land = land_s.reshape(nn * rows, piece)
+    res = (land.astype(F32) - dot_nn(twa, my_b) * scale).astype(BF16).astype(F32)
+    leftover = jnp.where(gmask, res - (dot_nn(f3a, fkw) + back_bias), 0).astype(BF16)
+    pred = dot_nn(twa, my_f) * scale_f + dot_nn(f3a, fow) + fore_bias
+    gmid = [
+        pad_to(dot_tn(c1, pooled), mwid[0]),
+        dot_tn(c2, h1),
+        dot_tn(c3, h2),
+        dot_tn(h3, dth),
+        dot_tn(d2, f1),
+        dot_tn(d3, f2),
+    ]
+    gmid = jnp.concatenate(gmid, axis=1).astype(BF16).reshape(nc, 2, hw, moff[-1])
+    gf = jnp.stack([pad_to(dot_tn(d1, resid[j]), pw) for j in range(nn)]).astype(BF16)
+    gf = gf.reshape(nn, nc, 2, hw, pw)
+    gb = jnp.concatenate([pad_to(dot_tn(f3a, back_grad), pw), pad_to(dot_tn(f3a, fut), qw)], axis=1)
+    gb = gb.astype(BF16).reshape(nc, 2, hw, pw + qw)
+    sums = [jnp.sum(v.astype(F32), axis=0) for v in (c1, c2, c3, dth, d1, d2, d3, back_grad, fut)]
+    sums[7] = lax.dynamic_update_slice_in_dim(jnp.zeros((length,), F32), sums[7], n * piece, 0)
+    sums[8] = lax.dynamic_update_slice_in_dim(jnp.zeros((ahead,), F32), sums[8], n * part, 0)
+    soff = np.concatenate([[0], np.cumsum([s.shape[0] for s in sums])]).tolist()
+    bias = jnp.pad(jnp.concatenate(sums), (0, up(soff[-1], 8 * LANE) - soff[-1])).reshape(8, -1)
+    V = pltpu.VMEM
+    mw = moff[-1]
+    bs = bias.shape
+    om, of, ob, obias = pl.pallas_call(
+        functools.partial(out_kernel, sizes),
+        out_shape=(S((hs, mw), F32), S((hw, pw), F32), S((hw, pw + qw), F32), S(bs, F32)),
+        in_specs=[vspec] * 4,
+        out_specs=[vspec] * 4,
+        scratch_shapes=[
+            V((nc, hw, mw), BF16),
+            V((nn, nc, hw, pw), BF16),
+            V((nc, hw, pw + qw), BF16),
+            V((nc, hw, mw), BF16),
+            V((nn, nc, hw, pw), BF16),
+            V((nc, hw, pw + qw), BF16),
+            V((nc, hw, mw), BF16),
+            V((nn, nc, hw, pw), BF16),
+            V((nc, hw, pw + qw), BF16),
+            V((hw, mw), BF16),
+            V((nc, hw, pw), BF16),
+            V((nn, hs, mw), BF16),
+            V((nc, hw, pw), BF16),
+            V((nn + nc,) + bs, F32),
+            V((2,) + bs, F32),
+        ]
+        + sems,
+        compiler_params=params(3),
+    )(gmid, gf, gb, bias)
+    om = [om[:, moff[i] : moff[i] + m.shape[1]] for i, m in enumerate(mids)]
+    om[3] = jnp.concatenate([om[3][:, :back_count], om[3][:, bw : bw + fore_count]], axis=1)
+    flat = obias.reshape(-1)
+    bsum = [flat[a:b] for a, b in zip(soff[:-1], soff[1:])]
+    bsum[3] = jnp.concatenate([bsum[3][:back_count], bsum[3][bw : bw + fore_count]])
+    return (
+        leftover,
+        pred,
+        tid,
+        om[0],
+        bsum[0],
+        om[1],
+        bsum[1],
+        om[2],
+        bsum[2],
+        om[3],
+        bsum[3],
+        of[:, :piece],
+        bsum[4],
+        om[4],
+        bsum[5],
+        om[5],
+        bsum[6],
+        ob[:, :piece],
+        bsum[7],
+        ob[:, pw : pw + part],
+        bsum[8],
+    )
 
 
 def upsample(coef, length):
@@ -57,7 +571,7 @@
     return jnp.sum(values.astype(jnp.float32), axis=0)
 
 
-def on_device(
+def general(
     series,
     padding,
     coarse_first,
@@ -83,13 +597,14 @@
 ):
     slim_breadth = lax.axis_size("narrow")
     slim_position = lax.axis_index("narrow")
-    onsite_tally = series.shape[0]
-    sample_group = onsite_tally // MINIBATCHES
-    piece = L // slim_breadth
-    predicted_portion = AHEAD_TIMES // slim_breadth
+    onsite_tally, length = series.shape
+    ahead = future_cotangent_array.shape[1] * slim_breadth
+    sample_group = onsite_tally // PASSES
+    piece = length // slim_breadth
+    predicted_portion = ahead // slim_breadth
     group_pads = padding.reshape(slim_breadth, onsite_tally)
     own_pads = lax.dynamic_slice_in_dim(group_pads, slim_position, 1, 0)[0]
-    steps_all = jnp.arange(L, dtype=jnp.int32)
+    steps_all = jnp.arange(length, dtype=jnp.int32)
     time_start = slim_position * piece
     predict_onset = slim_position * predicted_portion
     steps_piece = time_start + jnp.arange(piece, dtype=jnp.int32)
@@ -97,9 +612,9 @@
     predict_offset = lax.dynamic_slice_in_dim(
         detailed_predict_offset, predict_onset, predicted_portion, 0
     )
-    resid_grid = grad_resid.reshape(slim_breadth, MINIBATCHES, sample_group, piece)
+    resid_grid = grad_resid.reshape(slim_breadth, PASSES, sample_group, piece)
     predict_mesh = future_cotangent_array.reshape(
-        slim_breadth, MINIBATCHES, sample_group, predicted_portion
+        slim_breadth, PASSES, sample_group, predicted_portion
     )
     own_start = slim_position * sample_group
     coarse_local = (
@@ -132,7 +647,7 @@
     residual_parts = []
     predicted_portions = []
     grad_parts = []
-    for iteration_index in range(MINIBATCHES):
+    for iteration_index in range(PASSES):
         shared = (
             lax.all_gather(coarse_first, ("wide", "narrow"), axis=0, tiled=True),
             lax.all_gather(coarse_second, ("wide", "narrow"), axis=0, tiled=True),
@@ -153,7 +668,7 @@
             jnp.float32
         )
         started = series[lower : lower + sample_group].astype(jnp.float32) * mask
-        pooled = jnp.mean(started.reshape(sample_group, L // POOL, POOL), axis=2).astype(
+        pooled = jnp.mean(started.reshape(sample_group, length // POOL, POOL), axis=2).astype(
             jnp.bfloat16
         )
         linear_one = project_rows(pooled, weight_one) + coarse_first_bias
@@ -163,8 +678,8 @@
         linear_three = project_rows(hidden_two, weight_three) + coarse_third_bias
         hidden_three = jax.nn.silu(linear_three).astype(jnp.bfloat16)
         theta = apply_rows(hidden_three, weight_basis) + coarse_basis_bias
-        backcast = upsample(theta[:, :KB], L)
-        coarse_fore = upsample(theta[:, KB:], AHEAD_TIMES)
+        backcast = upsample(theta[:, :KB], length)
+        coarse_fore = upsample(theta[:, KB:], ahead)
         residual_here = (started - backcast) * mask
         sent_resid, sent_fore = (
             lax.all_to_all(
@@ -235,8 +750,8 @@
         grad_inner_two = column_outer(own_two_grad, own_fine_one)
         grad_inner_three = column_outer(own_three_grad, own_fine_two)
         resid_grad = resid_back.astype(jnp.float32)
-        back_pull = jax.vjp(lambda coef: upsample(coef, L), theta[:, :KB])[1]
-        fore_pull = jax.vjp(lambda coef: upsample(coef, AHEAD_TIMES), theta[:, KB:])[1]
+        back_pull = jax.vjp(lambda coef: upsample(coef, length), theta[:, :KB])[1]
+        fore_pull = jax.vjp(lambda coef: upsample(coef, ahead), theta[:, KB:])[1]
         back_coef_grad = back_pull(-resid_grad * mask)[0]
         fore_coef_grad = fore_pull(fore_back.astype(jnp.float32))[0]
         theta_grad = jnp.concatenate([back_coef_grad, fore_coef_grad], axis=1).astype(jnp.bfloat16)
@@ -265,10 +780,10 @@
             column_sums(own_two_grad),
             column_sums(own_three_grad),
             lax.dynamic_update_slice_in_dim(
-                jnp.zeros((L,), jnp.float32), column_sums(back_grad), time_start, 0
+                jnp.zeros((length,), jnp.float32), column_sums(back_grad), time_start, 0
             ),
             lax.dynamic_update_slice_in_dim(
-                jnp.zeros((AHEAD_TIMES,), jnp.float32), column_sums(predict_cotan), predict_onset, 0
+                jnp.zeros((ahead,), jnp.float32), column_sums(predict_cotan), predict_onset, 0
             ),
         )
         bias_totals = tuple((total + term for total, term in zip(bias_totals, bias_terms)))
@@ -341,54 +856,22 @@
     )
 
 
+def fits(nn, nw, series, padding, first, first_bias, *rest):
+    hid, length = first_bias.shape[0], series.shape[1]
+    paired = all(k & (k - 1) == 0 for k in (nn, nw)) and nw % 2 == 0
+    return paired and hid % (16 * nn * nw) == 0 and length % (POOL * nn) == 0 and series.shape[0] % LANE == 0
+
+
 def solution(mesh):
-    in_specs = (
-        P(("wide", "narrow"), None),
-        P("wide"),
-        P(("wide", "narrow"), None),
-        P(),
-        P(("wide", "narrow"), None),
-        P(),
-        P(("wide", "narrow"), None),
-        P(),
-        P(("wide", "narrow"), None),
-        P(),
-        P("wide", "narrow"),
-        P(),
-        P(("wide", "narrow"), None),
-        P(),
-        P(("wide", "narrow"), None),
-        P(),
-        P("wide", "narrow"),
-        P(),
-        P("wide", "narrow"),
-        P(),
-        P("wide", "narrow"),
-        P("wide", "narrow"),
-    )
-    out_specs = (
-        P("wide", "narrow"),
-        P("wide", "narrow"),
-        P(("wide", "narrow"), None),
-        P(("wide", "narrow"), None),
-        P(),
-        P(("wide", "narrow"), None),
-        P(),
-        P(("wide", "narrow"), None),
-        P(),
-        P(("wide", "narrow"), None),
-        P(),
-        P("wide", "narrow"),
-        P(),
-        P(("wide", "narrow"), None),
-        P(),
-        P(("wide", "narrow"), None),
-        P(),
-        P("wide", "narrow"),
-        P(),
-        P("wide", "narrow"),
-        P(),
-    )
-    return jax.shard_map(
-        on_device, mesh=mesh, in_specs=in_specs, out_specs=out_specs, check_vma=False
-    )
+    both, rows = P(("wide", "narrow"), None), P("wide", "narrow")
+    in_specs = (both, P("wide"))
+    in_specs += (both, P()) * 4 + (rows, P()) + (both, P()) * 2 + (rows, P()) * 2 + (rows, rows)
+    out_specs = (rows, rows, both) + (both, P()) * 4 + (rows, P()) + (both, P()) * 2 + (rows, P()) * 2
+    nn, nw = mesh.shape["narrow"], mesh.shape["wide"]
+
+    def body(*args):
+        if fits(nn, nw, *args):
+            return fast(nn, nw, *args)
+        return general(*args)
+
+    return jax.shard_map(body, mesh=mesh, in_specs=in_specs, out_specs=out_specs, check_vma=False)

time: 1960 us -> 465 us (0.24)
  waiting for transfers between devices: 693 us -> 0 us
  blocking collectives: 511 us -> 0 us
  local copies, waits for them, and re-layouts: 373 us -> 89 us
  Pallas kernels: 0 us -> 239 us
  other arithmetic: 145 us -> 35.9 us
  starting transfers between devices: 67.9 us -> 0 us
  matrix products: 142 us -> 91.6 us
    reduce_scatter x18 -> x0, waiting for transfers between devices: 657 us -> none  [the longest x1 136 us: on_device(): lax.psum_scatter(grad_weight_one, ('wide', 'narrow'), scatter_dimension=0...]
    all_gather x9 -> x0, blocking collectives: 471 us -> none  [the longest x1 75.6 us: on_device(): lax.all_gather(coarse_first, ('wide', 'narrow'), axis=0, tiled=True)]
    pallas_call x0 -> x4, Pallas kernels: none -> 239 us  [the longest x1 108 us: fast(): pl.pallas_call(functools.partial(in_kernel, sizes), out_shape=(S((nn, row...]
    reshape x39 -> x7, local copies, waits for them, and re-layouts: 94.6 us -> 15 us  [the longest x3 13.3 us: fast(): chunks = jnp.transpose(series.reshape(rows, nn, piece), (1, 0, 2))]
    all_to_all x16 -> x0, starting transfers between devices: 65.6 us -> none  [the longest x4 16.9 us: on_device(): lax.all_to_all(residual_here.astype(jnp.bfloat16), 'narrow', split_axis=1...]
    convert_element_type x32 -> x3, local copies, waits for them, and re-layouts: 70.5 us -> 17.2 us  [the longest x2 10.8 us: fast(): tid = jnp.where(rmask, dsent.astype(F32) + dpool, 0).astype(BF16)]
    dot_general x108 -> x51, matrix products: 142 us -> 91.6 us  [the longest x22 35.3 us: dot_nn(): lax.dot_general(a, b, (((1,), (0,)), ((), ())), preferred_element_type=F32)]
    reduce_sum x20 -> x4, other arithmetic: 51.3 us -> 10.8 us  [the longest x1 6.72 us: fast(): jnp.mean(flat.reshape(rows, length // POOL, POOL), axis=2).astype(BF16)]
  transfers between devices with their start and end apart: 35 -> 0, of which waited for: 14 -> 0; matrix products, arithmetic and copies ran while one was open for 26% -> 0% of each run, Pallas kernels for 0% -> 0%
where the time goes in v1:
time: 465 us; the launch traced here: 457 us
  Pallas kernels  239 us (51%)
  matrix products  91.6 us (20%)
  local copies, waits for them, and re-layouts  89 us (19%)
  other arithmetic  35.9 us (8%)
    pallas_call x1, Pallas kernels, fast(): pl.pallas_call(functools.partial(in_kernel, sizes), out_shape=(S((nn, row...  108 us
    pallas_call x1, Pallas kernels, fast(): pl.pallas_call(functools.partial(out_kernel, sizes), out_shape=(S((hs, mw...  75.8 us
    dot_general x22, matrix products, dot_nn(): lax.dot_general(a, b, (((1,), (0,)), ((), ())), preferred_element_type=F32)  35.3 us
    dot_general x17, matrix products, dot_nt(): lax.dot_general(a, b, (((1,), (1,)), ((), ())), preferred_element_type=F32)  34.7 us
    pallas_call x1, Pallas kernels, fast(): pl.pallas_call(functools.partial(partial_kernel, sizes), out_shape=S((row...  30.4 us
    unnamed x195, local copies, waits for them, and re-layouts  25.7 us
    pallas_call x1, Pallas kernels, fast(): pl.pallas_call(functools.partial(share_kernel, sizes), out_shape=(S((nn,...  24.6 us
    dot_general x12, matrix products, dot_tn(): lax.dot_general(a, b, (((0,), (0,)), ((), ())), preferred_element_type=F32)  21.5 us

profile of v1, /device:TPU:0, one launch (start us, length us, event | category | flops | bytes accessed | tf_op | source)
XLA Modules:
  0.0 457.4 jit_solution(18051815813020470068)
XLA Ops:
  1.4 5.6 %reshape.180 = bf16[384,900,4]{0,2,1:T(4,128)(2,1)} reshape(bf16[384,3600]{0,1:T(8,128)(2,1)} %param.41) | data formatting | bytes 5529600 | tf_op jit(solution)/shard_map/reshape | solution.py:353
  7.4 6.7 %convert_reduce_fusion.1 = f32[384,900]{0,1:T(8,128)S(1)} fusion(bf16[384,900,4]{0,2,1:T(4,128)(2,1)} %reshape.180, s32[384]{0:T(512)S(1)} %dynamic-slice_reduce_fusion, s32[900,4]{1,0:T(8,128)S(1)} %copy.84), kind=kLoop, calls=%fused_computation.8 | loop fusion | flops 5184000 | bytes 4163136 | tf_op jit(solution)/shard_map/reduce_sum | solution.py:397
  14.2 3.2 reshape.171
  17.3 4.6 %copy.82 = bf16[384,4,900]{2,0,1:T(8,128)(2,1)} copy(bf16[384,4,900]{0,2,1:T(8,128)(2,1)} %reshape.171) | data formatting | bytes 5529600 | tf_op jit(solution)/shard_map/reshape | solution.py:353
  22.0 5.2 %copy.83.grad = bf16[1536,900]{1,0:T(8,128)(2,1)} copy(bf16[1536,900]{0,1:T(8,128)(2,1)} %param.61) | data formatting | bytes 5529600 | tf_op args[20]
  28.8 107.8 %shard_map.544 = (bf16[4,384,900]{2,1,0:T(8,128)(2,1)}, bf16[4,384,900]{2,1,0:T(8,128)(2,1)}, bf16[512,3584]{1,0:T(8,128)(2,1)}, bf16[4,512,1024]{2,1,0:T(8,128)(2,1)}, bf16[512,1280]{1,0:T(8,128)(2,1)}) custom-call(bf16[4,384,900]{2,1,0:T(8,128)(2,1)} %bitcast.221, bf16[1536,900]{1,0:T(8,128)(2,1)} %copy.83.grad, bf16[16,3584]{1,0:T(8,128)(2,1)} %copy-done.44, ...), custom_call_target="tpu_custom_call" | custom-call | tf_op jit(solution)/shard_map/pallas_call | solution.py:359
  159.5 4.2 fusion.36
  171.7 30.4 %shard_map.546 = f32[384,640]{1,0:T(8,128)} custom-call(bf16[4,384,640]{2,1,0:T(8,128)(2,1)} %pad_maximum_fusion.1.part), custom_call_target="tpu_custom_call" | custom-call | tf_op jit(solution)/shard_map/pallas_call | solution.py:385
  202.1 2.8 convert_reduce_fusion.3
  210.6 2.9 fusion.26
  213.5 3.1 add_convert_fusion.2
  216.6 3.0 convolution_add_fusion.12
  221.8 3.1 convolution_add_fusion.11
  224.9 3.1 add_convert_fusion
  228.0 2.9 fusion.21
  239.4 2.9 convert_reduce_fusion
  253.4 2.8 convolution_convert_fusion.3
  258.8 2.8 convolution_convert_fusion.4
  264.6 3.3 pad_maximum_fusion.gf
  281.8 24.6 %shard_map.545 = (bf16[4,384,512]{2,1,0:T(8,128)(2,1)}, bf16[4,384,128]{2,1,0:T(8,128)(2,1)}) custom-call(bf16[384,512]{1,0:T(8,128)(2,1)} %get-tuple-element.45.f3, bf16[4,384,128]{2,1,0:T(8,128)(2,1)} %pad_maximum_fusion.3.tw), custom_call_target="tpu_custom_call" | custom-call | tf_op jit(solution)/shard_map/pallas_call | solution.py:416
  306.4 3.1 convolution_convert_fusion
  313.4 75.8 %shard_map.547 = (f32[16,3584]{1,0:T(8,128)}, f32[64,1024]{1,0:T(8,128)}, f32[64,1280]{1,0:T(8,128)}, f32[8,1024]{1,0:T(8,128)}) custom-call(bf16[4,2,64,3584]{3,2,1,0:T(8,128)(2,1)} %constant_dynamic-update-slice_fusion.6.gm, bf16[4,4,2,64,1024]{4,3,2,1,0:T(8,128)(2,1)} %pad_maximum_fusion.gf, bf16[4,2,64,1280]{3,2,1,0:T(8,128)(2,1)} %pad_maximum_fusion.2.gb, ...), custom_call_target="tpu_custom_call" | custom-call | tf_op jit(solution)/shard_map/pallas_call | solution.py:472
  402.6 3.4 broadcast_in_dim.65
  406.0 7.6 %div.46 = f32[384,3600]{0,1:T(8,128)} reshape(f32[384,900,4]{0,2,1:T(4,128)} %broadcast_in_dim.65) | data formatting | bytes 11059200 | tf_op jit(solution)/shard_map/div | solution.py:439
  413.6 3.0 convert_bitcast_fusion
  416.6 6.3 %copy.96 = f32[384,4,900]{0,2,1:T(8,128)} copy(f32[384,4,900]{2,0,1:T(8,128)} %convert_bitcast_fusion) | data formatting | bytes 11059200 | tf_op jit(solution)/shard_map/convert_element_type | solution.py:442
  422.9 4.5 reshape.190
  427.4 6.9 %select_convert_fusion = bf16[384,3600]{0,1:T(8,128)(2,1)} fusion(f32[384,3600]{0,1:T(8,128)} %reshape.190, f32[384,3600]{0,1:T(8,128)} %div.46, s32[384]{0:T(512)S(1)} %dynamic-slice_reduce_fusion), kind=kLoop, calls=%fused_computation.6 | loop fusion | flops 5529600 | bytes 13825536 | tf_op jit(solution)/shard_map/convert_element_type | solution.py:442
  438.1 3.6 bitcast_convert_fusion
  441.7 6.4 %copy.89 = f32[1536,900]{0,1:T(8,128)} copy(f32[1536,900]{1,0:T(8,128)} %bitcast_convert_fusion) | data formatting | bytes 11059200 | tf_op jit(solution)/shard_map/convert_element_type | solution.py:448
  448.1 3.6 subtract_convert_fusion
  452.5 3.8 fusion
  (290 shorter events, 102.3 us)
Async XLA Ops:
  21.9 5.2 %copy-start.53 = (bf16[16,900]{1,0:T(8,128)(2,1)S(1)}, bf16[16,900]{1,0:T(8,128)(2,1)}, u32[]{:S(2)}) copy-start(bf16[16,900]{1,0:T(8,128)(2,1)} %param.43) | copy-start | bytes 86404
  21.9 5.3 %copy-start.55 = (bf16[16,512]{1,0:T(8,128)(2,1)S(1)}, bf16[16,512]{1,0:T(8,128)(2,1)}, u32[]{:S(2)}) copy-start(bf16[16,512]{1,0:T(8,128)(2,1)} %param.45) | copy-start | bytes 49156
  21.9 5.3 %copy-start.56 = (bf16[16,512]{1,0:T(8,128)(2,1)S(1)}, bf16[16,512]{1,0:T(8,128)(2,1)}, u32[]{:S(2)}) copy-start(bf16[16,512]{1,0:T(8,128)(2,1)} %param.47) | copy-start | bytes 49156
  21.9 5.3 %copy-start.54 = (bf16[16,360]{1,0:T(8,128)(2,1)S(1)}, bf16[16,360]{1,0:T(8,128)(2,1)}, u32[]{:S(2)}) copy-start(bf16[16,360]{1,0:T(8,128)(2,1)} %param.49) | copy-start | bytes 34564
  21.9 5.4 %copy-start.57 = (bf16[16,512]{1,0:T(8,128)(2,1)S(1)}, bf16[16,512]{1,0:T(8,128)(2,1)}, u32[]{:S(2)}) copy-start(bf16[16,512]{1,0:T(8,128)(2,1)} %param.53) | copy-start | bytes 49156
  21.9 5.4 %copy-start.58 = (bf16[16,512]{1,0:T(8,128)(2,1)S(1)}, bf16[16,512]{1,0:T(8,128)(2,1)}, u32[]{:S(2)}) copy-start(bf16[16,512]{1,0:T(8,128)(2,1)} %param.55) | copy-start | bytes 49156
  21.9 5.4 %copy-start.49 = (bf16[64,900]{1,0:T(8,128)(2,1)S(1)}, bf16[64,900]{1,0:T(8,128)(2,1)}, u32[]{:S(2)}) copy-start(bf16[64,900]{1,0:T(8,128)(2,1)} %param.57) | copy-start | bytes 345604
  21.9 5.4 %copy-start.52 = (bf16[64,180]{1,0:T(8,128)(2,1)S(1)}, bf16[64,180]{1,0:T(8,128)(2,1)}, u32[]{:S(2)}) copy-start(bf16[64,180]{1,0:T(8,128)(2,1)} %param.59) | copy-start | bytes 69124
  22.0 6.1 %copy-start.50 = (bf16[64,900]{1,0:T(8,128)(2,1)S(1)}, bf16[64,900]{1,0:T(8,128)(2,1)}, u32[]{:S(2)}) copy-start(bf16[64,900]{1,0:T(8,128)(2,1)} %param.51) | copy-start | bytes 345604
  28.7 107.8 %copy-start.61 = (f32[512]{0:T(512)S(1)}, f32[512]{0:T(512)}, u32[]{:S(2)}) copy-start(f32[512]{0:T(512)} %param.44) | copy-start | bytes 6148
  140.2 3.6 copy-start.72
  145.1 8.3 %copy-start.12 = (pred[4,384,900]{2,1,0:T(32,128)(4,1)}, pred[4,384,900]{2,1,0:T(32,128)(4,1)S(1)}, u32[]{:S(2)}) copy-start(pred[4,384,900]{2,1,0:T(32,128)(4,1)S(1)} %broadcast_compare_fusion) | copy-start | bytes 4147204
  146.2 3.6 copy-start.68
  159.5 4.2 copy-start.2
  169.2 32.9 %copy-start.65 = (f32[512]{0:T(512)S(1)}, f32[512]{0:T(512)}, u32[]{:S(2)}) copy-start(f32[512]{0:T(512)} %param.56) | copy-start | bytes 6148
  169.2 32.9 %copy-start.77 = (f32[384,512]{1,0:T(8,128)S(1)}, f32[384,512]{1,0:T(8,128)}, u32[]{:S(2)}) copy-start(f32[384,512]{1,0:T(8,128)} %convolution_add_fusion.6) | copy-start | bytes 2359300
  210.6 6.0 %copy-start.15 = (bf16[384,900]{1,0:T(8,128)(2,1)}, bf16[384,900]{1,0:T(8,128)(2,1)S(1)}, u32[]{:S(2)}) copy-start(bf16[384,900]{1,0:T(8,128)(2,1)S(1)} %add_convert_fusion.3) | copy-start | bytes 2073604
  221.8 6.2 %copy-start.18 = (bf16[384,900]{1,0:T(8,128)(2,1)}, bf16[384,900]{1,0:T(8,128)(2,1)S(1)}, u32[]{:S(2)}) copy-start(bf16[384,900]{1,0:T(8,128)(2,1)S(1)} %add_convert_fusion.1) | copy-start | bytes 2073604
  239.4 4.5 copy-start.7
  274.8 3.9 copy-start.28
  274.8 4.7 %copy-start.78 = (f32[384,512]{1,0:T(8,128)S(1)}, f32[384,512]{1,0:T(8,128)}, u32[]{:S(2)}) copy-start(f32[384,512]{1,0:T(8,128)} %convolution_add_fusion.6) | copy-start | bytes 2359300
  274.8 4.7 %copy-start.80 = (bf16[384,512]{1,0:T(8,128)(2,1)S(1)}, bf16[384,512]{1,0:T(8,128)(2,1)}, u32[]{:S(2)}) copy-start(bf16[384,512]{1,0:T(8,128)(2,1)} %copy-done.79) | copy-start | bytes 1179652
  279.6 26.8 %copy-start.1 = (bf16[1536,900]{0,1:T(8,128)(2,1)S(1)}, bf16[1536,900]{0,1:T(8,128)(2,1)}, u32[]{:S(2)}) copy-start(bf16[1536,900]{0,1:T(8,128)(2,1)} %param.61) | copy-start | bytes 8294404
  406.0 7.6 %copy-start.16 = (bf16[384,900]{1,0:T(8,128)(2,1)S(1)}, bf16[384,900]{1,0:T(8,128)(2,1)}, u32[]{:S(2)}) copy-start(bf16[384,900]{1,0:T(8,128)(2,1)} %copy-done.15) | copy-start | bytes 2073604
  406.0 7.6 %copy-start.17 = (bf16[384,900]{1,0:T(8,128)(2,1)S(1)}, bf16[384,900]{1,0:T(8,128)(2,1)}, u32[]{:S(2)}) copy-start(bf16[384,900]{1,0:T(8,128)(2,1)} %add_convert_fusion.2) | copy-start | bytes 2073604
  406.0 7.6 %copy-start.19 = (bf16[384,900]{1,0:T(8,128)(2,1)S(1)}, bf16[384,900]{1,0:T(8,128)(2,1)}, u32[]{:S(2)}) copy-start(bf16[384,900]{1,0:T(8,128)(2,1)} %copy-done.18) | copy-start | bytes 2073604
  406.0 7.6 %copy-start.20 = (bf16[384,900]{1,0:T(8,128)(2,1)S(1)}, bf16[384,900]{1,0:T(8,128)(2,1)}, u32[]{:S(2)}) copy-start(bf16[384,900]{1,0:T(8,128)(2,1)} %add_convert_fusion) | copy-start | bytes 2073604
  427.4 6.9 %copy-start.14 = (bf16[4,384,128]{2,1,0:T(8,128)(2,1)S(1)}, bf16[4,384,128]{2,1,0:T(8,128)(2,1)}, u32[]{:S(2)}) copy-start(bf16[4,384,128]{2,1,0:T(8,128)(2,1)} %get-tuple-element.35) | copy-start | bytes 1179652
  427.4 9.0 %copy-start.11 = (bf16[4,384,512]{2,1,0:T(8,128)(2,1)S(1)}, bf16[4,384,512]{2,1,0:T(8,128)(2,1)}, u32[]{:S(2)}) copy-start(bf16[4,384,512]{2,1,0:T(8,128)(2,1)} %get-tuple-element.36) | copy-start | bytes 4718596
  427.4 9.0 %copy-start.43 = (bf16[512,1280]{1,0:T(8,128)(2,1)S(1)}, bf16[512,1280]{1,0:T(8,128)(2,1)}, u32[]{:S(2)}) copy-start(bf16[512,1280]{1,0:T(8,128)(2,1)} %get-tuple-element.37) | copy-start | bytes 3932164
  434.3 3.8 copy-start.5
  452.5 3.8 copy-start.41
  (55 other events, 103.8 us)

commit v2 on v0

--- a/solution.py
+++ b/solution.py
@@ -1,13 +1,673 @@
+import functools
+import types
+
 import jax
 import jax.numpy as jnp
+import numpy as np
 from jax import lax
+from jax.experimental import pallas as pl
+from jax.experimental.pallas import tpu as pltpu
 from jax.sharding import PartitionSpec as P
 
-L = 3600
-AHEAD_TIMES = 720
+MESH = pl.DeviceIdType.MESH
 POOL = 4
 KB = 300
-MINIBATCHES = 4
+PASSES = 1
+LANE = 128
+F32 = jnp.float32
+BF16 = jnp.bfloat16
+
+
+def up(value, unit):
+    return -(-value // unit) * unit
+
+
+def interp_table(count, length):
+    stride = length // count
+    table = np.zeros((count, length), np.float32)
+    for t in range(length):
+        doubled = 2 * t + 1 - stride
+        low = doubled // (2 * stride)
+        part = doubled - low * 2 * stride
+        table[min(max(low, 0), count - 1), t] += 2 * stride - part
+        table[min(max(low + 1, 0), count - 1), t] += part
+    return table
+
+
+def window_tables(nn, length, ahead, back_count, fore_count):
+    back, fore = interp_table(back_count, length), interp_table(fore_count, ahead)
+    piece, part = length // nn, ahead // nn
+    spans = []
+    for n in range(nn):
+        rows_b = np.nonzero(back[:, n * piece : (n + 1) * piece].any(1))[0]
+        rows_f = np.nonzero(fore[:, n * part : (n + 1) * part].any(1))[0]
+        spans.append((rows_b, rows_f))
+    wide_b = max(len(b) for b, _ in spans)
+    wide_f = max(len(f) for _, f in spans)
+    width = up(wide_b + wide_f, LANE)
+    bw, fw = up(back_count, LANE), up(fore_count, LANE)
+    pick = np.zeros((nn, bw + fw, width), np.float32)
+    mix_b = np.zeros((nn, width, piece), np.float32)
+    mix_f = np.zeros((nn, width, part), np.float32)
+    all_f = np.zeros((nn, fw, part), np.float32)
+    for n, (rows_b, rows_f) in enumerate(spans):
+        all_f[n, :fore_count] = fore[:, n * part : (n + 1) * part]
+        for slot, row in enumerate(rows_b):
+            pick[n, row, slot] = 1
+            mix_b[n, slot] = back[row, n * piece : (n + 1) * piece]
+        for slot, row in enumerate(rows_f):
+            pick[n, bw + row, wide_b + slot] = 1
+            mix_f[n, wide_b + slot] = fore[row, n * part : (n + 1) * part]
+    return tuple(t.astype(BF16) for t in (pick, mix_b, mix_f, all_f))
+
+
+class Net:
+    def __init__(self, sizes, sends, recvs):
+        self.nn, self.nc = sizes
+        self.sends, self.recvs = sends, recvs
+        self.count = 0
+        self.w, self.n = lax.axis_index("wide"), lax.axis_index("narrow")
+        self.chip, self.core = self.w // 2, self.w % 2
+
+    def at(self, d=0, e=0, c=0):
+        return ((self.chip ^ e) * 2 + (self.core ^ c), self.n ^ d)
+
+    def partners(self):
+        return (
+            [self.at(d=d) for d in range(1, self.nn)]
+            + [self.at(e=e) for e in range(1, self.nc)]
+            + [self.at(c=1)]
+        )
+
+    def greet(self):
+        barrier = pltpu.get_barrier_semaphore()
+        others = self.partners()
+        for other in others:
+            pl.semaphore_signal(barrier, 1, device_id=other, device_id_type=MESH)
+        pl.semaphore_wait(barrier, len(others))
+
+    def send(self, src, dst, to):
+        k = self.count
+        self.count += 1
+        copy = pltpu.make_async_remote_copy(
+            src_ref=src,
+            dst_ref=dst,
+            send_sem=self.sends.at[k],
+            recv_sem=self.recvs.at[k],
+            device_id=to,
+            device_id_type=MESH,
+        )
+        copy.start()
+        return copy
+
+
+def params(cid):
+    return pltpu.CompilerParams(
+        collective_id=cid, has_side_effects=True, vmem_limit_bytes=62 << 20
+    )
+
+
+def dot_nt(a, b):
+    return lax.dot_general(a, b, (((1,), (1,)), ((), ())), preferred_element_type=F32)
+
+
+def dot_nn(a, b):
+    return lax.dot_general(a, b, (((1,), (0,)), ((), ())), preferred_element_type=F32)
+
+
+def dot_tn(a, b):
+    return lax.dot_general(a, b, (((0,), (0,)), ((), ())), preferred_element_type=F32)
+
+
+def slope(v):
+    s = jax.nn.sigmoid(v)
+    return s * (1.0 + v * (1.0 - s))
+
+
+def pad_to(x, width):
+    return jnp.pad(x, ((0, 0), (0, width - x.shape[1])))
+
+
+def spread_basis(x, back_count, bw, fw):
+    return jnp.concatenate([pad_to(x[:, :back_count], bw), pad_to(x[:, back_count:], fw)], axis=1)
+
+
+def row_loop(total, unit, body):
+    def step(i, carry):
+        body(pl.multiple_of(i * unit, unit))
+        return carry
+
+    lax.fori_loop(0, total // unit, step, 0)
+
+
+def each(count, body):
+    def step(i, carry):
+        body(i)
+        return carry
+
+    lax.fori_loop(0, count, step, 0)
+
+
+def whole(c, *refs):
+    (
+        pads, pick, mix_b, mix_f, all_f, pool, cfb, csb, ctb, cbb, ffb, fsb, ftb, fkb, fob,
+        series, grad, fut_in, mid, ff, fk, fo,
+        left_out, pred_out, tid_out, om, of, ok, oo, obias, chunk_hbm, land_s,
+        ser, chunk, land_g, bg, fut, wmid, wf, wk, wo, part3, land3, f3a, tw, twa,
+        pre, act, pooled, pred, gk, go, cm, cf, ck, co, nm, m2, zm, zf, f2, nf, zk, zo,
+        temp, temp2, grads, sfore, pgb, bt, bl, kbias, obias_own, sends, recvs, own,
+    ) = refs
+    nn, nc, rows, piece, part, hid, pw, bw = c.nn, c.nc, c.rows, c.piece, c.part, c.hid, c.pw, c.bw
+    net = Net((nn, nc), sends, recvs)
+    n, chip, core = net.n, net.chip, net.core
+    keep = []
+    owned = []
+    unit = 32
+    ds = pl.ds
+
+    def go_send(*a):
+        copy = net.send(*a)
+        keep.append(copy)
+        return copy
+
+    def local(src, dst):
+        copy = pltpu.make_async_copy(src, dst, own.at[len(owned)])
+        owned.append(copy)
+        copy.start()
+        return copy
+
+    def weight(k):
+        return wmid[:, :, :, :, c.off[k] : c.off[k + 1]].reshape(hid, c.off[k + 1] - c.off[k])
+
+    def put_weight(k, value):
+        width = c.off[k + 1] - c.off[k]
+        wmid[:, :, :, :, c.off[k] : c.off[k + 1]] = value.astype(BF16).reshape(nc, 2, nn, c.hs, width)
+
+    def lane(count):
+        return lax.broadcasted_iota(jnp.int32, (unit, count), 1)
+
+    def row_mask(j, r):
+        return lane(piece) + j * piece >= pads[ds(pl.multiple_of(n * rows + r, unit), unit), :]
+
+    def piece_mask(j, r):
+        return lane(piece) + n * piece >= pads[ds(pl.multiple_of(j * rows + r, unit), unit), :]
+
+    def activate(k, bias, out):
+        def body(r):
+            v = pre[k, ds(r, unit), :] + bias[...]
+            pre[k, ds(r, unit), :] = v
+            act[out, ds(r, unit), :] = (v * jax.nn.sigmoid(v)).astype(BF16)
+
+        row_loop(rows, unit, body)
+
+    def sloped(k, out):
+        def body(r):
+            grads[out, ds(r, unit), :] = (temp[ds(r, unit), :hid] * slope(pre[k, ds(r, unit), :])).astype(BF16)
+
+        row_loop(rows, unit, body)
+
+    ones = jnp.ones((8, rows), BF16)
+
+    def sums(value):
+        return dot_nn(ones, value)[0:1]
+
+    c_ser = local(series, ser)
+    c_mid = local(mid, wmid.at[chip, core, n])
+    c_ff = local(ff, wf.at[n, chip, core])
+    c_fk = local(fk, wk.at[chip, core])
+    c_fo = local(fo, wo.at[chip, core])
+    c_bg = local(grad, bg)
+    c_fut = local(fut_in, fut)
+    net.greet()
+    a_zm = [go_send(mid, wmid.at[chip, core, n], net.at(e=e)) for e in range(1, nc)]
+    a_nm = [[go_send(mid, wmid.at[chip, core, n], net.at(d=d)) for d in range(1, nn)]]
+    a_fn = [go_send(ff, wf.at[n, chip, core], net.at(d=d)) for d in range(1, nn)]
+    a_zk = [go_send(fk, wk.at[chip, core], net.at(e=e)) for e in range(1, nc)]
+    a_zk += [go_send(fo, wo.at[chip, core], net.at(e=e)) for e in range(1, nc)]
+    for j in range(nn):
+        pl.when(n == j)(functools.partial(take_bias, kbias, obias_own, fkb, fob, j, piece, part))
+    bt[...] = jnp.zeros_like(bt)
+    c_ser.wait()
+    for j in range(nn):
+
+        def cut(r, j=j):
+            x = ser[ds(r, unit), j * piece : (j + 1) * piece]
+            chunk[j, ds(r, unit), :] = jnp.where(row_mask(j, r), x.astype(F32), 0).astype(BF16)
+
+        row_loop(rows, unit, cut)
+    c_chunk = local(chunk, chunk_hbm)
+    c_mid.wait()
+    for e in range(1, nc):
+        a_zm[e - 1].wait_recv()
+        block = wmid.at[chip ^ e, core, n]
+        a_nm.append([go_send(block, block, net.at(d=d)) for d in range(1, nn)])
+    c_ff.wait()
+    for copy in a_fn:
+        copy.wait_recv()
+    block = wf.at[:, chip, core]
+    a_zf = [go_send(block, block, net.at(e=e)) for e in range(1, nc)]
+    for j in range(nn):
+        pooled[:, j * c.poolw : (j + 1) * c.poolw] = dot_nn(chunk[j], pool[...]).astype(BF16)
+    c_bg.wait()
+    c_fut.wait()
+
+    def negate(j):
+        def body(r):
+            at = ds(pl.multiple_of(j * rows + r, unit), unit)
+            bg[at, :] = jnp.where(piece_mask(j, r), -bg[at, :].astype(F32), 0).astype(BF16)
+
+        row_loop(rows, unit, body)
+
+    each(nn, negate)
+    c_fk.wait()
+    c_fo.wait()
+    for copy in a_zk:
+        copy.wait_recv()
+    a_ck = [go_send(wk.at[:, core], wk.at[:, core], net.at(c=1)), go_send(wo.at[:, core], wo.at[:, core], net.at(c=1))]
+    a_cm = []
+    for e in range(nc):
+        for copy in a_nm[e]:
+            copy.wait_recv()
+        block = wmid.at[chip ^ e, core]
+        a_cm.append(go_send(block, block, net.at(c=1)))
+    for copy in a_ck:
+        copy.wait_recv()
+
+    def partial(j):
+        at = ds(pl.multiple_of(j * rows, rows), rows)
+        back = wk[...].reshape(hid, piece)
+        fore = wo[...].reshape(hid, part)
+        part3[j, :, :hid] = (dot_nt(bg[at, :], back) + dot_nt(fut[at, :], fore)).astype(BF16)
+        part3[j, :, hid:] = (dot_nt(fut[at, :], all_f[n]) * c.scale_f).astype(BF16)
+        bt[0, ds(4 + n, 1), :piece] += sums(bg[at, :])
+        bt[0, ds(4 + nn + n, 1), :part] += sums(fut[at, :])
+
+    each(nn, partial)
+    a_p = [go_send(part3.at[n ^ d], land3.at[d], net.at(d=d)) for d in range(1, nn)]
+
+    def grad_rows(j):
+        return grad.at[ds(pl.multiple_of(j * rows, rows), rows)]
+
+    c_ga = local(grad_rows(n), land_g.at[n])
+    a_ga = [go_send(grad_rows(n ^ d), land_g.at[n], net.at(d=d)) for d in range(1, nn)]
+    for copy in a_cm:
+        copy.wait_recv()
+    pre[0] = dot_nt(pooled[...], weight(0))
+    activate(0, cfb, 0)
+    pre[1] = dot_nt(act[0], weight(1))
+    activate(1, csb, 1)
+    pre[2] = dot_nt(act[1], weight(2))
+    activate(2, ctb, 2)
+    theta = act.at[6]
+    theta[...] = (dot_nn(act[2], weight(3)) + cbb[...]).astype(BF16)
+    c_chunk.wait()
+
+    def residual(j):
+        tw[j] = dot_nn(theta[...], pick[j]).astype(BF16)
+        temp[:, :piece] = dot_nn(tw[j], mix_b[j])
+
+        def body(r):
+            x = chunk[j, ds(r, unit), :].astype(F32) - temp[ds(r, unit), :piece] * c.scale
+            chunk[j, ds(r, unit), :] = jnp.where(row_mask(j, r), x, 0).astype(BF16)
+
+        row_loop(rows, unit, body)
+
+    each(nn, residual)
+    a_tw = [go_send(tw.at[n ^ d], twa.at[n], net.at(d=d)) for d in range(1, nn)]
+    twa[n] = tw[n]
+    a_cf = []
+    for e in range(nc):
+        if e:
+            a_zf[e - 1].wait_recv()
+        block = wf.at[:, chip ^ e, core]
+        a_cf.append(go_send(block, block, net.at(c=1)))
+    for copy in a_cf:
+        copy.wait_recv()
+    pre[3] = jnp.zeros((rows, hid), F32)
+
+    def lift(j):
+        pre[3] += dot_nt(chunk[j], wf[j].reshape(hid, piece))
+
+    each(nn, lift)
+    activate(3, ffb, 3)
+    pre[4] = dot_nt(act[3], weight(4))
+    activate(4, fsb, 4)
+    pre[5] = dot_nt(act[4], weight(5))
+    activate(5, ftb, 5)
+    f3a[n] = act[5]
+    a_f3 = [go_send(act.at[5], f3a.at[n], net.at(d=d)) for d in range(1, nn)]
+    a_sa = [go_send(chunk_hbm.at[n ^ d], land_s.at[n], net.at(d=d)) for d in range(1, nn)]
+    c_sa = local(chunk_hbm.at[n], land_s.at[n])
+    for copy in a_p:
+        copy.wait_recv()
+
+    def collect(r):
+        at = ds(r, unit)
+        total = part3[n, at, :].astype(F32)
+        for d in range(1, nn):
+            total += land3[d, at, :].astype(F32)
+        grads[0, at, :] = (total[:, :hid] * slope(pre[5, at, :])).astype(BF16)
+        sfore[at, :] = total[:, hid:].astype(BF16)
+
+    row_loop(rows, unit, collect)
+    temp[:, :hid] = dot_nn(grads[0], weight(5))
+    sloped(4, 1)
+    temp[:, :hid] = dot_nn(grads[1], weight(4))
+    sloped(3, 2)
+    c_ga.wait()
+    for copy in a_ga:
+        copy.wait_recv()
+    for copy in a_cf + a_zf + a_fn:
+        copy.wait_send()
+    temp2[...] = jnp.zeros_like(temp2)
+
+    def resid_grad(j):
+        temp[:, :piece] = dot_nn(grads[2], wf[j].reshape(hid, piece))
+
+        def body(r):
+            at = ds(r, unit)
+            x = land_g[j, at, :].astype(F32) + temp[at, :piece]
+            land_g[j, at, :] = jnp.where(row_mask(j, r), x, 0).astype(BF16)
+
+        row_loop(rows, unit, body)
+        pull = (dot_nt(land_g[j], mix_b[j]) * -c.scale).astype(BF16)
+        temp2[...] += dot_nt(pull, pick[j, :bw])
+        wf[j] = dot_tn(grads[2], chunk[j]).astype(BF16).reshape(nc, 2, c.hw, piece)
+
+    each(nn, resid_grad)
+    r_cf = go_send(wf.at[:, :, 1 - core], cf, net.at(c=1))
+    dth = grads.at[3]
+    dth[:, :bw] = temp2[...].astype(BF16)
+    dth[:, bw:] = sfore[...]
+    temp[:, :hid] = dot_nt(dth[...], weight(3))
+    sloped(2, 4)
+    temp[:, :hid] = dot_nn(grads[4], weight(2))
+    sloped(1, 5)
+    temp[:, :hid] = dot_nn(grads[5], weight(1))
+    sloped(0, 6)
+    pgb[...] = dot_nn(grads[6], weight(0)).astype(BF16)
+    for copy in a_cm + a_zm + [x for y in a_nm for x in y]:
+        copy.wait_send()
+    r_cf.wait_recv()
+
+    def add_f(j):
+        for z in range(nc):
+            cf[j, z] = (wf[j, z, core].astype(F32) + cf[j, z].astype(F32)).astype(BF16)
+
+    each(nn, add_f)
+    r_zf = [go_send(cf.at[:, chip ^ e], zf.at[e], net.at(e=e)) for e in range(1, nc)]
+    put_weight(5, dot_tn(grads[0], act[4]))
+    put_weight(4, dot_tn(grads[1], act[3]))
+    put_weight(3, dot_tn(act[2], dth[...]))
+    put_weight(2, dot_tn(grads[4], act[1]))
+    put_weight(1, dot_tn(grads[5], act[0]))
+    put_weight(0, dot_tn(grads[6], pooled[...]))
+    r_cm = go_send(wmid.at[:, 1 - core], cm, net.at(c=1))
+    for k, slot in enumerate((6, 5, 4, 3, 2, 1, 0)):
+        bt[0, k // 2 : k // 2 + 1, (k % 2) * hid : (k % 2 + 1) * hid] = sums(grads[slot])
+    r_cv = go_send(bt.at[0], bl.at[0], net.at(c=1))
+    for copy in a_f3:
+        copy.wait_recv()
+    every = f3a[...].reshape(nn * rows, hid)
+    gk[...] = dot_tn(every, bg[...]).astype(BF16).reshape(nc, 2, c.hw, piece)
+    go[...] = dot_tn(every, fut[...]).astype(BF16).reshape(nc, 2, c.hw, part)
+    r_ck = [go_send(gk.at[:, 1 - core], ck, net.at(c=1)), go_send(go.at[:, 1 - core], co, net.at(c=1))]
+    r_cm.wait_recv()
+    for z in range(nc):
+        cm[z] = (wmid[z, core].astype(F32) + cm[z].astype(F32)).astype(BF16)
+    r_nm = [go_send(cm.at[:, n ^ d], nm.at[d], net.at(d=d)) for d in range(1, nn)]
+    r_cv.wait_recv()
+    bt[1] = bt[0] + bl[0]
+    r_zv = [go_send(bt.at[1], bl.at[e], net.at(e=e)) for e in range(1, nc)]
+    for copy in r_ck:
+        copy.wait_recv()
+    for z in range(nc):
+        ck[z] = (gk[z, core].astype(F32) + ck[z].astype(F32)).astype(BF16)
+        co[z] = (go[z, core].astype(F32) + co[z].astype(F32)).astype(BF16)
+    r_zk = [go_send(ck.at[chip ^ e], zk.at[e], net.at(e=e)) for e in range(1, nc)]
+    r_zo = [go_send(co.at[chip ^ e], zo.at[e], net.at(e=e)) for e in range(1, nc)]
+    for j in range(nn):
+        temp[:, :piece] = dot_nt(pgb[:, j * c.poolw : (j + 1) * c.poolw], pool[...])
+
+        def join(r, j=j):
+            at = ds(r, unit)
+            x = land_g[j, at, :].astype(F32) + temp[at, :piece]
+            ser[at, j * piece : (j + 1) * piece] = jnp.where(row_mask(j, r), x, 0).astype(BF16)
+
+        row_loop(rows, unit, join)
+    c_tid = local(ser, tid_out)
+    for copy in a_tw:
+        copy.wait_recv()
+    c_sa.wait()
+    for copy in a_sa:
+        copy.wait_recv()
+    c_land = local(land_s, chunk)
+    c_land.wait()
+
+    def outputs(j):
+        at = ds(pl.multiple_of(j * rows, rows), rows)
+        temp[:, :piece] = dot_nn(twa[j], mix_b[n])
+
+        def first(r):
+            x = chunk[j, ds(r, unit), :].astype(F32) - temp[ds(r, unit), :piece] * c.scale
+            chunk[j, ds(r, unit), :] = x.astype(BF16)
+
+        row_loop(rows, unit, first)
+        temp[:, :piece] = dot_nn(f3a[j], wk[...].reshape(hid, piece))
+
+        def second(r):
+            x = chunk[j, ds(r, unit), :].astype(F32) - (temp[ds(r, unit), :piece] + kbias[...])
+            chunk[j, ds(r, unit), :] = jnp.where(piece_mask(j, r), x, 0).astype(BF16)
+
+        row_loop(rows, unit, second)
+        pred[at, :] = (
+            dot_nn(twa[j], mix_f[n]) * c.scale_f
+            + dot_nn(f3a[j], wo[...].reshape(hid, part))
+            + obias_own[...]
+        )
+
+    each(nn, outputs)
+    c_left = [local(chunk.at[j], left_out.at[ds(j * rows, rows)]) for j in range(nn)]
+    c_pred = local(pred, pred_out)
+    for copy in r_zv:
+        copy.wait_recv()
+    total = bt[1]
+    for e in range(1, nc):
+        total += bl[e]
+    bt[2] = total
+    r_nv = [go_send(bt.at[2], bl.at[nc - 1 + d], net.at(d=d)) for d in range(1, nn)]
+    for copy in r_nm:
+        copy.wait_recv()
+    for z in range(nc):
+        total = cm[z, n].astype(F32)
+        for d in range(1, nn):
+            total += nm[d, z].astype(F32)
+        m2[z] = total.astype(BF16)
+    r_zm = [go_send(m2.at[chip ^ e], zm.at[e], net.at(e=e)) for e in range(1, nc)]
+    for copy in r_zf:
+        copy.wait_recv()
+
+    def sum_f(j):
+        total = cf[j, chip].astype(F32)
+        for e in range(1, nc):
+            total += zf[e, j].astype(F32)
+        f2[j] = total.astype(BF16)
+
+    each(nn, sum_f)
+    r_nf = [go_send(f2.at[n ^ d], nf.at[d], net.at(d=d)) for d in range(1, nn)]
+    for copy in r_zk + r_zo:
+        copy.wait_recv()
+    total, other = ck[chip].astype(F32), co[chip].astype(F32)
+    for e in range(1, nc):
+        total += zk[e].astype(F32)
+        other += zo[e].astype(F32)
+    ok[...] = total
+    oo[...] = other
+    for copy in r_nv:
+        copy.wait_recv()
+    total = bt[2]
+    for d in range(1, nn):
+        total += bl[nc - 1 + d]
+    obias[...] = total
+    for copy in r_zm:
+        copy.wait_recv()
+    total = m2[chip].astype(F32)
+    for e in range(1, nc):
+        total += zm[e].astype(F32)
+    om[...] = total
+    for copy in r_nf:
+        copy.wait_recv()
+    total = f2[n].astype(F32)
+    for d in range(1, nn):
+        total += nf[d].astype(F32)
+    of[...] = total
+    waited = a_cf + a_zf + a_fn + a_cm + a_zm + [x for y in a_nm for x in y]
+    for copy in keep:
+        if not any(copy is x for x in waited):
+            copy.wait_send()
+    for copy in [c_tid, c_pred] + c_left:
+        copy.wait()
+
+
+def take_bias(kbias, obias_own, fkb, fob, j, piece, part):
+    kbias[...] = fkb[:, j * piece : (j + 1) * piece]
+    obias_own[...] = fob[:, j * part : (j + 1) * part]
+
+
+def fast(nn, nw, series, padding, *rest):
+    (cf, cfb, cs, csb, ct, ctb, cb, cbb, ff, ffb, fs, fsb, ft, ftb, fk, fkb, fo, fob, grad, fut) = rest
+    nc = nw // 2
+    rows, length = series.shape
+    piece, part = grad.shape[1], fut.shape[1]
+    ahead = part * nn
+    hid = cfb.shape[0]
+    hs, hw = hid // (nn * nw), hid // nw
+    back_count, fore_count = KB, cbb.shape[0] - KB
+    bw, fw = up(back_count, LANE), up(fore_count, LANE)
+    pick, mix_b, mix_f, all_f = window_tables(nn, length, ahead, back_count, fore_count)
+    width = pick.shape[2]
+    pools = piece // POOL
+    poolw = up(pools, LANE)
+    pool = np.zeros((piece, poolw), np.float32)
+    pool[np.arange(piece), np.arange(piece) // POOL] = 1 / POOL
+    first = jnp.pad(cf.reshape(hs, nn, pools), ((0, 0), (0, 0), (0, poolw - pools))).reshape(hs, -1)
+    mids = (first, cs, ct, spread_basis(cb, back_count, bw, fw), fs, ft)
+    off = np.concatenate([[0], np.cumsum([m.shape[1] for m in mids])]).tolist()
+    mid = jnp.concatenate(mids, axis=1)
+    mw = off[-1]
+    pw = up(piece, LANE)
+    c = types.SimpleNamespace(
+        nn=nn, nc=nc, rows=rows, piece=piece, part=part, hid=hid, hs=hs, hw=hw, pw=pw, bw=bw,
+        off=off, poolw=poolw,
+        scale=1.0 / (2 * (length // back_count)),
+        scale_f=1.0 / (2 * (ahead // fore_count)),
+    )
+    anyspec = pl.BlockSpec(memory_space=pl.ANY)
+    vspec = pl.BlockSpec(memory_space=pltpu.VMEM)
+    S, V = jax.ShapeDtypeStruct, pltpu.VMEM
+    bs = (up(4 + 2 * nn, 8), max(2 * hid, pw))
+    ncopies = 24 + 10 * (nn + nc) + 2 * nn * nc
+    line = lambda b: b.reshape(1, -1)
+    small = (cfb, csb, ctb, spread_basis(line(cbb), back_count, bw, fw), ffb, fsb, ftb, fkb, fob)
+    scratch = [
+        V((rows, length), BF16),
+        V((nn, rows, piece), BF16),
+        V((nn, rows, piece), BF16),
+        V((nn * rows, piece), BF16),
+        V((nn * rows, part), BF16),
+        V((nc, 2, nn, hs, mw), BF16),
+        V((nn, nc, 2, hw, piece), BF16),
+        V((nc, 2, hw, piece), BF16),
+        V((nc, 2, hw, part), BF16),
+        V((nn, rows, hid + fw), BF16),
+        V((nn, rows, hid + fw), BF16),
+        V((nn, rows, hid), BF16),
+        V((nn, rows, width), BF16),
+        V((nn, rows, width), BF16),
+        V((6, rows, hid), F32),
+        V((7, rows, max(hid, bw + fw)), BF16),
+        V((rows, nn * poolw), BF16),
+        V((nn * rows, part), F32),
+        V((nc, 2, hw, piece), BF16),
+        V((nc, 2, hw, part), BF16),
+        V((nc, nn, hs, mw), BF16),
+        V((nn, nc, hw, piece), BF16),
+        V((nc, hw, piece), BF16),
+        V((nc, hw, part), BF16),
+        V((nn, nc, hs, mw), BF16),
+        V((nc, hs, mw), BF16),
+        V((nc, hs, mw), BF16),
+        V((nc, nn, hw, piece), BF16),
+        V((nn, hw, piece), BF16),
+        V((nn, hw, piece), BF16),
+        V((nc, hw, piece), BF16),
+        V((nc, hw, part), BF16),
+        V((rows, max(pw, nn * poolw, hid)), F32),
+        V((rows, bw), F32),
+        V((7, rows, max(hid, bw + fw)), BF16),
+        V((rows, fw), BF16),
+        V((rows, nn * poolw), BF16),
+        V((3,) + bs, F32),
+        V((nn + nc,) + bs, F32),
+        V((1, piece), F32),
+        V((1, part), F32),
+        pltpu.SemaphoreType.DMA((ncopies,)),
+        pltpu.SemaphoreType.DMA((ncopies,)),
+        pltpu.SemaphoreType.DMA((16 + nn,)),
+    ]
+    leftover, pred, tid, om, of, ok, oo, obias, _, _ = pl.pallas_call(
+        functools.partial(whole, c),
+        out_shape=(
+            S((nn * rows, piece), BF16),
+            S((nn * rows, part), F32),
+            S((rows, length), BF16),
+            S((hs, mw), F32),
+            S((hw, piece), F32),
+            S((hw, piece), F32),
+            S((hw, part), F32),
+            S(bs, F32),
+            S((nn, rows, piece), BF16),
+            S((nn, rows, piece), BF16),
+        ),
+        in_specs=[vspec] * 15 + [anyspec] * 7,
+        out_specs=[anyspec] * 3 + [vspec] * 5 + [anyspec] * 2,
+        scratch_shapes=scratch,
+        compiler_params=params(0),
+    )(
+        padding.reshape(-1, 1), pick, mix_b, mix_f, all_f, pool.astype(BF16), *[line(b) for b in small],
+        series, grad, fut, mid, ff, fk, fo,
+    )
+    om = [om[:, off[i] : off[i + 1]] for i in range(6)]
+    om[0] = om[0].reshape(hs, nn, poolw)[:, :, :pools].reshape(hs, -1)
+    om[3] = jnp.concatenate([om[3][:, :back_count], om[3][:, bw : bw + fore_count]], axis=1)
+    flat = [obias[k // 2, (k % 2) * hid : (k % 2 + 1) * hid] for k in range(7)]
+    tg = flat[3]
+    flat[3] = jnp.concatenate([tg[:back_count], tg[bw : bw + fore_count]])
+    back_sum = obias[4 : 4 + nn, :piece].reshape(-1)
+    fore_sum = obias[4 + nn : 4 + 2 * nn, :part].reshape(-1)
+    return (
+        leftover,
+        pred,
+        tid,
+        om[0],
+        flat[0],
+        om[1],
+        flat[1],
+        om[2],
+        flat[2],
+        om[3],
+        flat[3],
+        of,
+        flat[4],
+        om[4],
+        flat[5],
+        om[5],
+        flat[6],
+        ok,
+        back_sum,
+        oo,
+        fore_sum,
+    )
 
 
 def upsample(coef, length):
@@ -57,7 +717,7 @@
     return jnp.sum(values.astype(jnp.float32), axis=0)
 
 
-def on_device(
+def general(
     series,
     padding,
     coarse_first,
@@ -83,13 +743,14 @@
 ):
     slim_breadth = lax.axis_size("narrow")
     slim_position = lax.axis_index("narrow")
-    onsite_tally = series.shape[0]
-    sample_group = onsite_tally // MINIBATCHES
-    piece = L // slim_breadth
-    predicted_portion = AHEAD_TIMES // slim_breadth
+    onsite_tally, length = series.shape
+    ahead = future_cotangent_array.shape[1] * slim_breadth
+    sample_group = onsite_tally // PASSES
+    piece = length // slim_breadth
+    predicted_portion = ahead // slim_breadth
     group_pads = padding.reshape(slim_breadth, onsite_tally)
     own_pads = lax.dynamic_slice_in_dim(group_pads, slim_position, 1, 0)[0]
-    steps_all = jnp.arange(L, dtype=jnp.int32)
+    steps_all = jnp.arange(length, dtype=jnp.int32)
     time_start = slim_position * piece
     predict_onset = slim_position * predicted_portion
     steps_piece = time_start + jnp.arange(piece, dtype=jnp.int32)
@@ -97,9 +758,9 @@
     predict_offset = lax.dynamic_slice_in_dim(
         detailed_predict_offset, predict_onset, predicted_portion, 0
     )
-    resid_grid = grad_resid.reshape(slim_breadth, MINIBATCHES, sample_group, piece)
+    resid_grid = grad_resid.reshape(slim_breadth, PASSES, sample_group, piece)
     predict_mesh = future_cotangent_array.reshape(
-        slim_breadth, MINIBATCHES, sample_group, predicted_portion
+        slim_breadth, PASSES, sample_group, predicted_portion
     )
     own_start = slim_position * sample_group
     coarse_local = (
@@ -132,7 +793,7 @@
     residual_parts = []
     predicted_portions = []
     grad_parts = []
-    for iteration_index in range(MINIBATCHES):
+    for iteration_index in range(PASSES):
         shared = (
             lax.all_gather(coarse_first, ("wide", "narrow"), axis=0, tiled=True),
             lax.all_gather(coarse_second, ("wide", "narrow"), axis=0, tiled=True),
@@ -153,7 +814,7 @@
             jnp.float32
         )
         started = series[lower : lower + sample_group].astype(jnp.float32) * mask
-        pooled = jnp.mean(started.reshape(sample_group, L // POOL, POOL), axis=2).astype(
+        pooled = jnp.mean(started.reshape(sample_group, length // POOL, POOL), axis=2).astype(
             jnp.bfloat16
         )
         linear_one = project_rows(pooled, weight_one) + coarse_first_bias
@@ -163,8 +824,8 @@
         linear_three = project_rows(hidden_two, weight_three) + coarse_third_bias
         hidden_three = jax.nn.silu(linear_three).astype(jnp.bfloat16)
         theta = apply_rows(hidden_three, weight_basis) + coarse_basis_bias
-        backcast = upsample(theta[:, :KB], L)
-        coarse_fore = upsample(theta[:, KB:], AHEAD_TIMES)
+        backcast = upsample(theta[:, :KB], length)
+        coarse_fore = upsample(theta[:, KB:], ahead)
         residual_here = (started - backcast) * mask
         sent_resid, sent_fore = (
             lax.all_to_all(
@@ -235,8 +896,8 @@
         grad_inner_two = column_outer(own_two_grad, own_fine_one)
         grad_inner_three = column_outer(own_three_grad, own_fine_two)
         resid_grad = resid_back.astype(jnp.float32)
-        back_pull = jax.vjp(lambda coef: upsample(coef, L), theta[:, :KB])[1]
-        fore_pull = jax.vjp(lambda coef: upsample(coef, AHEAD_TIMES), theta[:, KB:])[1]
+        back_pull = jax.vjp(lambda coef: upsample(coef, length), theta[:, :KB])[1]
+        fore_pull = jax.vjp(lambda coef: upsample(coef, ahead), theta[:, KB:])[1]
         back_coef_grad = back_pull(-resid_grad * mask)[0]
         fore_coef_grad = fore_pull(fore_back.astype(jnp.float32))[0]
         theta_grad = jnp.concatenate([back_coef_grad, fore_coef_grad], axis=1).astype(jnp.bfloat16)
@@ -265,10 +926,10 @@
             column_sums(own_two_grad),
             column_sums(own_three_grad),
             lax.dynamic_update_slice_in_dim(
-                jnp.zeros((L,), jnp.float32), column_sums(back_grad), time_start, 0
+                jnp.zeros((length,), jnp.float32), column_sums(back_grad), time_start, 0
             ),
             lax.dynamic_update_slice_in_dim(
-                jnp.zeros((AHEAD_TIMES,), jnp.float32), column_sums(predict_cotan), predict_onset, 0
+                jnp.zeros((ahead,), jnp.float32), column_sums(predict_cotan), predict_onset, 0
             ),
         )
         bias_totals = tuple((total + term for total, term in zip(bias_totals, bias_terms)))
@@ -341,54 +1002,22 @@
     )
 
 
+def fits(nn, nw, series, padding, first, first_bias, *rest):
+    hid, length = first_bias.shape[0], series.shape[1]
+    paired = all(k & (k - 1) == 0 for k in (nn, nw)) and nw % 2 == 0
+    return paired and hid % (16 * nn * nw) == 0 and length % (POOL * nn) == 0 and series.shape[0] % LANE == 0
+
+
 def solution(mesh):
-    in_specs = (
-        P(("wide", "narrow"), None),
-        P("wide"),
-        P(("wide", "narrow"), None),
-        P(),
-        P(("wide", "narrow"), None),
-        P(),
-        P(("wide", "narrow"), None),
-        P(),
-        P(("wide", "narrow"), None),
-        P(),
-        P("wide", "narrow"),
-        P(),
-        P(("wide", "narrow"), None),
-        P(),
-        P(("wide", "narrow"), None),
-        P(),
-        P("wide", "narrow"),
-        P(),
-        P("wide", "narrow"),
-        P(),
-        P("wide", "narrow"),
-        P("wide", "narrow"),
-    )
-    out_specs = (
-        P("wide", "narrow"),
-        P("wide", "narrow"),
-        P(("wide", "narrow"), None),
-        P(("wide", "narrow"), None),
-        P(),
-        P(("wide", "narrow"), None),
-        P(),
-        P(("wide", "narrow"), None),
-        P(),
-        P(("wide", "narrow"), None),
-        P(),
-        P("wide", "narrow"),
-        P(),
-        P(("wide", "narrow"), None),
-        P(),
-        P(("wide", "narrow"), None),
-        P(),
-        P("wide", "narrow"),
-        P(),
-        P("wide", "narrow"),
-        P(),
-    )
-    return jax.shard_map(
-        on_device, mesh=mesh, in_specs=in_specs, out_specs=out_specs, check_vma=False
-    )
+    both, rows = P(("wide", "narrow"), None), P("wide", "narrow")
+    in_specs = (both, P("wide"))
+    in_specs += (both, P()) * 4 + (rows, P()) + (both, P()) * 2 + (rows, P()) * 2 + (rows, rows)
+    out_specs = (rows, rows, both) + (both, P()) * 4 + (rows, P()) + (both, P()) * 2 + (rows, P()) * 2
+    nn, nw = mesh.shape["narrow"], mesh.shape["wide"]
+
+    def body(*args):
+        if fits(nn, nw, *args):
+            return fast(nn, nw, *args)
+        return general(*args)
+
+    return jax.shard_map(body, mesh=mesh, in_specs=in_specs, out_specs=out_specs, check_vma=False)

time: 1960 us -> 231 us (0.12)
  waiting for transfers between devices: 693 us -> 0 us
  blocking collectives: 511 us -> 0 us
  local copies, waits for them, and re-layouts: 373 us -> 35.9 us
  Pallas kernels: 0 us -> 192 us
  other arithmetic: 145 us -> 1.92 us
  matrix products: 142 us -> 0 us
  starting transfers between devices: 67.9 us -> 0 us
    reduce_scatter x18 -> x0, waiting for transfers between devices: 657 us -> none  [the longest x1 136 us: on_device(): lax.psum_scatter(grad_weight_one, ('wide', 'narrow'), scatter_dimension=0...]
    all_gather x9 -> x0, blocking collectives: 471 us -> none  [the longest x1 75.6 us: on_device(): lax.all_gather(coarse_first, ('wide', 'narrow'), axis=0, tiled=True)]
    pallas_call x0 -> x1, Pallas kernels: none -> 192 us  [fast(): pl.pallas_call(functools.partial(whole, c), out_shape=(S((nn * rows, piec...]
    dot_general x108 -> x0, matrix products: 142 us -> none  [the longest x36 48.7 us: project_rows(): lax.dot_general(rows_in, matrix, (((1,), (1,)), ((), ())), preferred_elem...]
    reshape x39 -> x9, local copies, waits for them, and re-layouts: 94.6 us -> 8.1 us  [the longest x3 3.28 us: fast(): line = lambda b: b.reshape(1, -1)]
    convert_element_type x32 -> x0, local copies, waits for them, and re-layouts: 70.5 us -> none  [the longest x8 21.4 us: on_device(): resid_grad = resid_back.astype(jnp.float32)]
    all_to_all x16 -> x0, starting transfers between devices: 65.6 us -> none  [the longest x4 16.9 us: on_device(): lax.all_to_all(residual_here.astype(jnp.bfloat16), 'narrow', split_axis=1...]
    reduce_sum x20 -> x0, other arithmetic: 51.3 us -> none  [the longest x14 23.8 us: column_sums(): return jnp.sum(values.astype(jnp.float32), axis=0)]
  transfers between devices with their start and end apart: 35 -> 0, of which waited for: 14 -> 0; matrix products, arithmetic and copies ran while one was open for 26% -> 0% of each run, Pallas kernels for 0% -> 0%
where the time goes in v2:
time: 231 us; the launch traced here: 230 us
  Pallas kernels  192 us (83%)
  local copies, waits for them, and re-layouts  35.9 us (16%)
    pallas_call x1, Pallas kernels, fast(): pl.pallas_call(functools.partial(whole, c), out_shape=(S((nn * rows, piec...  192 us
    unnamed x32, local copies, waits for them, and re-layouts  24.9 us

profile of v2, /device:TPU:0, one launch (start us, length us, event | category | flops | bytes accessed | tf_op | source)
XLA Modules:
  0.0 230.3 jit_solution(7562312302532396358)
XLA Ops:
  0.7 0.7 reshape.96
  1.3 0.1 slice.103
  1.4 0.6 fusion.refs_9_
  2.0 1.3 reshape.101.refs_14_
  3.3 0.8 slice.81
  4.0 1.3 reshape.100.refs_13_
  5.4 0.9 reshape.102
  6.3 0.7 constant_dynamic-update-slice_fusion.5
  7.0 0.7 constant_dynamic-update-slice_fusion.4
  7.7 0.7 constant_dynamic-update-slice_fusion.3
  8.4 0.7 constant_dynamic-update-slice_fusion.1
  9.2 0.7 constant_dynamic-update-slice_fusion.refs_18_
  9.9 1.8 reshape.108.refs_0_
  11.7 2.2 copy.57.refs_17_
  13.9 4.6 %copy.55.refs_15_ = bf16[384,3600]{1,0:T(8,128)(2,1)} copy(bf16[384,3600]{0,1:T(8,128)(2,1)} %param.27) | data formatting | bytes 5529600 | tf_op args[0]
  18.6 0.0 copy-done.5
  18.6 0.0 copy-done.1
  18.6 2.8 %copy.56.refs_16_ = bf16[1536,900]{1,0:T(8,128)(2,1)} copy(bf16[1536,900]{0,1:T(8,128)(2,1)S(1)} %copy-done.1) | data formatting | bytes 5529600 | tf_op args[20]
  21.4 191.8 %shard_map.418 = (bf16[1536,900]{1,0:T(8,128)(2,1)}, f32[1536,180]{1,0:T(8,128)}, bf16[384,3600]{1,0:T(8,128)(2,1)}, f32[16,3584]{1,0:T(8,128)}, f32[64,900]{1,0...) custom-call(s32[1536,1]{1,0:T(8,128)} %reshape.108.refs_0_, ...), custom_call_target="tpu_custom_call" | custom-call | tf_op jit(solution)/shard_map/pallas_call | solution.py:618
  213.3 4.7 %copy.58 = bf16[1536,900]{0,1:T(8,128)(2,1)} copy(bf16[1536,900]{1,0:T(8,128)(2,1)} %get-tuple-element.58) | data formatting | bytes 5529600
  218.0 0.7 pad_maximum_fusion.1
  218.6 0.7 reshape.107
  219.3 0.6 fusion.2
  219.9 0.7 reshape.106
  220.6 0.7 pad_maximum_fusion
  221.3 0.7 fusion.1
  222.0 0.7 reshape.105
  222.7 2.9 %copy.59 = f32[1536,180]{0,1:T(8,128)} copy(f32[1536,180]{1,0:T(8,128)} %get-tuple-element.59) | data formatting | bytes 2211840
  225.6 2.7 %copy.60 = bf16[384,3600]{0,1:T(8,128)(2,1)} copy(bf16[384,3600]{1,0:T(8,128)(2,1)S(1)} %copy-done) | data formatting | bytes 5529600
  228.3 0.7 copy.71
  229.0 0.7 copy.72
  229.7 0.6 copy.73
  (26 shorter events, 0.1 us)
Async XLA Ops:
  9.9 8.7 %copy-start.5 = (bf16[16,3584]{1,0:T(8,128)(2,1)}, bf16[16,3584]{1,0:T(8,128)(2,1)S(1)}, u32[]{:S(2)}) copy-start(bf16[16,3584]{1,0:T(8,128)(2,1)S(1)} %constant_dynamic-update-slice_fusion.refs_18_) | copy-start | bytes 344068
  13.9 4.7 %copy-start.1 = (bf16[1536,900]{0,1:T(8,128)(2,1)S(1)}, bf16[1536,900]{0,1:T(8,128)(2,1)}, u32[]{:S(2)}) copy-start(bf16[1536,900]{0,1:T(8,128)(2,1)} %param.47) | copy-start | bytes 8294404
  213.2 4.7 %copy-start.7 = (f32[16,1024]{1,0:T(8,128)S(1)}, f32[16,1024]{1,0:T(8,128)}, u32[]{:S(2)}) copy-start(f32[16,1024]{1,0:T(8,128)} %get-tuple-element.33) | copy-start | bytes 196612
  213.3 6.0 %copy-start.4 = (f32[16,3584]{1,0:T(8,128)S(1)}, f32[16,3584]{1,0:T(8,128)}, u32[]{:S(2)}) copy-start(f32[16,3584]{1,0:T(8,128)} %get-tuple-element.32) | copy-start | bytes 688132
  217.9 7.6 %copy-start = (bf16[384,3600]{1,0:T(8,128)(2,1)S(1)}, bf16[384,3600]{1,0:T(8,128)(2,1)}, u32[]{:S(2)}) copy-start(bf16[384,3600]{1,0:T(8,128)(2,1)} %get-tuple-element.60) | copy-start | bytes 8294404
  225.6 2.7 %copy-start.3 = (f32[64,900]{1,0:T(8,128)S(1)}, f32[64,900]{1,0:T(8,128)}, u32[]{:S(2)}) copy-start(f32[64,900]{1,0:T(8,128)} %get-tuple-element.121) | copy-start | bytes 691204
  225.6 3.4 %copy-start.2 = (f32[64,900]{1,0:T(8,128)S(1)}, f32[64,900]{1,0:T(8,128)}, u32[]{:S(2)}) copy-start(f32[64,900]{1,0:T(8,128)} %get-tuple-element.127) | copy-start | bytes 691204
  225.6 4.1 %copy-start.6 = (f32[64,180]{1,0:T(8,128)S(1)}, f32[64,180]{1,0:T(8,128)}, u32[]{:S(2)}) copy-start(f32[64,180]{1,0:T(8,128)} %get-tuple-element.129) | copy-start | bytes 138244

commit v3 on v0

--- a/solution.py
+++ b/solution.py
@@ -1,13 +1,954 @@
+import functools
+import types
+
 import jax
 import jax.numpy as jnp
+import numpy as np
 from jax import lax
+from jax.experimental import pallas as pl
+from jax.experimental.pallas import tpu as pltpu
 from jax.sharding import PartitionSpec as P
 
-L = 3600
-AHEAD_TIMES = 720
+MESH = pl.DeviceIdType.MESH
 POOL = 4
 KB = 300
-MINIBATCHES = 4
+PASSES = 1
+LANE = 128
+F32 = jnp.float32
+BF16 = jnp.bfloat16
+
+
+def up(value, unit):
+    return -(-value // unit) * unit
+
+
+def interp_table(count, length):
+    stride = length // count
+    table = np.zeros((count, length), np.float32)
+    for t in range(length):
+        doubled = 2 * t + 1 - stride
+        low = doubled // (2 * stride)
+        part = doubled - low * 2 * stride
+        table[min(max(low, 0), count - 1), t] += 2 * stride - part
+        table[min(max(low + 1, 0), count - 1), t] += part
+    return table
+
+
+def window_tables(nn, length, ahead, back_count, fore_count):
+    back, fore = interp_table(back_count, length), interp_table(fore_count, ahead)
+    piece, part = length // nn, ahead // nn
+    spans = []
+    for n in range(nn):
+        rows_b = np.nonzero(back[:, n * piece : (n + 1) * piece].any(1))[0]
+        rows_f = np.nonzero(fore[:, n * part : (n + 1) * part].any(1))[0]
+        spans.append((rows_b, rows_f))
+    wide_b = max(len(b) for b, _ in spans)
+    wide_f = max(len(f) for _, f in spans)
+    width = up(wide_b + wide_f, LANE)
+    bw, fw = up(back_count, LANE), up(fore_count, LANE)
+    pick = np.zeros((nn, width, bw + fw), np.float32)
+    mix_b = np.zeros((nn, piece, width), np.float32)
+    mix_f = np.zeros((nn, part, width), np.float32)
+    all_f = np.zeros((nn, part, fw), np.float32)
+    for n, (rows_b, rows_f) in enumerate(spans):
+        all_f[n, :, :fore_count] = fore[:, n * part : (n + 1) * part].T
+        for slot, row in enumerate(rows_b):
+            pick[n, slot, row] = 1
+            mix_b[n, :, slot] = back[row, n * piece : (n + 1) * piece]
+        for slot, row in enumerate(rows_f):
+            pick[n, wide_b + slot, bw + row] = 1
+            mix_f[n, :, wide_b + slot] = fore[row, n * part : (n + 1) * part]
+    return wide_b + wide_f, tuple(t.astype(BF16) for t in (pick, mix_b, mix_f, all_f))
+
+
+class Copy:
+    def __init__(self, copy, remote):
+        self.copy, self.sent, self.received = copy, False, not remote
+
+    def wait_recv(self):
+        if not self.received:
+            self.copy.wait_recv()
+        self.received = True
+
+    def wait_send(self):
+        if not self.sent:
+            self.copy.wait_send()
+        self.sent = True
+
+    def wait(self):
+        if not self.sent:
+            self.copy.wait()
+        self.sent = True
+
+
+class Net:
+    def __init__(self, sizes, sends, recvs):
+        self.nn, self.nc = sizes
+        self.sends, self.recvs = sends, recvs
+        self.copies = []
+        self.w, self.n = lax.axis_index("wide"), lax.axis_index("narrow")
+        self.chip, self.core = self.w // 2, self.w % 2
+
+    def chips(self, bit):
+        return ((self.chip ^ bit) * 2 + self.core, self.n)
+
+    def narrow(self, bit):
+        return (self.w, self.n ^ bit)
+
+    def sibling(self):
+        return (self.w ^ 1, self.n)
+
+    def hail(self):
+        others = [self.narrow(d) for d in range(1, self.nn)] + [self.chips(b) for b in bits(self.nc)]
+        others.append(self.sibling())
+        for other in others:
+            pl.semaphore_signal(pltpu.get_barrier_semaphore(), 1, device_id=other, device_id_type=MESH)
+        self.others = len(others)
+
+    def meet(self):
+        pl.semaphore_wait(pltpu.get_barrier_semaphore(), self.others)
+
+    def send(self, src, dst, to):
+        k = len(self.copies)
+        copy = pltpu.make_async_remote_copy(
+            src_ref=src,
+            dst_ref=dst,
+            send_sem=self.sends.at[k],
+            recv_sem=self.recvs.at[k],
+            device_id=to,
+            device_id_type=MESH,
+        )
+        copy.start()
+        self.copies.append(Copy(copy, True))
+        return self.copies[-1]
+
+    def drain(self):
+        for copy in self.copies:
+            copy.wait_recv()
+            copy.wait_send()
+
+
+def bits(count):
+    return [1 << k for k in reversed(range(count.bit_length() - 1))]
+
+
+class Gather:
+    def __init__(self, net, to, order, block, own=None):
+        self.net, self.to, self.order, self.block = net, to, order, block
+        self.coming = {}
+        self.push(0, 0, block(0) if own is None else own)
+
+    def push(self, m, first, src):
+        for i in range(first, len(self.order)):
+            b = self.order[i]
+            self.coming[m | b] = (self.net.send(src, self.block(m), self.to(b)), i)
+
+    def pull(self, m):
+        copy, i = self.coming[m]
+        copy.wait_recv()
+        self.push(m, i + 1, self.block(m))
+
+    def masks(self):
+        out = [0]
+        for b in self.order:
+            out += [m | b for m in out]
+        return out[1:]
+
+
+class Scatter:
+    def __init__(self, net, to, order, block, land, add):
+        self.net, self.to, self.order, self.block, self.land, self.add = net, to, order, block, land, add
+        self.masks = list(range(1 << len(order)))
+        self.used = 0
+        self.step = 0
+
+    def start(self):
+        b = self.order[self.step]
+        rest = [m for m in self.masks if not m & b]
+        self.pending = []
+        for m in rest:
+            copy = self.net.send(self.block(m | b), self.land(self.used), self.to(b))
+            self.pending.append((copy, m, self.used))
+            self.used += 1
+        self.masks = rest
+        self.step += 1
+
+    def finish(self):
+        for copy, m, k in self.pending:
+            copy.wait_recv()
+            self.add(m, k)
+
+    def last(self):
+        ((copy, m, k),) = self.pending
+        copy.wait_recv()
+        return k
+
+
+def params(cid):
+    return pltpu.CompilerParams(
+        collective_id=cid, has_side_effects=True, vmem_limit_bytes=62 << 20
+    )
+
+
+def dot_nt(a, b):
+    return lax.dot_general(a, b, (((1,), (1,)), ((), ())), preferred_element_type=F32)
+
+
+def dot_nn(a, b):
+    return lax.dot_general(a, b, (((1,), (0,)), ((), ())), preferred_element_type=F32)
+
+
+def dot_tn(a, b):
+    return lax.dot_general(a, b, (((0,), (0,)), ((), ())), preferred_element_type=F32)
+
+
+def slope(v):
+    s = jax.nn.sigmoid(v)
+    return s * (1.0 + v * (1.0 - s))
+
+
+def pad_to(x, width):
+    return jnp.pad(x, ((0, 0), (0, width - x.shape[1])))
+
+
+def spread_basis(x, back_count, bw, fw):
+    return jnp.concatenate([pad_to(x[:, :back_count], bw), pad_to(x[:, back_count:], fw)], axis=1)
+
+
+def row_loop(total, unit, body):
+    def step(i, carry):
+        body(pl.multiple_of(i * unit, unit), unit)
+        return carry
+
+    lax.fori_loop(0, total // unit, step, 0)
+    if total % unit:
+        body(total - total % unit, total % unit)
+
+
+def each(count, body):
+    def step(i, carry):
+        body(i)
+        return carry
+
+    lax.fori_loop(0, count, step, 0)
+
+
+def whole(c, *refs):
+    (
+        pads_in, b1, b2, b3, b4, b5, b6, b7, fkb, fob, w1, w2, w3, w4, w5, w6, mix_f_in, all_f_in,
+        pick_in, mix_in, series, grad, fut_in, ff, fk, fo,
+        left_out, pred_out, tid_out, om, of, ok, oo, obias, chunk_hbm, land_s,
+        pick, mix_b, ser, chunk, land_g, bg, fut, wmid, wf, wk, wo, part3, land3, f3a, tw, twa,
+        pre, act, pooled, pred, gf, gk, go, cm, cf, ck, co, nm, zm, zf, nf, zk, zo,
+        temp, temp2, grads, sfore, pgb, pool, pads, brow, erow, bcol, ecol, bt, bl,
+        p1, p2, p3, p4, p5, p6, q0, q1, q2, q3, q4, q5, q6, q7, q8, q9, mix_f, all_f, sends, recvs, own,
+    ) = refs
+    nn, nc, rows, piece, part, hid, pw, bw = c.nn, c.nc, c.rows, c.piece, c.part, c.hid, c.pw, c.bw
+    net = Net((nn, nc), sends, recvs)
+    n, chip, core = net.n, net.chip, net.core
+    owned = []
+    ds = pl.ds
+    send = net.send
+    near = bits(nn)
+    orders = (near, near[::-1])
+    far, back_far = bits(nc), bits(nc)[::-1]
+    half_lane = [ds(0, c.half), ds(c.half, c.off[-1] - c.half)]
+    halves = lambda count: [ds(0, count // 2), ds(count // 2, count // 2)]
+
+    def local(src, dst):
+        copy = pltpu.make_async_copy(src, dst, own.at[len(owned)])
+        copy.start()
+        owned.append(Copy(copy, False))
+        return owned[-1]
+
+    def drain():
+        for copy in owned:
+            copy.wait()
+        net.drain()
+
+    def weight(k):
+        return wmid[:, :, :, :, c.off[k] : c.off[k + 1]].reshape(hid, c.off[k + 1] - c.off[k])
+
+    def put_weight(k, value):
+        width = c.off[k + 1] - c.off[k]
+        wmid[:, :, :, :, c.off[k] : c.off[k + 1]] = value.astype(BF16).reshape(nc, 2, nn, c.hs, width)
+
+    def lanes(j):
+        return ds(pl.multiple_of(j * rows, LANE), rows)
+
+    def steps(unit, width):
+        return lax.broadcasted_iota(jnp.int32, (unit, width), 0)
+
+    def row_mask(j, r, unit):
+        return steps(unit, rows) + (j * piece + r) >= pads[:, lanes(n)]
+
+    def activate(k, out):
+        def body(r, unit):
+            at = ds(r, unit)
+            v = pre[k, at, :] + bcol[at, k : k + 1]
+            pre[k, at, :] = v
+            act[out, at, :] = (v * jax.nn.sigmoid(v)).astype(BF16)
+
+        row_loop(hid, 32, body)
+
+    def sloped(k, out):
+        def body(r, unit):
+            at = ds(r, unit)
+            grads[out, at, :] = (temp[at, :] * slope(pre[k, at, :])).astype(BF16)
+
+        row_loop(hid, 32, body)
+
+    def sums(value):
+        return dot_nt(jnp.ones((8, value.shape[1]), BF16), value)[0:1]
+
+    net.hail()
+    c_mids = [local(x, y) for x, y in zip((w1, w2, w3, w4, w5, w6), (p1, p2, p3, p4, p5, p6))]
+    c_ser = local(series, ser)
+    c_bg = local(grad, bg)
+    c_fut = local(fut_in, fut)
+    c_ff = local(ff, wf.at[n, chip, core])
+    c_fk = local(fk, wk.at[chip, core])
+    c_fo = local(fo, wo.at[chip, core])
+    c_pick = local(pick_in, pick)
+    c_mix = local(mix_in, mix_b)
+    slot = wmid.at[chip, core, n]
+    slot[...] = jnp.zeros_like(slot)
+    for copy in c_mids:
+        copy.wait()
+    for j in range(nn):
+        slot[:, j * c.poolw : j * c.poolw + c.pools] = p1[:, j * c.pools : (j + 1) * c.pools]
+    for k, w in ((1, p2), (2, p3), (4, p5), (5, p6)):
+        slot[:, c.off[k] : c.off[k + 1]] = w[...]
+    slot[:, c.off[3] : c.off[3] + c.bcount] = p4[:, : c.bcount]
+    slot[:, c.off[3] + bw : c.off[3] + bw + p4.shape[1] - c.bcount] = p4[:, c.bcount :]
+    net.meet()
+
+    z_mid = Gather(net, net.chips, far, lambda e: wmid.at[chip ^ e, core, n])
+
+    def gather_mid(e):
+        return [
+            Gather(net, net.narrow, order, lambda m, h=h: wmid.at[chip ^ e, core, n ^ m, :, h])
+            for order, h in zip(orders, half_lane)
+        ]
+
+    def pull_first(gathers):
+        for g in gathers:
+            g.pull(g.masks()[0])
+
+    def pull_rest(gathers):
+        for g in gathers:
+            for m in g.masks()[1:]:
+                g.pull(m)
+
+    n_mid = {0: gather_mid(0)}
+    n_ff = [
+        Gather(net, net.narrow, order, lambda m, h=h: wf.at[n ^ m, chip, core, h], ff.at[h])
+        for order, h in zip(orders, halves(c.hw))
+    ]
+    c_small = [
+        local(x, y)
+        for x, y in zip((pads_in, b1, b2, b3, b4, b5, b6, b7, fkb, fob), (q0, q1, q2, q3, q4, q5, q6, q7, q8, q9))
+    ]
+    c_tables = [local(mix_f_in.at[n], mix_f), local(all_f_in.at[n], all_f)]
+    for copy in c_small:
+        copy.wait()
+    pads[...] = q0[...].reshape(1, nn * rows)
+    brow[...] = jnp.zeros_like(brow)
+    for k, b in enumerate((q1, q2, q3, q5, q6, q7)):
+        brow[k : k + 1, :] = b[...].reshape(1, hid)
+    theta_bias = q4[...].reshape(1, q4.shape[0])
+    brow[6:7, : c.bcount] = theta_bias[:, : c.bcount]
+    brow[6:7, bw : bw + q4.shape[0] - c.bcount] = theta_bias[:, c.bcount :]
+    bcol[...] = jnp.transpose(brow[...])
+    z_mid.pull(z_mid.masks()[0])
+    n_mid[z_mid.masks()[0]] = gather_mid(z_mid.masks()[0])
+    z_k = [
+        Gather(net, net.chips, far, lambda e: wk.at[chip ^ e, core], fk),
+        Gather(net, net.chips, far, lambda e: wo.at[chip ^ e, core], fo),
+    ]
+    pull_first(n_mid[0])
+    for m in z_mid.masks()[1:]:
+        z_mid.pull(m)
+        n_mid[m] = gather_mid(m)
+    pull_first(n_ff)
+    erow[...] = jnp.zeros_like(erow)
+    for j in range(nn):
+
+        @pl.when(n == j)
+        def _(j=j):
+            erow[0:1, :piece] = q8[j * piece : (j + 1) * piece].reshape(1, piece)
+            erow[0:1, pw : pw + part] = q9[j * part : (j + 1) * part].reshape(1, part)
+
+    ecol[...] = jnp.transpose(erow[...])
+    bt[...] = jnp.zeros_like(bt)
+    twa[...] = jnp.zeros_like(twa)
+    first_step = lax.broadcasted_iota(jnp.int32, (c.poolw, piece), 0) * POOL
+    behind = lax.broadcasted_iota(jnp.int32, (c.poolw, piece), 1) - first_step
+    pool[...] = jnp.where((behind >= 0) & (behind < POOL), 1.0 / POOL, 0.0).astype(BF16)
+
+    pull_first(z_k)
+    others = [m for m in n_mid if m]
+    pull_first([g for m in others[:-1] for g in n_mid[m]])
+    pull_rest(n_ff)
+    c_ff.wait()
+    z_f = Gather(net, net.chips, far, lambda e: wf.at[:, chip ^ e, core])
+    a_cf = []
+
+    def hand_over(e):
+        block = wf.at[:, chip ^ e, core]
+        a_cf.append(send(block, block, net.sibling()))
+
+    hand_over(0)
+    c_ser.wait()
+
+    def cut_piece(j):
+        for r in range(0, piece, 64):
+            unit = min(64, piece - r)
+            x = ser[j * piece + r : j * piece + r + unit, :]
+            chunk[j, r : r + unit, :] = jnp.where(row_mask(j, r, unit), x.astype(F32), 0).astype(BF16)
+
+    for j in range(nn // 2):
+        cut_piece(j)
+    pull_first(n_mid[others[-1]])
+    third = up(piece // 3, 16)
+    thirds = [ds(0, third), ds(third, third), ds(2 * third, piece - 2 * third)]
+    c_ga = local(grad.at[:, lanes(n)], land_g.at[n])
+    a_ga, a_sa = [], []
+
+    def exchange_grad(k):
+        h = thirds[k]
+        for d in range(1, nn):
+            a_ga.append(send(grad.at[h, lanes(n ^ d)], land_g.at[n, h], net.narrow(d)))
+
+    def exchange_series(k):
+        h = thirds[k]
+        for d in range(1, nn):
+            a_sa.append(send(chunk_hbm.at[n ^ d, h], land_s.at[h, lanes(n)], net.narrow(d)))
+
+    exchange_grad(0)
+
+    for j in range(nn // 2, nn):
+        cut_piece(j)
+    c_chunk = local(chunk, chunk_hbm)
+    for j in range(nn):
+        pooled[j * c.poolw : (j + 1) * c.poolw, :] = dot_nn(pool[...], chunk[j]).astype(BF16)
+    pull_rest(z_k)
+    c_fk.wait()
+    c_fo.wait()
+    a_ck = [send(wk.at[:, core], wk.at[:, core], net.sibling()), send(wo.at[:, core], wo.at[:, core], net.sibling())]
+    c_bg.wait()
+    c_fut.wait()
+
+    def negate(r, unit):
+        at = ds(r, unit)
+        mask = steps(unit, nn * rows) + (n * piece + r) >= pads[...]
+        bg[at, :] = jnp.where(mask, -bg[at, :].astype(F32), 0).astype(BF16)
+
+    row_loop(piece, 16, negate)
+    a_cm = []
+    for e in n_mid:
+        pull_rest(n_mid[e])
+        block = wmid.at[chip ^ e, core]
+        a_cm.append(send(block, block, net.sibling()))
+
+    for copy in c_tables:
+        copy.wait()
+    for copy in a_ck:
+        copy.wait_recv()
+
+    def partial(j):
+        back = wk[...].reshape(hid, piece)
+        fore = wo[...].reshape(hid, part)
+        part3[j, :hid, :] = (dot_nn(back, bg[:, lanes(j)]) + dot_nn(fore, fut[:, lanes(j)])).astype(BF16)
+        ahead = dot_tn(all_f[...], fut[:, lanes(j)]) * c.scale_f
+        part3[j, hid:, :] = ahead[: c.fcount].astype(BF16)
+
+    each(nn, partial)
+
+    def add_part(m, k, h):
+        part3[n ^ m, h, :] = (part3[n ^ m, h, :].astype(F32) + land3[k, h, :].astype(F32)).astype(BF16)
+
+    s_part = [
+        Scatter(
+            net, net.narrow, order,
+            lambda m, h=h: part3.at[n ^ m, h],
+            lambda k, h=h: land3.at[k, h],
+            lambda m, k, h=h: add_part(m, k, h),
+        )
+        for order, h in zip(orders, halves(hid + c.fcount))
+    ]
+    for s in s_part:
+        s.start()
+    exchange_grad(1)
+
+    for copy in a_cm:
+        copy.wait_recv()
+    pre[0] = dot_nn(weight(0), pooled[...])
+    activate(0, 0)
+    z_f.pull(z_f.masks()[0])
+    hand_over(z_f.masks()[0])
+    pre[1] = dot_nn(weight(1), act[0])
+    activate(1, 1)
+    pre[2] = dot_nn(weight(2), act[1])
+    activate(2, 2)
+    theta = act.at[6]
+    theta[...] = (dot_tn(weight(3), act[2]) + bcol[:, 6:7]).astype(BF16)
+    for s in s_part:
+        s.finish()
+        if s.step < len(near):
+            s.start()
+    exchange_grad(2)
+    c_chunk.wait()
+
+    c_pick.wait()
+    c_mix.wait()
+
+    def residual(j):
+        tw[j] = dot_nn(pick[j], theta[...]).astype(BF16)
+        temp[:piece, :] = dot_nn(mix_b[j], tw[j])
+
+        def body(r, unit):
+            at = ds(r, unit)
+            x = chunk[j, at, :].astype(F32) - temp[at, :] * c.scale
+            chunk[j, at, :] = jnp.where(row_mask(j, r, unit), x, 0).astype(BF16)
+
+        row_loop(piece, 48, body)
+
+    each(nn, residual)
+    used = ds(0, c.used)
+    twa[n, : c.used, :] = tw[n, : c.used, :]
+    for m in z_f.masks()[1:]:
+        z_f.pull(m)
+        hand_over(m)
+    early = len(net.copies)
+
+    for copy in a_cf:
+        copy.wait_recv()
+    pre[3] = jnp.zeros((hid, rows), F32)
+
+    def lift(j):
+        pre[3] += dot_nn(wf[j].reshape(hid, piece), chunk[j])
+
+    each(nn, lift)
+    activate(3, 3)
+    pre[4] = dot_nn(weight(4), act[3])
+    activate(4, 4)
+    pre[5] = dot_nn(weight(5), act[4])
+    activate(5, 5)
+    f3a[:, lanes(n)] = act[5]
+    n_f3 = [
+        Gather(net, net.narrow, order, lambda m, h=h: f3a.at[h, lanes(n ^ m)], act.at[5, h])
+        for order, h in zip(orders, halves(hid))
+    ]
+    exchange_series(0)
+
+    while s_part[0].step < len(near):
+        for s in s_part:
+            s.finish()
+            s.start()
+    k3 = [s.last() for s in s_part]
+
+    def collect(h, k):
+        def body(r, unit):
+            at = ds(h.start + r, unit)
+            total = part3[n, at, :].astype(F32) + land3[k, at, :].astype(F32)
+            grads[0, at, :] = (total * slope(pre[5, at, :])).astype(BF16)
+
+        return body
+
+    cut = (hid + c.fcount) // 2
+    row_loop(cut, 32, collect(ds(0, cut), k3[0]))
+    row_loop(hid - cut, 32, collect(ds(cut, hid - cut), k3[1]))
+    sfore[...] = (part3[n, hid:, :].astype(F32) + land3[k3[1], hid:, :].astype(F32)).astype(BF16)
+    temp[:hid, :] = dot_tn(weight(5), grads[0])
+    sloped(4, 1)
+    temp[:hid, :] = dot_tn(weight(4), grads[1])
+    sloped(3, 2)
+
+    pull_first(n_f3)
+    a_tw = [send(tw.at[n ^ d, used], twa.at[n, used], net.narrow(d)) for d in range(1, nn)]
+    exchange_series(1)
+    r_cf = []
+    for j in range(nn):
+        gf[j] = dot_nt(grads[2], chunk[j]).astype(BF16).reshape(nc, 2, c.hw, piece)
+        r_cf.append(send(gf.at[j, :, 1 - core], cf.at[j], net.sibling()))
+
+    c_ga.wait()
+    for copy in a_ga:
+        copy.wait_recv()
+    temp2[...] = jnp.zeros_like(temp2)
+
+    def resid_grad(j):
+        temp[:piece, :] = dot_tn(wf[j].reshape(hid, piece), grads[2])
+
+        def body(r, unit):
+            at = ds(r, unit)
+            x = land_g[j, at, :].astype(F32) + temp[at, :]
+            land_g[j, at, :] = jnp.where(row_mask(j, r, unit), x, 0).astype(BF16)
+
+        row_loop(piece, 48, body)
+        pull = (dot_tn(mix_b[j], land_g[j]) * -c.scale).astype(BF16)
+        temp2[...] += dot_tn(pick[j, :, :bw], pull)
+
+    each(nn // 2, resid_grad)
+    for j in range(nn):
+        r_cf[j].wait_recv()
+
+    def add_f(j):
+        for z in range(nc):
+            cf[j, z] = (gf[j, z, core].astype(F32) + cf[j, z].astype(F32)).astype(BF16)
+
+    each(nn, add_f)
+
+    def add_zf(e, k):
+        def body(j):
+            cf[j, chip ^ e] = (cf[j, chip ^ e].astype(F32) + zf[k, j].astype(F32)).astype(BF16)
+
+        each(nn, body)
+
+    r_zf = Scatter(net, net.chips, back_far, lambda e: cf.at[:, chip ^ e], lambda k: zf.at[k], add_zf)
+    r_zf.start()
+    each(nn - nn // 2, lambda i: resid_grad(i + nn // 2))
+
+    dth = grads.at[3]
+    dth[:bw, :] = temp2[...].astype(BF16)
+    dth[bw:, :] = jnp.zeros_like(dth[bw:, :])
+    dth[bw : bw + c.fcount, :] = sfore[...]
+    temp[:hid, :] = dot_nn(weight(3), dth[...])
+    sloped(2, 4)
+    temp[:hid, :] = dot_tn(weight(2), grads[4])
+    sloped(1, 5)
+    temp[:hid, :] = dot_tn(weight(1), grads[5])
+    sloped(0, 6)
+    pgb[...] = dot_tn(weight(0), grads[6]).astype(BF16)
+    for copy in net.copies[: early]:
+        copy.wait_send()
+    put_weight(5, dot_nt(grads[0], act[4]))
+    put_weight(4, dot_nt(grads[1], act[3]))
+    put_weight(3, dot_nt(act[2], dth[...]))
+    put_weight(2, dot_nt(grads[4], act[1]))
+    put_weight(1, dot_nt(grads[5], act[0]))
+    put_weight(0, dot_nt(grads[6], pooled[...]))
+    r_cm = send(wmid.at[:, 1 - core], cm, net.sibling())
+
+    bt[0, ds(4 + n, 1), :piece] = sums(bg[...])
+    bt[0, ds(4 + nn + n, 1), :part] = sums(fut[...])
+    for k, slot_k in enumerate((6, 5, 4, 3, 2, 1, 0)):
+        bt[0, k // 2 : k // 2 + 1, (k % 2) * hid : (k % 2 + 1) * hid] = sums(grads[slot_k])
+    travel = [net.sibling()] + [net.narrow(b) for b in near] + [net.chips(b) for b in back_far]
+    v_copies = []
+
+    def send_bias():
+        k = len(v_copies)
+        v_copies.append(send(bt.at[k], bl.at[k], travel[k]))
+
+    def add_bias():
+        k = len(v_copies) - 1
+        v_copies[k].wait_recv()
+        bt[k + 1] = bt[k] + bl[k]
+
+    send_bias()
+    pull_rest(n_f3)
+    gk[...] = dot_nt(f3a[...], bg[...]).astype(BF16).reshape(nc, 2, c.hw, piece)
+    go[...] = dot_nt(f3a[...], fut[...]).astype(BF16).reshape(nc, 2, c.hw, part)
+    r_ck = [send(gk.at[:, 1 - core], ck, net.sibling()), send(go.at[:, 1 - core], co, net.sibling())]
+    r_cm.wait_recv()
+    for z in range(nc):
+        cm[z] = (wmid[z, core].astype(F32) + cm[z].astype(F32)).astype(BF16)
+
+    def add_nm(m, k, h):
+        cm[:, n ^ m, :, h] = (cm[:, n ^ m, :, h].astype(F32) + nm[k, :, :, h].astype(F32)).astype(BF16)
+
+    r_nm = [
+        Scatter(
+            net, net.narrow, order,
+            lambda m, h=h: cm.at[:, n ^ m, :, h],
+            lambda k, h=h: nm.at[k, :, :, h],
+            lambda m, k, h=h: add_nm(m, k, h),
+        )
+        for order, h in zip(orders, half_lane)
+    ]
+    for s in r_nm:
+        s.start()
+    exchange_series(2)
+    add_bias()
+    send_bias()
+
+    for copy in r_ck:
+        copy.wait_recv()
+    for z in range(nc):
+        ck[z] = (gk[z, core].astype(F32) + ck[z].astype(F32)).astype(BF16)
+        co[z] = (go[z, core].astype(F32) + co[z].astype(F32)).astype(BF16)
+
+    def add_k(e, k):
+        ck[chip ^ e] = (ck[chip ^ e].astype(F32) + zk[k].astype(F32)).astype(BF16)
+
+    def add_o(e, k):
+        co[chip ^ e] = (co[chip ^ e].astype(F32) + zo[k].astype(F32)).astype(BF16)
+
+    r_zk = [
+        Scatter(net, net.chips, back_far, lambda e: ck.at[chip ^ e], lambda k: zk.at[k], add_k),
+        Scatter(net, net.chips, back_far, lambda e: co.at[chip ^ e], lambda k: zo.at[k], add_o),
+    ]
+
+    def series_grad(j):
+        temp[:piece, :] = dot_tn(pool[...], pgb[j * c.poolw : (j + 1) * c.poolw, :])
+        for r in range(0, piece, 64):
+            unit = min(64, piece - r)
+            x = land_g[j, r : r + unit, :].astype(F32) + temp[r : r + unit, :]
+            x = jnp.where(row_mask(j, r, unit), x, 0).astype(BF16)
+            ser[j * piece + r : j * piece + r + unit, :] = x
+
+    def outputs(j):
+        temp[:piece, :] = dot_nn(mix_b[n], twa[j])
+
+        def first(r, unit):
+            at = ds(r, unit)
+            x = chunk[j, at, :].astype(F32) - temp[at, :] * c.scale
+            chunk[j, at, :] = x.astype(BF16)
+
+        row_loop(piece, 48, first)
+        temp[:piece, :] = dot_tn(wk[...].reshape(hid, piece), f3a[:, lanes(j)])
+
+        def second(r, unit):
+            at = ds(r, unit)
+            x = chunk[j, at, :].astype(F32) - (temp[at, :] + ecol[at, 0:1])
+            mask = steps(unit, rows) + (n * piece + r) >= pads[:, lanes(j)]
+            chunk[j, at, :] = jnp.where(mask, x, 0).astype(BF16)
+
+        row_loop(piece, 48, second)
+        pred[:, lanes(j)] = (
+            dot_nn(mix_f[...], twa[j]) * c.scale_f
+            + dot_tn(wo[...].reshape(hid, part), f3a[:, lanes(j)])
+            + ecol[pw : pw + part, 0:1]
+        )
+
+    for j in range(nn // 2):
+        series_grad(j)
+    r_zf.finish()
+    r_zf.start()
+    for s in r_zk:
+        s.start()
+    for j in range(nn // 2, nn):
+        series_grad(j)
+    c_tid = local(ser, tid_out)
+    for s in r_nm:
+        s.finish()
+        s.start()
+    add_bias()
+    send_bias()
+
+
+    def add_nf(m, k, h):
+        cf[n ^ m, chip, h, :] = (cf[n ^ m, chip, h, :].astype(F32) + nf[k, h, :].astype(F32)).astype(BF16)
+
+    def add_zm(e, k):
+        cm[chip ^ e, n] = (cm[chip ^ e, n].astype(F32) + zm[k].astype(F32)).astype(BF16)
+
+    r_nf = lambda: [
+        Scatter(
+            net, net.narrow, order,
+            lambda m, h=h: cf.at[n ^ m, chip, h],
+            lambda k, h=h: nf.at[k, h],
+            lambda m, k, h=h: add_nf(m, k, h),
+        )
+        for order, h in zip(orders, halves(c.hw))
+    ]
+    r_zm = Scatter(net, net.chips, back_far, lambda e: cm.at[chip ^ e, n], lambda k: zm.at[k], add_zm)
+    for copy in a_tw:
+        copy.wait_recv()
+    r_zf.finish()
+    r_nf = r_nf()
+    for s in r_nf:
+        s.start()
+    for s in r_nm:
+        s.finish()
+    r_zm.start()
+    add_bias()
+    send_bias()
+    for s in r_zk:
+        s.finish()
+        s.start()
+    for copy in a_sa:
+        copy.wait_recv()
+    c_land = [local(chunk_hbm.at[n], chunk.at[n])]
+    c_land += [local(land_s.at[:, lanes(n ^ d)], chunk.at[n ^ d]) for d in range(1, nn)]
+    for copy in c_land:
+        copy.wait()
+
+    each(nn // 2, outputs)
+    for s in r_nf:
+        s.finish()
+        s.start()
+    r_zm.finish()
+    r_zm.start()
+    add_bias()
+    send_bias()
+    each(nn - nn // 2, lambda i: outputs(i + nn // 2))
+    c_left = [local(chunk.at[j], left_out.at[:, lanes(j)]) for j in range(nn)]
+    c_pred = local(pred, pred_out)
+
+    for s in r_zk:
+        s.finish()
+    ok[...] = ck[chip].astype(F32)
+    oo[...] = co[chip].astype(F32)
+    for s in r_nf:
+        s.finish()
+    of[...] = cf[n, chip].astype(F32)
+    add_bias()
+    obias[...] = bt[len(travel)]
+    r_zm.finish()
+    om[...] = cm[chip, n].astype(F32)
+    drain()
+
+
+def finish(c, *refs):
+    om, of, ok, oo, obias = refs[:5]
+    (
+        g1, v1, g2, v2, g3, v3, g4, v4, gf, vf1, g5, vf2, g6, vf3, gk, vk, go, vo,
+    ) = refs[5:]
+    nn, piece, part, hid, bw = c.nn, c.piece, c.part, c.hid, c.bw
+    for j in range(nn):
+        g1[:, j * c.pools : (j + 1) * c.pools] = om[:, j * c.poolw : j * c.poolw + c.pools]
+    for k, g in ((1, g2), (2, g3), (4, g5), (5, g6)):
+        g[...] = om[:, c.off[k] : c.off[k + 1]]
+    fore = g4.shape[1] - c.bcount
+    g4[:, : c.bcount] = om[:, c.off[3] : c.off[3] + c.bcount]
+    g4[:, c.bcount :] = om[:, c.off[3] + bw : c.off[3] + bw + fore]
+    gf[...] = of[...]
+    gk[...] = ok[...]
+    go[...] = oo[...]
+    for k, v in enumerate((v1, v2, v3, None, vf1, vf2, vf3)):
+        if v is not None:
+            v[...] = obias[k // 2 : k // 2 + 1, (k % 2) * hid : (k % 2 + 1) * hid].reshape(hid)
+    theta = obias[1:2, hid : 2 * hid]
+    v4[...] = jnp.concatenate([theta[:, : c.bcount], theta[:, bw : bw + fore]], axis=1).reshape(v4.shape[0])
+    vk[...] = jnp.concatenate([obias[4 + j : 5 + j, :piece] for j in range(nn)], axis=1).reshape(vk.shape[0])
+    vo[...] = jnp.concatenate([obias[4 + nn + j : 5 + nn + j, :part] for j in range(nn)], axis=1).reshape(vo.shape[0])
+
+
+def fast(nn, nw, series, padding, *rest):
+    (cf, cfb, cs, csb, ct, ctb, cb, cbb, ff, ffb, fs, fsb, ft, ftb, fk, fkb, fo, fob, grad, fut) = rest
+    nc = nw // 2
+    rows, length = series.shape
+    piece, part = grad.shape[1], fut.shape[1]
+    ahead = part * nn
+    hid = cfb.shape[0]
+    hs, hw = hid // (nn * nw), hid // nw
+    back_count, fore_count = KB, cbb.shape[0] - KB
+    bw, fw = up(back_count, LANE), up(fore_count, LANE)
+    used, (pick, mix_b, mix_f, all_f) = window_tables(nn, length, ahead, back_count, fore_count)
+    width = pick.shape[1]
+    fcount = up(fore_count, 16)
+    pools = piece // POOL
+    poolw = up(pools, LANE)
+    widths = (nn * poolw, hid, hid, bw + fw, hid, hid)
+    off = np.concatenate([[0], np.cumsum(widths)]).tolist()
+    mw = off[-1]
+    pw = up(piece, LANE)
+    assert bw + fw == hid
+    c = types.SimpleNamespace(
+        nn=nn, nc=nc, rows=rows, piece=piece, part=part, hid=hid, hs=hs, hw=hw, pw=pw, bw=bw,
+        off=off, poolw=poolw, pools=pools, used=up(used, 16), fcount=fcount,
+        bcount=back_count, half=up(mw // 2, LANE),
+        scale=1.0 / (2 * (length // back_count)),
+        scale_f=1.0 / (2 * (ahead // fore_count)),
+    )
+    anyspec = pl.BlockSpec(memory_space=pl.ANY)
+    vspec = pl.BlockSpec(memory_space=pltpu.VMEM)
+    S, V = jax.ShapeDtypeStruct, pltpu.VMEM
+    bs = (up(4 + 2 * nn, 8), max(2 * hid, pw))
+    stages = 1 + len(bits(nn)) + len(bits(nc))
+    gathers = (nc - 1) + 2 * nc * (nn - 1) + 2 * (nn - 1) + 3 * (nc - 1) + 2 + 2 * nc
+    ncopies = gathers + 12 * (nn + nc) + 2 * nn * nc
+    qw = up(part, LANE)
+    scratch = [
+        V((nn, width, bw + fw), BF16),
+        V((nn, piece, width), BF16),
+        V((length, rows), BF16),
+        V((nn, piece, rows), BF16),
+        V((nn, piece, rows), BF16),
+        V((piece, nn * rows), BF16),
+        V((part, nn * rows), BF16),
+        V((nc, 2, nn, hs, mw), BF16),
+        V((nn, nc, 2, hw, piece), BF16),
+        V((nc, 2, hw, piece), BF16),
+        V((nc, 2, hw, part), BF16),
+        V((nn, hid + fcount, rows), BF16),
+        V((nn - 1, hid + fcount, rows), BF16),
+        V((hid, nn * rows), BF16),
+        V((nn, width, rows), BF16),
+        V((nn, width, rows), BF16),
+        V((6, hid, rows), F32),
+        V((7, hid, rows), BF16),
+        V((nn * poolw, rows), BF16),
+        V((part, nn * rows), F32),
+        V((nn, nc, 2, hw, piece), BF16),
+        V((nc, 2, hw, piece), BF16),
+        V((nc, 2, hw, part), BF16),
+        V((nc, nn, hs, mw), BF16),
+        V((nn, nc, hw, piece), BF16),
+        V((nc, hw, piece), BF16),
+        V((nc, hw, part), BF16),
+        V((nn - 1, nc, hs, mw), BF16),
+        V((nc - 1, hs, mw), BF16),
+        V((nc - 1, nn, hw, piece), BF16),
+        V((nn - 1, hw, piece), BF16),
+        V((nc - 1, hw, piece), BF16),
+        V((nc - 1, hw, part), BF16),
+        V((max(piece, hid), rows), F32),
+        V((bw, rows), F32),
+        V((7, hid, rows), BF16),
+        V((fcount, rows), BF16),
+        V((nn * poolw, rows), BF16),
+        V((poolw, piece), BF16),
+        V((1, nn * rows), jnp.int32),
+        V((8, hid), F32),
+        V((8, pw + qw), F32),
+        V((hid, 8), F32),
+        V((pw + qw, 8), F32),
+        V((stages + 1,) + bs, F32),
+        V((stages,) + bs, F32),
+    ]
+    scratch += [V(w.shape, BF16) for w in (cf, cs, ct, cb, fs, ft)]
+    scratch += [V(b.shape, b.dtype) for b in (padding, cfb, csb, ctb, cbb, ffb, fsb, ftb, fkb, fob)]
+    scratch += [
+        V(mix_f.shape[1:], BF16),
+        V(all_f.shape[1:], BF16),
+        pltpu.SemaphoreType.DMA((ncopies,)),
+        pltpu.SemaphoreType.DMA((ncopies,)),
+        pltpu.SemaphoreType.DMA((40 + 2 * nn,)),
+    ]
+    leftover, pred, tid, om, of, ok, oo, obias, _, _ = pl.pallas_call(
+        functools.partial(whole, c),
+        out_shape=(
+            S((piece, nn * rows), BF16),
+            S((part, nn * rows), F32),
+            S((length, rows), BF16),
+            S((hs, mw), F32),
+            S((hw, piece), F32),
+            S((hw, piece), F32),
+            S((hw, part), F32),
+            S(bs, F32),
+            S((nn, piece, rows), BF16),
+            S((piece, nn * rows), BF16),
+        ),
+        in_specs=[anyspec] * 26,
+        out_specs=[anyspec] * 3 + [vspec] * 5 + [anyspec] * 2,
+        scratch_shapes=scratch,
+        compiler_params=params(0),
+    )(
+        padding, cfb, csb, ctb, cbb, ffb, fsb, ftb, fkb, fob, cf, cs, ct, cb, fs, ft, mix_f, all_f,
+        pick, mix_b, series.T, grad.T, fut.T, ff, fk, fo,
+    )
+    params_like = (cf, cfb, cs, csb, ct, ctb, cb, cbb, ff, ffb, fs, fsb, ft, ftb, fk, fkb, fo, fob)
+    outs = pl.pallas_call(
+        functools.partial(finish, c),
+        out_shape=tuple(S(p.shape, F32) for p in params_like),
+        in_specs=[vspec] * 5,
+        out_specs=[vspec] * 18,
+    )(om, of, ok, oo, obias)
+    return (leftover.T, pred.T, tid.T) + tuple(outs)
 
 
 def upsample(coef, length):
@@ -57,7 +998,7 @@
     return jnp.sum(values.astype(jnp.float32), axis=0)
 
 
-def on_device(
+def general(
     series,
     padding,
     coarse_first,
@@ -83,13 +1024,14 @@
 ):
     slim_breadth = lax.axis_size("narrow")
     slim_position = lax.axis_index("narrow")
-    onsite_tally = series.shape[0]
-    sample_group = onsite_tally // MINIBATCHES
-    piece = L // slim_breadth
-    predicted_portion = AHEAD_TIMES // slim_breadth
+    onsite_tally, length = series.shape
+    ahead = future_cotangent_array.shape[1] * slim_breadth
+    sample_group = onsite_tally // PASSES
+    piece = length // slim_breadth
+    predicted_portion = ahead // slim_breadth
     group_pads = padding.reshape(slim_breadth, onsite_tally)
     own_pads = lax.dynamic_slice_in_dim(group_pads, slim_position, 1, 0)[0]
-    steps_all = jnp.arange(L, dtype=jnp.int32)
+    steps_all = jnp.arange(length, dtype=jnp.int32)
     time_start = slim_position * piece
     predict_onset = slim_position * predicted_portion
     steps_piece = time_start + jnp.arange(piece, dtype=jnp.int32)
@@ -97,9 +1039,9 @@
     predict_offset = lax.dynamic_slice_in_dim(
         detailed_predict_offset, predict_onset, predicted_portion, 0
     )
-    resid_grid = grad_resid.reshape(slim_breadth, MINIBATCHES, sample_group, piece)
+    resid_grid = grad_resid.reshape(slim_breadth, PASSES, sample_group, piece)
     predict_mesh = future_cotangent_array.reshape(
-        slim_breadth, MINIBATCHES, sample_group, predicted_portion
+        slim_breadth, PASSES, sample_group, predicted_portion
     )
     own_start = slim_position * sample_group
     coarse_local = (
@@ -132,7 +1074,7 @@
     residual_parts = []
     predicted_portions = []
     grad_parts = []
-    for iteration_index in range(MINIBATCHES):
+    for iteration_index in range(PASSES):
         shared = (
             lax.all_gather(coarse_first, ("wide", "narrow"), axis=0, tiled=True),
             lax.all_gather(coarse_second, ("wide", "narrow"), axis=0, tiled=True),
@@ -153,7 +1095,7 @@
             jnp.float32
         )
         started = series[lower : lower + sample_group].astype(jnp.float32) * mask
-        pooled = jnp.mean(started.reshape(sample_group, L // POOL, POOL), axis=2).astype(
+        pooled = jnp.mean(started.reshape(sample_group, length // POOL, POOL), axis=2).astype(
             jnp.bfloat16
         )
         linear_one = project_rows(pooled, weight_one) + coarse_first_bias
@@ -163,8 +1105,8 @@
         linear_three = project_rows(hidden_two, weight_three) + coarse_third_bias
         hidden_three = jax.nn.silu(linear_three).astype(jnp.bfloat16)
         theta = apply_rows(hidden_three, weight_basis) + coarse_basis_bias
-        backcast = upsample(theta[:, :KB], L)
-        coarse_fore = upsample(theta[:, KB:], AHEAD_TIMES)
+        backcast = upsample(theta[:, :KB], length)
+        coarse_fore = upsample(theta[:, KB:], ahead)
         residual_here = (started - backcast) * mask
         sent_resid, sent_fore = (
             lax.all_to_all(
@@ -235,8 +1177,8 @@
         grad_inner_two = column_outer(own_two_grad, own_fine_one)
         grad_inner_three = column_outer(own_three_grad, own_fine_two)
         resid_grad = resid_back.astype(jnp.float32)
-        back_pull = jax.vjp(lambda coef: upsample(coef, L), theta[:, :KB])[1]
-        fore_pull = jax.vjp(lambda coef: upsample(coef, AHEAD_TIMES), theta[:, KB:])[1]
+        back_pull = jax.vjp(lambda coef: upsample(coef, length), theta[:, :KB])[1]
+        fore_pull = jax.vjp(lambda coef: upsample(coef, ahead), theta[:, KB:])[1]
         back_coef_grad = back_pull(-resid_grad * mask)[0]
         fore_coef_grad = fore_pull(fore_back.astype(jnp.float32))[0]
         theta_grad = jnp.concatenate([back_coef_grad, fore_coef_grad], axis=1).astype(jnp.bfloat16)
@@ -265,10 +1207,10 @@
             column_sums(own_two_grad),
             column_sums(own_three_grad),
             lax.dynamic_update_slice_in_dim(
-                jnp.zeros((L,), jnp.float32), column_sums(back_grad), time_start, 0
+                jnp.zeros((length,), jnp.float32), column_sums(back_grad), time_start, 0
             ),
             lax.dynamic_update_slice_in_dim(
-                jnp.zeros((AHEAD_TIMES,), jnp.float32), column_sums(predict_cotan), predict_onset, 0
+                jnp.zeros((ahead,), jnp.float32), column_sums(predict_cotan), predict_onset, 0
             ),
         )
         bias_totals = tuple((total + term for total, term in zip(bias_totals, bias_terms)))
@@ -341,54 +1283,23 @@
     )
 
 
+def fits(nn, nw, series, padding, first, first_bias, *rest):
+    hid, length = first_bias.shape[0], series.shape[1]
+    paired = all(k & (k - 1) == 0 for k in (nn, nw)) and nw % 2 == 0
+    paired = paired and len(bits(nn)) == 2 and len(bits(nw // 2)) == 2
+    return paired and hid % (16 * nn * nw) == 0 and length % (POOL * nn) == 0 and series.shape[0] % LANE == 0
+
+
 def solution(mesh):
-    in_specs = (
-        P(("wide", "narrow"), None),
-        P("wide"),
-        P(("wide", "narrow"), None),
-        P(),
-        P(("wide", "narrow"), None),
-        P(),
-        P(("wide", "narrow"), None),
-        P(),
-        P(("wide", "narrow"), None),
-        P(),
-        P("wide", "narrow"),
-        P(),
-        P(("wide", "narrow"), None),
-        P(),
-        P(("wide", "narrow"), None),
-        P(),
-        P("wide", "narrow"),
-        P(),
-        P("wide", "narrow"),
-        P(),
-        P("wide", "narrow"),
-        P("wide", "narrow"),
-    )
-    out_specs = (
-        P("wide", "narrow"),
-        P("wide", "narrow"),
-        P(("wide", "narrow"), None),
-        P(("wide", "narrow"), None),
-        P(),
-        P(("wide", "narrow"), None),
-        P(),
-        P(("wide", "narrow"), None),
-        P(),
-        P(("wide", "narrow"), None),
-        P(),
-        P("wide", "narrow"),
-        P(),
-        P(("wide", "narrow"), None),
-        P(),
-        P(("wide", "narrow"), None),
-        P(),
-        P("wide", "narrow"),
-        P(),
-        P("wide", "narrow"),
-        P(),
-    )
-    return jax.shard_map(
-        on_device, mesh=mesh, in_specs=in_specs, out_specs=out_specs, check_vma=False
-    )
+    both, rows = P(("wide", "narrow"), None), P("wide", "narrow")
+    in_specs = (both, P("wide"))
+    in_specs += (both, P()) * 4 + (rows, P()) + (both, P()) * 2 + (rows, P()) * 2 + (rows, rows)
+    out_specs = (rows, rows, both) + (both, P()) * 4 + (rows, P()) + (both, P()) * 2 + (rows, P()) * 2
+    nn, nw = mesh.shape["narrow"], mesh.shape["wide"]
+
+    def body(*args):
+        if fits(nn, nw, *args):
+            return fast(nn, nw, *args)
+        return general(*args)
+
+    return jax.shard_map(body, mesh=mesh, in_specs=in_specs, out_specs=out_specs, check_vma=False)

time: 1960 us -> 169 us (0.09)
  waiting for transfers between devices: 693 us -> 0 us
  blocking collectives: 511 us -> 0 us
  local copies, waits for them, and re-layouts: 373 us -> 6.2 us
  Pallas kernels: 0 us -> 162 us
  other arithmetic: 145 us -> 0 us
  matrix products: 142 us -> 0 us
  starting transfers between devices: 67.9 us -> 0 us
    reduce_scatter x18 -> x0, waiting for transfers between devices: 657 us -> none  [the longest x1 136 us: on_device(): lax.psum_scatter(grad_weight_one, ('wide', 'narrow'), scatter_dimension=0...]
    all_gather x9 -> x0, blocking collectives: 471 us -> none  [the longest x1 75.6 us: on_device(): lax.all_gather(coarse_first, ('wide', 'narrow'), axis=0, tiled=True)]
    pallas_call x0 -> x2, Pallas kernels: none -> 162 us  [the longest x1 160 us: fast(): pl.pallas_call(functools.partial(whole, c), out_shape=(S((piece, nn * row...]
    dot_general x108 -> x0, matrix products: 142 us -> none  [the longest x36 48.7 us: project_rows(): lax.dot_general(rows_in, matrix, (((1,), (1,)), ((), ())), preferred_elem...]
    reshape x39 -> x0, local copies, waits for them, and re-layouts: 94.6 us -> none  [the longest x12 30 us: upsample(): preceding = jnp.repeat(padded[:, :coef_count], stride, axis=1)]
    convert_element_type x32 -> x0, local copies, waits for them, and re-layouts: 70.5 us -> none  [the longest x8 21.4 us: on_device(): resid_grad = resid_back.astype(jnp.float32)]
    all_to_all x16 -> x0, starting transfers between devices: 65.6 us -> none  [the longest x4 16.9 us: on_device(): lax.all_to_all(residual_here.astype(jnp.bfloat16), 'narrow', split_axis=1...]
    reduce_sum x20 -> x0, other arithmetic: 51.3 us -> none  [the longest x14 23.8 us: column_sums(): return jnp.sum(values.astype(jnp.float32), axis=0)]
  transfers between devices with their start and end apart: 35 -> 0, of which waited for: 14 -> 0; matrix products, arithmetic and copies ran while one was open for 26% -> 0% of each run, Pallas kernels for 0% -> 0%
where the time goes in v3:
time: 169 us
  Pallas kernels  162 us (96%)
  local copies, waits for them, and re-layouts  6.2 us (4%)
    pallas_call x1, Pallas kernels, fast(): pl.pallas_call(functools.partial(whole, c), out_shape=(S((piece, nn * row...  160 us
    unnamed x7, local copies, waits for them, and re-layouts  6.2 us

profile of v3, /device:TPU:0, one launch (start us, length us, event | category | flops | bytes accessed | tf_op | source)
XLA Modules:
  0.0 169.1 jit_solution(13322162942609563508)
XLA Ops:
  0.7 160.0 %shard_map.409 = (bf16[900,1536]{1,0:T(8,128)(2,1)}, f32[180,1536]{1,0:T(8,128)}, bf16[3600,384]{1,0:T(8,128)(2,1)}, f32[16,3584]{1,0:T(8,128)}, f32[64,900]{1,0...) custom-call(s32[1536]{0:T(1024)} %refs_0_.1, ...), custom_call_target="tpu_custom_call" | custom-call | tf_op jit(solution)/shard_map/pallas_call | solution.py:922
  160.7 2.1 %shard_map.410 = (f32[16,900]{1,0:T(8,128)}, f32[512]{0:T(512)}, f32[16,512]{1,0:T(8,128)}, f32[512]{0:T(512)}, f32[16,512]{1,0:T(8,128)}, /*index=5*/f32[512]{0...) custom-call(f32[16,3584]{1,0:T(8,128)} %get-tuple-element.50.refs_0_, ...), custom_call_target="tpu_custom_call" | custom-call | tf_op jit(solution)/shard_map/pallas_call | solution.py:945
  162.9 0.0 copy-start.1
  162.9 0.0 copy-start
  162.9 3.7 %copy.50 = bf16[1536,900]{0,1:T(8,128)(2,1)} copy(bf16[1536,900]{0,1:T(8,128)(2,1)} %bitcast.6) | data formatting | bytes 5529600
  166.5 0.0 copy-done.1
  166.5 1.0 copy.51
  167.5 0.0 copy-done
  167.5 1.5 copy.52
Async XLA Ops:
  162.9 3.7 %copy-start.1 = (f32[180,1536]{1,0:T(8,128)S(1)}, f32[180,1536]{1,0:T(8,128)}, u32[]{:S(2)}) copy-start(f32[180,1536]{1,0:T(8,128)} %get-tuple-element.48) | copy-start | bytes 3317764
  162.9 4.7 %copy-start = (bf16[3600,384]{1,0:T(8,128)(2,1)S(1)}, bf16[3600,384]{1,0:T(8,128)(2,1)}, u32[]{:S(2)}) copy-start(bf16[3600,384]{1,0:T(8,128)(2,1)} %get-tuple-element.49) | copy-start | bytes 8294404

commit v4 on v3

--- a/solution.py
+++ b/solution.py
@@ -239,8 +239,8 @@
         pick_in, mix_in, series, grad, fut_in, ff, fk, fo,
         left_out, pred_out, tid_out, om, of, ok, oo, obias, chunk_hbm, land_s,
         pick, mix_b, ser, chunk, land_g, bg, fut, wmid, wf, wk, wo, part3, land3, f3a, tw, twa,
-        pre, act, pooled, pred, gf, gk, go, cm, cf, ck, co, nm, zm, zf, nf, zk, zo,
-        temp, temp2, grads, sfore, pgb, pool, pads, brow, erow, bcol, ecol, bt, bl,
+        pre, act, pooled, pred, gf, gk, go, cm, cf, ck, co, nm, zm, zi, ni, zf, nf, zk, zo,
+        temp, temp3, temp4, temp2, grads, sfore, pgb, pool, pads, brow, erow, bcol, ecol, bt, bl,
         p1, p2, p3, p4, p5, p6, q0, q1, q2, q3, q4, q5, q6, q7, q8, q9, mix_f, all_f, sends, recvs, own,
     ) = refs
     nn, nc, rows, piece, part, hid, pw, bw = c.nn, c.nc, c.rows, c.piece, c.part, c.hid, c.pw, c.bw
@@ -253,6 +253,7 @@
     orders = (near, near[::-1])
     far, back_far = bits(nc), bits(nc)[::-1]
     half_lane = [ds(0, c.half), ds(c.half, c.off[-1] - c.half)]
+    half_outer = [ds(0, c.off[4] // 2), ds(c.off[4] // 2, c.off[4] // 2)]
     halves = lambda count: [ds(0, count // 2), ds(count // 2, count // 2)]
 
     def local(src, dst):
@@ -282,21 +283,27 @@
     def row_mask(j, r, unit):
         return steps(unit, rows) + (j * piece + r) >= pads[:, lanes(n)]
 
-    def activate(k, out):
-        def body(r, unit):
-            at = ds(r, unit)
-            v = pre[k, at, :] + bcol[at, k : k + 1]
-            pre[k, at, :] = v
-            act[out, at, :] = (v * jax.nn.sigmoid(v)).astype(BF16)
-
-        row_loop(hid, 32, body)
-
-    def sloped(k, out):
-        def body(r, unit):
-            at = ds(r, unit)
-            grads[out, at, :] = (temp[at, :] * slope(pre[k, at, :])).astype(BF16)
-
-        row_loop(hid, 32, body)
+    def settle(k, r, value, out):
+        v = value + bcol[r, k : k + 1]
+        pre[k, r, :] = v
+        act[out, r, :] = (v * jax.nn.sigmoid(v)).astype(BF16)
+
+    tall = 2 * c.hw
+    bands = [ds(z * tall, tall) for z in range(nc)]
+
+    def weight_rows(k, z):
+        return wmid[z, :, :, :, c.off[k] : c.off[k + 1]].reshape(tall, c.off[k + 1] - c.off[k])
+
+    def weight_columns(k, r):
+        return wmid[:, :, :, :, c.off[k] + r.start : c.off[k] + r.start + r.size].reshape(hid, r.size)
+
+    def layer(k, x, out):
+        for z, r in enumerate(bands):
+            settle(k, r, dot_nn(weight_rows(k, z), x[...]), out)
+
+    def layer_back(k, x, j, out):
+        for r in bands:
+            grads[out, r, :] = (dot_tn(weight_columns(k, r), x[...]) * slope(pre[j, r, :])).astype(BF16)
 
     def sums(value):
         return dot_nt(jnp.ones((8, value.shape[1]), BF16), value)[0:1]
@@ -322,7 +329,6 @@
     slot[:, c.off[3] : c.off[3] + c.bcount] = p4[:, : c.bcount]
     slot[:, c.off[3] + bw : c.off[3] + bw + p4.shape[1] - c.bcount] = p4[:, c.bcount :]
     net.meet()
-
     z_mid = Gather(net, net.chips, far, lambda e: wmid.at[chip ^ e, core, n])
 
     def gather_mid(e):
@@ -345,6 +351,22 @@
         Gather(net, net.narrow, order, lambda m, h=h: wf.at[n ^ m, chip, core, h], ff.at[h])
         for order, h in zip(orders, halves(c.hw))
     ]
+    cuts = list(range(0, piece, up(piece // 4, LANE))) + [piece]
+    cuts = [ds(a, b - a) for a, b in zip(cuts[:-1], cuts[1:])]
+    c_ga = local(grad.at[:, lanes(n)], land_g.at[n])
+    a_ga, a_sa = [], []
+
+    def exchange_grad(k):
+        h = cuts[k]
+        for d in range(1, nn):
+            a_ga.append(send(grad.at[h, lanes(n ^ d)], land_g.at[n, h], net.narrow(d)))
+
+    def exchange_series(k):
+        h = cuts[k]
+        for d in range(1, nn):
+            a_sa.append(send(chunk_hbm.at[n ^ d, h], land_s.at[h, lanes(n)], net.narrow(d)))
+
+    exchange_grad(3)
     c_small = [
         local(x, y)
         for x, y in zip((pads_in, b1, b2, b3, b4, b5, b6, b7, fkb, fob), (q0, q1, q2, q3, q4, q5, q6, q7, q8, q9))
@@ -385,7 +407,6 @@
     first_step = lax.broadcasted_iota(jnp.int32, (c.poolw, piece), 0) * POOL
     behind = lax.broadcasted_iota(jnp.int32, (c.poolw, piece), 1) - first_step
     pool[...] = jnp.where((behind >= 0) & (behind < POOL), 1.0 / POOL, 0.0).astype(BF16)
-
     pull_first(z_k)
     others = [m for m in n_mid if m]
     pull_first([g for m in others[:-1] for g in n_mid[m]])
@@ -410,26 +431,10 @@
     for j in range(nn // 2):
         cut_piece(j)
     pull_first(n_mid[others[-1]])
-    third = up(piece // 3, 16)
-    thirds = [ds(0, third), ds(third, third), ds(2 * third, piece - 2 * third)]
-    c_ga = local(grad.at[:, lanes(n)], land_g.at[n])
-    a_ga, a_sa = [], []
-
-    def exchange_grad(k):
-        h = thirds[k]
-        for d in range(1, nn):
-            a_ga.append(send(grad.at[h, lanes(n ^ d)], land_g.at[n, h], net.narrow(d)))
-
-    def exchange_series(k):
-        h = thirds[k]
-        for d in range(1, nn):
-            a_sa.append(send(chunk_hbm.at[n ^ d, h], land_s.at[h, lanes(n)], net.narrow(d)))
-
     exchange_grad(0)
-
     for j in range(nn // 2, nn):
         cut_piece(j)
-    c_chunk = local(chunk, chunk_hbm)
+    c_chunk = [local(chunk, chunk_hbm), local(chunk.at[n], land_s.at[:, lanes(n)])]
     for j in range(nn):
         pooled[j * c.poolw : (j + 1) * c.poolw, :] = dot_nn(pool[...], chunk[j]).astype(BF16)
     pull_rest(z_k)
@@ -450,7 +455,6 @@
         pull_rest(n_mid[e])
         block = wmid.at[chip ^ e, core]
         a_cm.append(send(block, block, net.sibling()))
-
     for copy in c_tables:
         copy.wait()
     for copy in a_ck:
@@ -480,26 +484,23 @@
     for s in s_part:
         s.start()
     exchange_grad(1)
-
     for copy in a_cm:
         copy.wait_recv()
-    pre[0] = dot_nn(weight(0), pooled[...])
-    activate(0, 0)
+    layer(0, pooled, 0)
     z_f.pull(z_f.masks()[0])
     hand_over(z_f.masks()[0])
-    pre[1] = dot_nn(weight(1), act[0])
-    activate(1, 1)
-    pre[2] = dot_nn(weight(2), act[1])
-    activate(2, 2)
+    layer(1, act.at[0], 1)
+    layer(2, act.at[1], 2)
     theta = act.at[6]
-    theta[...] = (dot_tn(weight(3), act[2]) + bcol[:, 6:7]).astype(BF16)
+    for r in bands:
+        theta[r, :] = (dot_tn(weight_columns(3, r), act[2]) + bcol[r, 6:7]).astype(BF16)
     for s in s_part:
         s.finish()
         if s.step < len(near):
             s.start()
     exchange_grad(2)
-    c_chunk.wait()
-
+    for copy in c_chunk:
+        copy.wait()
     c_pick.wait()
     c_mix.wait()
 
@@ -512,36 +513,30 @@
             x = chunk[j, at, :].astype(F32) - temp[at, :] * c.scale
             chunk[j, at, :] = jnp.where(row_mask(j, r, unit), x, 0).astype(BF16)
 
-        row_loop(piece, 48, body)
+        row_loop(piece, 144, body)
 
     each(nn, residual)
     used = ds(0, c.used)
-    twa[n, : c.used, :] = tw[n, : c.used, :]
+    twa[used, lanes(n)] = tw[n, : c.used, :]
     for m in z_f.masks()[1:]:
         z_f.pull(m)
         hand_over(m)
     early = len(net.copies)
-
     for copy in a_cf:
         copy.wait_recv()
-    pre[3] = jnp.zeros((hid, rows), F32)
-
-    def lift(j):
-        pre[3] += dot_nn(wf[j].reshape(hid, piece), chunk[j])
-
-    each(nn, lift)
-    activate(3, 3)
-    pre[4] = dot_nn(weight(4), act[3])
-    activate(4, 4)
-    pre[5] = dot_nn(weight(5), act[4])
-    activate(5, 5)
+    for z, r in enumerate(bands):
+        total = dot_nn(wf[0, z].reshape(tall, piece), chunk[0])
+        for j in range(1, nn):
+            total += dot_nn(wf[j, z].reshape(tall, piece), chunk[j])
+        settle(3, r, total, 3)
+    layer(4, act.at[3], 4)
+    layer(5, act.at[4], 5)
     f3a[:, lanes(n)] = act[5]
     n_f3 = [
         Gather(net, net.narrow, order, lambda m, h=h: f3a.at[h, lanes(n ^ m)], act.at[5, h])
         for order, h in zip(orders, halves(hid))
     ]
-    exchange_series(0)
-
+    a_tw = [send(tw.at[n ^ d, used], twa.at[used, lanes(n)], net.narrow(d)) for d in range(1, nn)]
     while s_part[0].step < len(near):
         for s in s_part:
             s.finish()
@@ -557,22 +552,55 @@
         return body
 
     cut = (hid + c.fcount) // 2
-    row_loop(cut, 32, collect(ds(0, cut), k3[0]))
-    row_loop(hid - cut, 32, collect(ds(cut, hid - cut), k3[1]))
+    row_loop(cut, 96, collect(ds(0, cut), k3[0]))
+    row_loop(hid - cut, 96, collect(ds(cut, hid - cut), k3[1]))
     sfore[...] = (part3[n, hid:, :].astype(F32) + land3[k3[1], hid:, :].astype(F32)).astype(BF16)
-    temp[:hid, :] = dot_tn(weight(5), grads[0])
-    sloped(4, 1)
-    temp[:hid, :] = dot_tn(weight(4), grads[1])
-    sloped(3, 2)
-
-    pull_first(n_f3)
-    a_tw = [send(tw.at[n ^ d, used], twa.at[n, used], net.narrow(d)) for d in range(1, nn)]
-    exchange_series(1)
+    layer_back(5, grads.at[0], 4, 1)
+    layer_back(4, grads.at[1], 3, 2)
     r_cf = []
     for j in range(nn):
         gf[j] = dot_nt(grads[2], chunk[j]).astype(BF16).reshape(nc, 2, c.hw, piece)
         r_cf.append(send(gf.at[j, :, 1 - core], cf.at[j], net.sibling()))
-
+    for copy in net.copies[:early]:
+        copy.wait_send()
+    put_weight(5, dot_nt(grads[0], act[4]))
+    put_weight(4, dot_nt(grads[1], act[3]))
+    inner, outer = ds(c.off[4], c.off[-1] - c.off[4]), ds(0, c.off[4])
+    r_ci = send(wmid.at[:, 1 - core, :, :, inner], cm.at[:, :, :, inner], net.sibling())
+
+    def add_f(j):
+        for z in range(nc):
+            cf[j, z] = (gf[j, z, core].astype(F32) + cf[j, z].astype(F32)).astype(BF16)
+
+    for j in range(nn):
+        r_cf[j].wait_recv()
+    each(nn, add_f)
+
+    def add_zf(e, k):
+        def body(j):
+            cf[j, chip ^ e] = (cf[j, chip ^ e].astype(F32) + zf[k, j].astype(F32)).astype(BF16)
+
+        each(nn, body)
+
+    r_zf = Scatter(net, net.chips, back_far, lambda e: cf.at[:, chip ^ e], lambda k: zf.at[k], add_zf)
+    r_zf.start()
+    pull_first(n_f3)
+    exchange_series(0)
+    r_ci.wait_recv()
+    for z in range(nc):
+        both = wmid[z, core, :, :, inner].astype(F32) + cm[z, :, :, inner].astype(F32)
+        cm[z, :, :, inner] = both.astype(BF16)
+
+    def add_zi(e, k):
+        both = cm[chip ^ e, :, :, inner].astype(F32) + zi[k].astype(F32)
+        cm[chip ^ e, :, :, inner] = both.astype(BF16)
+
+    def add_ni(m, k):
+        both = cm[chip, n ^ m, :, inner].astype(F32) + ni[k].astype(F32)
+        cm[chip, n ^ m, :, inner] = both.astype(BF16)
+
+    r_zi = Scatter(net, net.chips, back_far, lambda e: cm.at[chip ^ e, :, :, inner], lambda k: zi.at[k], add_zi)
+    r_zi.start()
     c_ga.wait()
     for copy in a_ga:
         copy.wait_recv()
@@ -586,53 +614,27 @@
             x = land_g[j, at, :].astype(F32) + temp[at, :]
             land_g[j, at, :] = jnp.where(row_mask(j, r, unit), x, 0).astype(BF16)
 
-        row_loop(piece, 48, body)
+        row_loop(piece, 144, body)
         pull = (dot_tn(mix_b[j], land_g[j]) * -c.scale).astype(BF16)
         temp2[...] += dot_tn(pick[j, :, :bw], pull)
 
-    each(nn // 2, resid_grad)
-    for j in range(nn):
-        r_cf[j].wait_recv()
-
-    def add_f(j):
-        for z in range(nc):
-            cf[j, z] = (gf[j, z, core].astype(F32) + cf[j, z].astype(F32)).astype(BF16)
-
-    each(nn, add_f)
-
-    def add_zf(e, k):
-        def body(j):
-            cf[j, chip ^ e] = (cf[j, chip ^ e].astype(F32) + zf[k, j].astype(F32)).astype(BF16)
-
-        each(nn, body)
-
-    r_zf = Scatter(net, net.chips, back_far, lambda e: cf.at[:, chip ^ e], lambda k: zf.at[k], add_zf)
-    r_zf.start()
-    each(nn - nn // 2, lambda i: resid_grad(i + nn // 2))
-
+    each(nn, resid_grad)
     dth = grads.at[3]
     dth[:bw, :] = temp2[...].astype(BF16)
     dth[bw:, :] = jnp.zeros_like(dth[bw:, :])
     dth[bw : bw + c.fcount, :] = sfore[...]
-    temp[:hid, :] = dot_nn(weight(3), dth[...])
-    sloped(2, 4)
-    temp[:hid, :] = dot_tn(weight(2), grads[4])
-    sloped(1, 5)
-    temp[:hid, :] = dot_tn(weight(1), grads[5])
-    sloped(0, 6)
+    for z, r in enumerate(bands):
+        grads[4, r, :] = (dot_nn(weight_rows(3, z), dth[...]) * slope(pre[2, r, :])).astype(BF16)
+    layer_back(2, grads.at[4], 1, 5)
+    layer_back(1, grads.at[5], 0, 6)
     pgb[...] = dot_tn(weight(0), grads[6]).astype(BF16)
-    for copy in net.copies[: early]:
-        copy.wait_send()
-    put_weight(5, dot_nt(grads[0], act[4]))
-    put_weight(4, dot_nt(grads[1], act[3]))
     put_weight(3, dot_nt(act[2], dth[...]))
     put_weight(2, dot_nt(grads[4], act[1]))
     put_weight(1, dot_nt(grads[5], act[0]))
     put_weight(0, dot_nt(grads[6], pooled[...]))
-    r_cm = send(wmid.at[:, 1 - core], cm, net.sibling())
-
+    r_cm = send(wmid.at[:, 1 - core, :, :, outer], cm.at[:, :, :, outer], net.sibling())
     bt[0, ds(4 + n, 1), :piece] = sums(bg[...])
-    bt[0, ds(4 + nn + n, 1), :part] = sums(fut[...])
+    bt[0, ds(4 + n, 1), pw : pw + part] = sums(fut[...])
     for k, slot_k in enumerate((6, 5, 4, 3, 2, 1, 0)):
         bt[0, k // 2 : k // 2 + 1, (k % 2) * hid : (k % 2 + 1) * hid] = sums(grads[slot_k])
     travel = [net.sibling()] + [net.narrow(b) for b in near] + [net.chips(b) for b in back_far]
@@ -648,13 +650,10 @@
         bt[k + 1] = bt[k] + bl[k]
 
     send_bias()
-    pull_rest(n_f3)
-    gk[...] = dot_nt(f3a[...], bg[...]).astype(BF16).reshape(nc, 2, c.hw, piece)
-    go[...] = dot_nt(f3a[...], fut[...]).astype(BF16).reshape(nc, 2, c.hw, part)
-    r_ck = [send(gk.at[:, 1 - core], ck, net.sibling()), send(go.at[:, 1 - core], co, net.sibling())]
     r_cm.wait_recv()
     for z in range(nc):
-        cm[z] = (wmid[z, core].astype(F32) + cm[z].astype(F32)).astype(BF16)
+        both = wmid[z, core, :, :, outer].astype(F32) + cm[z, :, :, outer].astype(F32)
+        cm[z, :, :, outer] = both.astype(BF16)
 
     def add_nm(m, k, h):
         cm[:, n ^ m, :, h] = (cm[:, n ^ m, :, h].astype(F32) + nm[k, :, :, h].astype(F32)).astype(BF16)
@@ -666,14 +665,21 @@
             lambda k, h=h: nm.at[k, :, :, h],
             lambda m, k, h=h: add_nm(m, k, h),
         )
-        for order, h in zip(orders, half_lane)
+        for order, h in zip(orders, half_outer)
     ]
     for s in r_nm:
         s.start()
-    exchange_series(2)
+    exchange_series(1)
     add_bias()
     send_bias()
-
+    pull_rest(n_f3)
+    gk[...] = dot_nt(f3a[...], bg[...]).astype(BF16).reshape(nc, 2, c.hw, piece)
+    go[...] = dot_nt(f3a[...], fut[...]).astype(BF16).reshape(nc, 2, c.hw, part)
+    r_ck = [send(gk.at[:, 1 - core], ck, net.sibling()), send(go.at[:, 1 - core], co, net.sibling())]
+    r_zf.finish()
+    r_zf.start()
+    r_zi.finish()
+    r_zi.start()
     for copy in r_ck:
         copy.wait_recv()
     for z in range(nc):
@@ -699,66 +705,62 @@
             x = jnp.where(row_mask(j, r, unit), x, 0).astype(BF16)
             ser[j * piece + r : j * piece + r + unit, :] = x
 
-    def outputs(j):
-        temp[:piece, :] = dot_nn(mix_b[n], twa[j])
-
-        def first(r, unit):
-            at = ds(r, unit)
-            x = chunk[j, at, :].astype(F32) - temp[at, :] * c.scale
-            chunk[j, at, :] = x.astype(BF16)
-
-        row_loop(piece, 48, first)
-        temp[:piece, :] = dot_tn(wk[...].reshape(hid, piece), f3a[:, lanes(j)])
-
-        def second(r, unit):
-            at = ds(r, unit)
-            x = chunk[j, at, :].astype(F32) - (temp[at, :] + ecol[at, 0:1])
-            mask = steps(unit, rows) + (n * piece + r) >= pads[:, lanes(j)]
-            chunk[j, at, :] = jnp.where(mask, x, 0).astype(BF16)
-
-        row_loop(piece, 48, second)
-        pred[:, lanes(j)] = (
-            dot_nn(mix_f[...], twa[j]) * c.scale_f
-            + dot_tn(wo[...].reshape(hid, part), f3a[:, lanes(j)])
-            + ecol[pw : pw + part, 0:1]
-        )
-
-    for j in range(nn // 2):
-        series_grad(j)
-    r_zf.finish()
-    r_zf.start()
+    def outputs(k):
+        h = cuts[k]
+        for copy in a_sa[k * (nn - 1) : (k + 1) * (nn - 1)]:
+            copy.wait_recv()
+        local(land_s.at[h], bg.at[h]).wait()
+        stop = h.start + h.size
+        marks = [r for r in range(h.start, stop, LANE) if stop - r >= LANE // 2] + [stop]
+        for low, high in zip(marks[:-1], marks[1:]):
+            temp3[: high - low, :] = dot_nn(mix_b[n, low:high, :], twa[...])
+            temp4[: high - low, :] = dot_tn(wk[:, :, :, low:high].reshape(hid, high - low), f3a[...])
+
+            def body(r, unit, low=low):
+                at, here = ds(low + r, unit), ds(r, unit)
+                x = (bg[at, :].astype(F32) - temp3[here, :] * c.scale).astype(BF16).astype(F32)
+                x = x - (temp4[here, :] + ecol[at, 0:1])
+                mask = steps(unit, nn * rows) + (n * piece + low + r) >= pads[...]
+                bg[at, :] = jnp.where(mask, x, 0).astype(BF16)
+
+            row_loop(high - low, 32, body)
+        local(bg.at[h], left_out.at[h])
+
+    def forecast():
+        fore = dot_nn(mix_f[...], twa[...]) * c.scale_f
+        pred[...] = fore + dot_tn(wo[...].reshape(hid, part), f3a[...]) + ecol[pw : pw + part, 0:1]
+
+    def add_nf(m, k, h):
+        cf[n ^ m, chip, h, :] = (cf[n ^ m, chip, h, :].astype(F32) + nf[k, h, :].astype(F32)).astype(BF16)
+
+    def add_zm(e, k):
+        both = cm[chip ^ e, n, :, outer].astype(F32) + zm[k].astype(F32)
+        cm[chip ^ e, n, :, outer] = both.astype(BF16)
+
+    r_zm = Scatter(net, net.chips, back_far, lambda e: cm.at[chip ^ e, n, :, outer], lambda k: zm.at[k], add_zm)
+    r_nf = [
+        Scatter(
+            net, net.narrow, order,
+            lambda m, h=h: cf.at[n ^ m, chip, h],
+            lambda k, h=h: nf.at[k, h],
+            lambda m, k, h=h: add_nf(m, k, h),
+        )
+        for order, h in zip(orders, halves(c.hw))
+    ]
     for s in r_zk:
         s.start()
-    for j in range(nn // 2, nn):
-        series_grad(j)
-    c_tid = local(ser, tid_out)
     for s in r_nm:
         s.finish()
         s.start()
     add_bias()
     send_bias()
-
-
-    def add_nf(m, k, h):
-        cf[n ^ m, chip, h, :] = (cf[n ^ m, chip, h, :].astype(F32) + nf[k, h, :].astype(F32)).astype(BF16)
-
-    def add_zm(e, k):
-        cm[chip ^ e, n] = (cm[chip ^ e, n].astype(F32) + zm[k].astype(F32)).astype(BF16)
-
-    r_nf = lambda: [
-        Scatter(
-            net, net.narrow, order,
-            lambda m, h=h: cf.at[n ^ m, chip, h],
-            lambda k, h=h: nf.at[k, h],
-            lambda m, k, h=h: add_nf(m, k, h),
-        )
-        for order, h in zip(orders, halves(c.hw))
-    ]
-    r_zm = Scatter(net, net.chips, back_far, lambda e: cm.at[chip ^ e, n], lambda k: zm.at[k], add_zm)
-    for copy in a_tw:
-        copy.wait_recv()
+    exchange_series(2)
+    r_zi.finish()
+    r_ni = Scatter(net, net.narrow, near, lambda m: cm.at[chip, n ^ m, :, inner], lambda k: ni.at[k], add_ni)
+    r_ni.start()
+    for j in range(nn // 2):
+        series_grad(j)
     r_zf.finish()
-    r_nf = r_nf()
     for s in r_nf:
         s.start()
     for s in r_nm:
@@ -766,32 +768,35 @@
     r_zm.start()
     add_bias()
     send_bias()
+    exchange_series(3)
+    for j in range(nn // 2, nn):
+        series_grad(j)
+    c_tid = local(ser, tid_out)
+    for copy in a_tw:
+        copy.wait_recv()
+    forecast()
+    c_pred = local(pred, pred_out)
     for s in r_zk:
         s.finish()
         s.start()
-    for copy in a_sa:
-        copy.wait_recv()
-    c_land = [local(chunk_hbm.at[n], chunk.at[n])]
-    c_land += [local(land_s.at[:, lanes(n ^ d)], chunk.at[n ^ d]) for d in range(1, nn)]
-    for copy in c_land:
-        copy.wait()
-
-    each(nn // 2, outputs)
+    outputs(0)
     for s in r_nf:
         s.finish()
         s.start()
+    r_ni.finish()
+    r_ni.start()
+    outputs(1)
     r_zm.finish()
     r_zm.start()
     add_bias()
     send_bias()
-    each(nn - nn // 2, lambda i: outputs(i + nn // 2))
-    c_left = [local(chunk.at[j], left_out.at[:, lanes(j)]) for j in range(nn)]
-    c_pred = local(pred, pred_out)
-
+    outputs(2)
+    outputs(3)
     for s in r_zk:
         s.finish()
     ok[...] = ck[chip].astype(F32)
     oo[...] = co[chip].astype(F32)
+    r_ni.finish()
     for s in r_nf:
         s.finish()
     of[...] = cf[n, chip].astype(F32)
@@ -803,10 +808,34 @@
 
 
 def finish(c, *refs):
-    om, of, ok, oo, obias = refs[:5]
-    (
-        g1, v1, g2, v2, g3, v3, g4, v4, gf, vf1, g5, vf2, g6, vf3, gk, vk, go, vo,
-    ) = refs[5:]
+    large_in, small_in, large_out, small_out = refs[:3], refs[3:8], refs[8:11], refs[11:29]
+    held, (om, of, ok, oo, obias), given, sems = refs[29:32], refs[32:37], refs[37:55], refs[55]
+    g1, v1, g2, v2, g3, v3, g4, v4, gf, vf1, g5, vf2, g6, vf3, gk, vk, go, vo = given
+    arriving = [
+        pltpu.make_async_copy(src, dst, sems.at[24 + k])
+        for k, (src, dst) in enumerate(zip(small_in, (om, of, ok, oo, obias)))
+    ]
+    leaving = [
+        pltpu.make_async_copy(src, dst, sems.at[29 + k]) for k, (src, dst) in enumerate(zip(given, small_out))
+    ]
+    for copy in arriving:
+        copy.start()
+    pieces = []
+    for a, (src, via, dst) in enumerate(zip(large_in, held, large_out)):
+        size = up(-(-src.shape[0] // 4), 16)
+        for b, r in enumerate(range(0, src.shape[0], size)):
+            h = pl.ds(r, min(size, src.shape[0] - r))
+            k = 8 * a + 2 * b
+            pieces.append(
+                (
+                    pltpu.make_async_copy(src.at[h], via.at[h], sems.at[k]),
+                    pltpu.make_async_copy(via.at[h], dst.at[h], sems.at[k + 1]),
+                )
+            )
+    for inward, outward in pieces:
+        inward.start()
+    for copy in arriving:
+        copy.wait()
     nn, piece, part, hid, bw = c.nn, c.piece, c.part, c.hid, c.bw
     for j in range(nn):
         g1[:, j * c.pools : (j + 1) * c.pools] = om[:, j * c.poolw : j * c.poolw + c.pools]
@@ -824,7 +853,16 @@
     theta = obias[1:2, hid : 2 * hid]
     v4[...] = jnp.concatenate([theta[:, : c.bcount], theta[:, bw : bw + fore]], axis=1).reshape(v4.shape[0])
     vk[...] = jnp.concatenate([obias[4 + j : 5 + j, :piece] for j in range(nn)], axis=1).reshape(vk.shape[0])
-    vo[...] = jnp.concatenate([obias[4 + nn + j : 5 + nn + j, :part] for j in range(nn)], axis=1).reshape(vo.shape[0])
+    vo[...] = jnp.concatenate([obias[4 + j : 5 + j, c.pw : c.pw + part] for j in range(nn)], axis=1).reshape(vo.shape[0])
+    for copy in leaving:
+        copy.start()
+    for inward, outward in pieces:
+        inward.wait()
+        outward.start()
+    for inward, outward in pieces:
+        outward.wait()
+    for copy in leaving:
+        copy.wait()
 
 
 def fast(nn, nw, series, padding, *rest):
@@ -857,7 +895,7 @@
     anyspec = pl.BlockSpec(memory_space=pl.ANY)
     vspec = pl.BlockSpec(memory_space=pltpu.VMEM)
     S, V = jax.ShapeDtypeStruct, pltpu.VMEM
-    bs = (up(4 + 2 * nn, 8), max(2 * hid, pw))
+    bs = (up(4 + nn, 8), max(2 * hid, pw + up(part, LANE)))
     stages = 1 + len(bits(nn)) + len(bits(nc))
     gathers = (nc - 1) + 2 * nc * (nn - 1) + 2 * (nn - 1) + 3 * (nc - 1) + 2 + 2 * nc
     ncopies = gathers + 12 * (nn + nc) + 2 * nn * nc
@@ -878,7 +916,7 @@
         V((nn - 1, hid + fcount, rows), BF16),
         V((hid, nn * rows), BF16),
         V((nn, width, rows), BF16),
-        V((nn, width, rows), BF16),
+        V((width, nn * rows), BF16),
         V((6, hid, rows), F32),
         V((7, hid, rows), BF16),
         V((nn * poolw, rows), BF16),
@@ -890,13 +928,17 @@
         V((nn, nc, hw, piece), BF16),
         V((nc, hw, piece), BF16),
         V((nc, hw, part), BF16),
-        V((nn - 1, nc, hs, mw), BF16),
-        V((nc - 1, hs, mw), BF16),
+        V((nn - 1, nc, hs, off[4]), BF16),
+        V((nc - 1, hs, off[4]), BF16),
+        V((nc - 1, nn, hs, mw - off[4]), BF16),
+        V((nn - 1, hs, mw - off[4]), BF16),
         V((nc - 1, nn, hw, piece), BF16),
         V((nn - 1, hw, piece), BF16),
         V((nc - 1, hw, piece), BF16),
         V((nc - 1, hw, part), BF16),
-        V((max(piece, hid), rows), F32),
+        V((piece, rows), F32),
+        V((LANE + up(piece % LANE, 16), nn * rows), F32),
+        V((LANE + up(piece % LANE, 16), nn * rows), F32),
         V((bw, rows), F32),
         V((7, hid, rows), BF16),
         V((fcount, rows), BF16),
@@ -917,7 +959,7 @@
         V(all_f.shape[1:], BF16),
         pltpu.SemaphoreType.DMA((ncopies,)),
         pltpu.SemaphoreType.DMA((ncopies,)),
-        pltpu.SemaphoreType.DMA((40 + 2 * nn,)),
+        pltpu.SemaphoreType.DMA((40 + 8 * nn,)),
     ]
     leftover, pred, tid, om, of, ok, oo, obias, _, _ = pl.pallas_call(
         functools.partial(whole, c),
@@ -944,11 +986,16 @@
     params_like = (cf, cfb, cs, csb, ct, ctb, cb, cbb, ff, ffb, fs, fsb, ft, ftb, fk, fkb, fo, fob)
     outs = pl.pallas_call(
         functools.partial(finish, c),
-        out_shape=tuple(S(p.shape, F32) for p in params_like),
-        in_specs=[vspec] * 5,
-        out_specs=[vspec] * 18,
-    )(om, of, ok, oo, obias)
-    return (leftover.T, pred.T, tid.T) + tuple(outs)
+        out_shape=tuple(S(x.shape, x.dtype) for x in (leftover, pred, tid))
+        + tuple(S(p.shape, F32) for p in params_like),
+        in_specs=[anyspec] * 8,
+        out_specs=[anyspec] * 21,
+        scratch_shapes=[V(x.shape, x.dtype) for x in (leftover, pred, tid, om, of, ok, oo, obias)]
+        + [V(p.shape, F32) for p in params_like]
+        + [pltpu.SemaphoreType.DMA((48,))],
+        compiler_params=pltpu.CompilerParams(vmem_limit_bytes=60 << 20),
+    )(leftover, pred, tid, om, of, ok, oo, obias)
+    return (outs[0].T, outs[1].T, outs[2].T) + tuple(outs[3:])
 
 
 def upsample(coef, length):

time: 169 us -> 156 us (0.923)
  Pallas kernels: 162 us -> 155 us
  local copies, waits for them, and re-layouts: 6.2 us -> 0 us
    pallas_call x1, Pallas kernels: 160 us -> 148 us  [fast(): pl.pallas_call(functools.partial(whole, c), out_shape=(S((piece, nn * row...]
    unnamed x7 -> x0, local copies, waits for them, and re-layouts: 6.2 us -> none
    pallas_call x1, Pallas kernels: 2.14 us -> 6.46 us  [fast(): pl.pallas_call(functools.partial(finish, c), out_shape=tuple((S(x.shape,...]
where the time goes in v4:
time: 156 us
  Pallas kernels  155 us (99%)
    pallas_call x1, Pallas kernels, fast(): pl.pallas_call(functools.partial(whole, c), out_shape=(S((piece, nn * row...  148 us
    pallas_call x1, Pallas kernels, fast(): pl.pallas_call(functools.partial(finish, c), out_shape=tuple((S(x.shape,...  6.46 us

profile of v4, /device:TPU:0, one launch (start us, length us, event | category | flops | bytes accessed | tf_op | source)
XLA Modules:
  0.0 155.5 jit_solution(2372860796222703443)
XLA Ops:
  0.7 148.2 %shard_map.409 = (bf16[900,1536]{1,0:T(8,128)(2,1)}, f32[180,1536]{1,0:T(8,128)}, bf16[3600,384]{1,0:T(8,128)(2,1)}, f32[16,3584]{1,0:T(8,128)}, f32[64,900]{1,0...) custom-call(s32[1536]{0:T(1024)} %refs_0_.1, ...), custom_call_target="tpu_custom_call" | custom-call | tf_op jit(solution)/shard_map/pallas_call | solution.py:964
  148.9 6.5 %shard_map.410 = (bf16[900,1536]{1,0:T(8,128)(2,1)}, f32[180,1536]{1,0:T(8,128)}, bf16[3600,384]{1,0:T(8,128)(2,1)}, f32[16,900]{1,0:T(8,128)}, f32[512]{0:T(512...) custom-call(bf16[900,1536]{1,0:T(8,128)(2,1)} %get-tuple-element.50., ...), custom_call_target="tpu_custom_call" | custom-call | tf_op jit(solution)/shard_map/pallas_call | solution.py:987

commit v5 on v4

--- a/solution.py
+++ b/solution.py
@@ -310,14 +310,9 @@
 
     net.hail()
     c_mids = [local(x, y) for x, y in zip((w1, w2, w3, w4, w5, w6), (p1, p2, p3, p4, p5, p6))]
-    c_ser = local(series, ser)
-    c_bg = local(grad, bg)
-    c_fut = local(fut_in, fut)
     c_ff = local(ff, wf.at[n, chip, core])
     c_fk = local(fk, wk.at[chip, core])
     c_fo = local(fo, wo.at[chip, core])
-    c_pick = local(pick_in, pick)
-    c_mix = local(mix_in, mix_b)
     slot = wmid.at[chip, core, n]
     slot[...] = jnp.zeros_like(slot)
     for copy in c_mids:
@@ -351,8 +346,15 @@
         Gather(net, net.narrow, order, lambda m, h=h: wf.at[n ^ m, chip, core, h], ff.at[h])
         for order, h in zip(orders, halves(c.hw))
     ]
+    c_ser = local(series, ser)
+    c_bg = local(grad, bg)
+    c_fut = local(fut_in, fut)
+    c_pick = local(pick_in, pick)
+    c_mix = local(mix_in, mix_b)
     cuts = list(range(0, piece, up(piece // 4, LANE))) + [piece]
     cuts = [ds(a, b - a) for a, b in zip(cuts[:-1], cuts[1:])]
+    starts = [0, 2 * LANE, 3 * LANE, 5 * LANE, 6 * LANE, piece]
+    parts = [ds(a, b - a) for a, b in zip(starts[:-1], starts[1:])]
     c_ga = local(grad.at[:, lanes(n)], land_g.at[n])
     a_ga, a_sa = [], []
 
@@ -362,11 +364,10 @@
             a_ga.append(send(grad.at[h, lanes(n ^ d)], land_g.at[n, h], net.narrow(d)))
 
     def exchange_series(k):
-        h = cuts[k]
+        h = parts[k]
         for d in range(1, nn):
             a_sa.append(send(chunk_hbm.at[n ^ d, h], land_s.at[h, lanes(n)], net.narrow(d)))
 
-    exchange_grad(3)
     c_small = [
         local(x, y)
         for x, y in zip((pads_in, b1, b2, b3, b4, b5, b6, b7, fkb, fob), (q0, q1, q2, q3, q4, q5, q6, q7, q8, q9))
@@ -382,17 +383,18 @@
     brow[6:7, : c.bcount] = theta_bias[:, : c.bcount]
     brow[6:7, bw : bw + q4.shape[0] - c.bcount] = theta_bias[:, c.bcount :]
     bcol[...] = jnp.transpose(brow[...])
+    exchange_grad(3)
     z_mid.pull(z_mid.masks()[0])
     n_mid[z_mid.masks()[0]] = gather_mid(z_mid.masks()[0])
     z_k = [
         Gather(net, net.chips, far, lambda e: wk.at[chip ^ e, core], fk),
         Gather(net, net.chips, far, lambda e: wo.at[chip ^ e, core], fo),
     ]
+    pull_first(n_ff)
     pull_first(n_mid[0])
     for m in z_mid.masks()[1:]:
         z_mid.pull(m)
         n_mid[m] = gather_mid(m)
-    pull_first(n_ff)
     erow[...] = jnp.zeros_like(erow)
     for j in range(nn):
 
@@ -408,18 +410,20 @@
     behind = lax.broadcasted_iota(jnp.int32, (c.poolw, piece), 1) - first_step
     pool[...] = jnp.where((behind >= 0) & (behind < POOL), 1.0 / POOL, 0.0).astype(BF16)
     pull_first(z_k)
-    others = [m for m in n_mid if m]
-    pull_first([g for m in others[:-1] for g in n_mid[m]])
+    others = z_mid.masks()
+    for m in others[:-1]:
+        pull_first(n_mid[m])
     pull_rest(n_ff)
     c_ff.wait()
-    z_f = Gather(net, net.chips, far, lambda e: wf.at[:, chip ^ e, core])
+    z_f = [Gather(net, net.chips, far, lambda e, j=j: wf.at[j, chip ^ e, core]) for j in range(nn)]
     a_cf = []
 
-    def hand_over(e):
-        block = wf.at[:, chip ^ e, core]
+    def hand_over(j, e):
+        block = wf.at[j, chip ^ e, core]
         a_cf.append(send(block, block, net.sibling()))
 
-    hand_over(0)
+    for j in range(nn):
+        hand_over(j, 0)
     c_ser.wait()
 
     def cut_piece(j):
@@ -431,8 +435,9 @@
     for j in range(nn // 2):
         cut_piece(j)
     pull_first(n_mid[others[-1]])
+    cut_piece(nn // 2)
     exchange_grad(0)
-    for j in range(nn // 2, nn):
+    for j in range(nn // 2 + 1, nn):
         cut_piece(j)
     c_chunk = [local(chunk, chunk_hbm), local(chunk.at[n], land_s.at[:, lanes(n)])]
     for j in range(nn):
@@ -450,11 +455,6 @@
         bg[at, :] = jnp.where(mask, -bg[at, :].astype(F32), 0).astype(BF16)
 
     row_loop(piece, 16, negate)
-    a_cm = []
-    for e in n_mid:
-        pull_rest(n_mid[e])
-        block = wmid.at[chip ^ e, core]
-        a_cm.append(send(block, block, net.sibling()))
     for copy in c_tables:
         copy.wait()
     for copy in a_ck:
@@ -483,12 +483,20 @@
     ]
     for s in s_part:
         s.start()
+    bt[0, ds(4 + n, 1), :piece] = sums(bg[...])
+    bt[0, ds(4 + n, 1), pw : pw + part] = sums(fut[...])
     exchange_grad(1)
+    for j, g in enumerate(z_f):
+        g.pull(g.masks()[0])
+        hand_over(j, g.masks()[0])
+    a_cm = []
+    for e in n_mid:
+        pull_rest(n_mid[e])
+        block = wmid.at[chip ^ e, core]
+        a_cm.append(send(block, block, net.sibling()))
     for copy in a_cm:
         copy.wait_recv()
     layer(0, pooled, 0)
-    z_f.pull(z_f.masks()[0])
-    hand_over(z_f.masks()[0])
     layer(1, act.at[0], 1)
     layer(2, act.at[1], 2)
     theta = act.at[6]
@@ -498,7 +506,6 @@
         s.finish()
         if s.step < len(near):
             s.start()
-    exchange_grad(2)
     for copy in c_chunk:
         copy.wait()
     c_pick.wait()
@@ -516,19 +523,26 @@
         row_loop(piece, 144, body)
 
     each(nn, residual)
+    exchange_grad(2)
     used = ds(0, c.used)
     twa[used, lanes(n)] = tw[n, : c.used, :]
-    for m in z_f.masks()[1:]:
-        z_f.pull(m)
-        hand_over(m)
+    for m in z_f[0].masks()[1:]:
+        for j, g in enumerate(z_f):
+            g.pull(m)
+            hand_over(j, m)
     early = len(net.copies)
-    for copy in a_cf:
+    for copy in a_cf[:-nn]:
         copy.wait_recv()
-    for z, r in enumerate(bands):
-        total = dot_nn(wf[0, z].reshape(tall, piece), chunk[0])
-        for j in range(1, nn):
-            total += dot_nn(wf[j, z].reshape(tall, piece), chunk[j])
-        settle(3, r, total, 3)
+    for j in range(nn):
+        a_cf[j - nn].wait_recv()
+        for z, r in enumerate(bands):
+            total = dot_nn(wf[j, z].reshape(tall, piece), chunk[j])
+            if j:
+                total += pre[3, r, :]
+            if j < nn - 1:
+                pre[3, r, :] = total
+            else:
+                settle(3, r, total, 3)
     layer(4, act.at[3], 4)
     layer(5, act.at[4], 5)
     f3a[:, lanes(n)] = act[5]
@@ -536,7 +550,6 @@
         Gather(net, net.narrow, order, lambda m, h=h: f3a.at[h, lanes(n ^ m)], act.at[5, h])
         for order, h in zip(orders, halves(hid))
     ]
-    a_tw = [send(tw.at[n ^ d, used], twa.at[used, lanes(n)], net.narrow(d)) for d in range(1, nn)]
     while s_part[0].step < len(near):
         for s in s_part:
             s.finish()
@@ -557,35 +570,61 @@
     sfore[...] = (part3[n, hid:, :].astype(F32) + land3[k3[1], hid:, :].astype(F32)).astype(BF16)
     layer_back(5, grads.at[0], 4, 1)
     layer_back(4, grads.at[1], 3, 2)
+    a_tw = [send(tw.at[n ^ d, used], twa.at[used, lanes(n)], net.narrow(d)) for d in range(1, nn)]
     r_cf = []
     for j in range(nn):
         gf[j] = dot_nt(grads[2], chunk[j]).astype(BF16).reshape(nc, 2, c.hw, piece)
         r_cf.append(send(gf.at[j, :, 1 - core], cf.at[j], net.sibling()))
+
+    def add_f(j):
+        for z in range(nc):
+            cf[j, z] = (gf[j, z, core].astype(F32) + cf[j, z].astype(F32)).astype(BF16)
+
+    def add_zf(j, e, k):
+        cf[j, chip ^ e] = (cf[j, chip ^ e].astype(F32) + zf[k, j].astype(F32)).astype(BF16)
+
+    def forward_f(j):
+        r_zf[j].finish()
+        r_zf[j].start()
+
+    r_zf = [
+        Scatter(
+            net, net.chips, back_far,
+            lambda e, j=j: cf.at[j, chip ^ e],
+            lambda k, j=j: zf.at[k, j],
+            lambda e, k, j=j: add_zf(j, e, k),
+        )
+        for j in range(nn)
+    ]
+    for j in range(nn):
+        r_cf[j].wait_recv()
+        add_f(j)
+        r_zf[j].start()
     for copy in net.copies[:early]:
         copy.wait_send()
     put_weight(5, dot_nt(grads[0], act[4]))
     put_weight(4, dot_nt(grads[1], act[3]))
     inner, outer = ds(c.off[4], c.off[-1] - c.off[4]), ds(0, c.off[4])
     r_ci = send(wmid.at[:, 1 - core, :, :, inner], cm.at[:, :, :, inner], net.sibling())
-
-    def add_f(j):
-        for z in range(nc):
-            cf[j, z] = (gf[j, z, core].astype(F32) + cf[j, z].astype(F32)).astype(BF16)
-
-    for j in range(nn):
-        r_cf[j].wait_recv()
-    each(nn, add_f)
-
-    def add_zf(e, k):
-        def body(j):
-            cf[j, chip ^ e] = (cf[j, chip ^ e].astype(F32) + zf[k, j].astype(F32)).astype(BF16)
-
-        each(nn, body)
-
-    r_zf = Scatter(net, net.chips, back_far, lambda e: cf.at[:, chip ^ e], lambda k: zf.at[k], add_zf)
-    r_zf.start()
+    c_ga.wait()
+    for copy in a_ga:
+        copy.wait_recv()
+    temp2[...] = jnp.zeros_like(temp2)
+
+    def resid_grad(j):
+        temp[:piece, :] = dot_tn(wf[j].reshape(hid, piece), grads[2])
+
+        def body(r, unit):
+            at = ds(r, unit)
+            x = land_g[j, at, :].astype(F32) + temp[at, :]
+            land_g[j, at, :] = jnp.where(row_mask(j, r, unit), x, 0).astype(BF16)
+
+        row_loop(piece, 144, body)
+        pull = (dot_tn(mix_b[j], land_g[j]) * -c.scale).astype(BF16)
+        temp2[...] += dot_tn(pick[j, :, :bw], pull)
+
+    each(nn // 2, resid_grad)
     pull_first(n_f3)
-    exchange_series(0)
     r_ci.wait_recv()
     for z in range(nc):
         both = wmid[z, core, :, :, inner].astype(F32) + cm[z, :, :, inner].astype(F32)
@@ -601,24 +640,8 @@
 
     r_zi = Scatter(net, net.chips, back_far, lambda e: cm.at[chip ^ e, :, :, inner], lambda k: zi.at[k], add_zi)
     r_zi.start()
-    c_ga.wait()
-    for copy in a_ga:
-        copy.wait_recv()
-    temp2[...] = jnp.zeros_like(temp2)
-
-    def resid_grad(j):
-        temp[:piece, :] = dot_tn(wf[j].reshape(hid, piece), grads[2])
-
-        def body(r, unit):
-            at = ds(r, unit)
-            x = land_g[j, at, :].astype(F32) + temp[at, :]
-            land_g[j, at, :] = jnp.where(row_mask(j, r, unit), x, 0).astype(BF16)
-
-        row_loop(piece, 144, body)
-        pull = (dot_tn(mix_b[j], land_g[j]) * -c.scale).astype(BF16)
-        temp2[...] += dot_tn(pick[j, :, :bw], pull)
-
-    each(nn, resid_grad)
+    exchange_series(0)
+    each(nn - nn // 2, lambda i: resid_grad(i + nn // 2))
     dth = grads.at[3]
     dth[:bw, :] = temp2[...].astype(BF16)
     dth[bw:, :] = jnp.zeros_like(dth[bw:, :])
@@ -627,14 +650,14 @@
         grads[4, r, :] = (dot_nn(weight_rows(3, z), dth[...]) * slope(pre[2, r, :])).astype(BF16)
     layer_back(2, grads.at[4], 1, 5)
     layer_back(1, grads.at[5], 0, 6)
+    forward_f(0)
     pgb[...] = dot_tn(weight(0), grads[6]).astype(BF16)
     put_weight(3, dot_nt(act[2], dth[...]))
     put_weight(2, dot_nt(grads[4], act[1]))
     put_weight(1, dot_nt(grads[5], act[0]))
     put_weight(0, dot_nt(grads[6], pooled[...]))
     r_cm = send(wmid.at[:, 1 - core, :, :, outer], cm.at[:, :, :, outer], net.sibling())
-    bt[0, ds(4 + n, 1), :piece] = sums(bg[...])
-    bt[0, ds(4 + n, 1), pw : pw + part] = sums(fut[...])
+    forward_f(1)
     for k, slot_k in enumerate((6, 5, 4, 3, 2, 1, 0)):
         bt[0, k // 2 : k // 2 + 1, (k % 2) * hid : (k % 2 + 1) * hid] = sums(grads[slot_k])
     travel = [net.sibling()] + [net.narrow(b) for b in near] + [net.chips(b) for b in back_far]
@@ -650,6 +673,8 @@
         bt[k + 1] = bt[k] + bl[k]
 
     send_bias()
+    pull_rest(n_f3)
+    gk[...] = dot_nt(f3a[...], bg[...]).astype(BF16).reshape(nc, 2, c.hw, piece)
     r_cm.wait_recv()
     for z in range(nc):
         both = wmid[z, core, :, :, outer].astype(F32) + cm[z, :, :, outer].astype(F32)
@@ -669,23 +694,11 @@
     ]
     for s in r_nm:
         s.start()
-    exchange_series(1)
     add_bias()
     send_bias()
-    pull_rest(n_f3)
-    gk[...] = dot_nt(f3a[...], bg[...]).astype(BF16).reshape(nc, 2, c.hw, piece)
+    exchange_series(1)
     go[...] = dot_nt(f3a[...], fut[...]).astype(BF16).reshape(nc, 2, c.hw, part)
     r_ck = [send(gk.at[:, 1 - core], ck, net.sibling()), send(go.at[:, 1 - core], co, net.sibling())]
-    r_zf.finish()
-    r_zf.start()
-    r_zi.finish()
-    r_zi.start()
-    for copy in r_ck:
-        copy.wait_recv()
-    for z in range(nc):
-        ck[z] = (gk[z, core].astype(F32) + ck[z].astype(F32)).astype(BF16)
-        co[z] = (go[z, core].astype(F32) + co[z].astype(F32)).astype(BF16)
-
     def add_k(e, k):
         ck[chip ^ e] = (ck[chip ^ e].astype(F32) + zk[k].astype(F32)).astype(BF16)
 
@@ -706,7 +719,7 @@
             ser[j * piece + r : j * piece + r + unit, :] = x
 
     def outputs(k):
-        h = cuts[k]
+        h = parts[k]
         for copy in a_sa[k * (nn - 1) : (k + 1) * (nn - 1)]:
             copy.wait_recv()
         local(land_s.at[h], bg.at[h]).wait()
@@ -747,64 +760,78 @@
         )
         for order, h in zip(orders, halves(c.hw))
     ]
-    for s in r_zk:
-        s.start()
+    series_grad(0)
+    forward_f(2)
+    for j in range(1, nn - 1):
+        series_grad(j)
+    for j in range(3, nn):
+        forward_f(j)
+    for copy in r_ck:
+        copy.wait_recv()
+    for z in range(nc):
+        ck[z] = (gk[z, core].astype(F32) + ck[z].astype(F32)).astype(BF16)
+        co[z] = (go[z, core].astype(F32) + co[z].astype(F32)).astype(BF16)
     for s in r_nm:
         s.finish()
         s.start()
     add_bias()
     send_bias()
+    series_grad(nn - 1)
     exchange_series(2)
-    r_zi.finish()
-    r_ni = Scatter(net, net.narrow, near, lambda m: cm.at[chip, n ^ m, :, inner], lambda k: ni.at[k], add_ni)
-    r_ni.start()
-    for j in range(nn // 2):
-        series_grad(j)
-    r_zf.finish()
-    for s in r_nf:
-        s.start()
+    c_tid = local(ser, tid_out)
+    for copy in a_tw:
+        copy.wait_recv()
+    forecast()
+    c_pred = local(pred, pred_out)
+    outputs(0)
     for s in r_nm:
         s.finish()
     r_zm.start()
     add_bias()
     send_bias()
+    for s in r_zk:
+        s.start()
+    r_zi.finish()
+    r_zi.start()
+    for s in r_zf:
+        s.finish()
+    for s in r_nf:
+        s.start()
+    outputs(1)
     exchange_series(3)
-    for j in range(nn // 2, nn):
-        series_grad(j)
-    c_tid = local(ser, tid_out)
-    for copy in a_tw:
-        copy.wait_recv()
-    forecast()
-    c_pred = local(pred, pred_out)
-    for s in r_zk:
-        s.finish()
-        s.start()
-    outputs(0)
-    for s in r_nf:
-        s.finish()
-        s.start()
-    r_ni.finish()
-    r_ni.start()
-    outputs(1)
+    exchange_series(4)
     r_zm.finish()
     r_zm.start()
     add_bias()
     send_bias()
     outputs(2)
+    for s in r_zk:
+        s.finish()
+        s.start()
+    for s in r_nf:
+        s.finish()
+        s.start()
+    r_zi.finish()
+    r_ni = Scatter(net, net.narrow, near, lambda m: cm.at[chip, n ^ m, :, inner], lambda k: ni.at[k], add_ni)
+    r_ni.start()
+    add_bias()
+    obias[...] = bt[len(travel)]
     outputs(3)
+    r_zm.finish()
+    outputs(4)
+    r_ni.finish()
+    r_ni.start()
+    for s in r_nf:
+        s.finish()
+    of[...] = cf[n, chip].astype(F32)
     for s in r_zk:
         s.finish()
     ok[...] = ck[chip].astype(F32)
     oo[...] = co[chip].astype(F32)
     r_ni.finish()
-    for s in r_nf:
-        s.finish()
-    of[...] = cf[n, chip].astype(F32)
-    add_bias()
-    obias[...] = bt[len(travel)]
-    r_zm.finish()
     om[...] = cm[chip, n].astype(F32)
     drain()
+    assert len(net.copies) <= sends.shape[0] and len(owned) <= own.shape[0]
 
 
 def finish(c, *refs):
@@ -812,20 +839,20 @@
     held, (om, of, ok, oo, obias), given, sems = refs[29:32], refs[32:37], refs[37:55], refs[55]
     g1, v1, g2, v2, g3, v3, g4, v4, gf, vf1, g5, vf2, g6, vf3, gk, vk, go, vo = given
     arriving = [
-        pltpu.make_async_copy(src, dst, sems.at[24 + k])
+        pltpu.make_async_copy(src, dst, sems.at[48 + k])
         for k, (src, dst) in enumerate(zip(small_in, (om, of, ok, oo, obias)))
     ]
     leaving = [
-        pltpu.make_async_copy(src, dst, sems.at[29 + k]) for k, (src, dst) in enumerate(zip(given, small_out))
+        pltpu.make_async_copy(src, dst, sems.at[53 + k]) for k, (src, dst) in enumerate(zip(given, small_out))
     ]
     for copy in arriving:
         copy.start()
     pieces = []
     for a, (src, via, dst) in enumerate(zip(large_in, held, large_out)):
-        size = up(-(-src.shape[0] // 4), 16)
+        size = up(-(-src.shape[0] // 8), 16)
         for b, r in enumerate(range(0, src.shape[0], size)):
             h = pl.ds(r, min(size, src.shape[0] - r))
-            k = 8 * a + 2 * b
+            k = 16 * a + 2 * b
             pieces.append(
                 (
                     pltpu.make_async_copy(src.at[h], via.at[h], sems.at[k]),
@@ -898,7 +925,7 @@
     bs = (up(4 + nn, 8), max(2 * hid, pw + up(part, LANE)))
     stages = 1 + len(bits(nn)) + len(bits(nc))
     gathers = (nc - 1) + 2 * nc * (nn - 1) + 2 * (nn - 1) + 3 * (nc - 1) + 2 + 2 * nc
-    ncopies = gathers + 12 * (nn + nc) + 2 * nn * nc
+    ncopies = gathers + 12 * (nn + nc) + 6 * nn * nc
     qw = up(part, LANE)
     scratch = [
         V((nn, width, bw + fw), BF16),
@@ -992,7 +1019,7 @@
         out_specs=[anyspec] * 21,
         scratch_shapes=[V(x.shape, x.dtype) for x in (leftover, pred, tid, om, of, ok, oo, obias)]
         + [V(p.shape, F32) for p in params_like]
-        + [pltpu.SemaphoreType.DMA((48,))],
+        + [pltpu.SemaphoreType.DMA((72,))],
         compiler_params=pltpu.CompilerParams(vmem_limit_bytes=60 << 20),
     )(leftover, pred, tid, om, of, ok, oo, obias)
     return (outs[0].T, outs[1].T, outs[2].T) + tuple(outs[3:])
@@ -1334,6 +1361,7 @@
     hid, length = first_bias.shape[0], series.shape[1]
     paired = all(k & (k - 1) == 0 for k in (nn, nw)) and nw % 2 == 0
     paired = paired and len(bits(nn)) == 2 and len(bits(nw // 2)) == 2
+    paired = paired and length > 6 * LANE * nn
     return paired and hid % (16 * nn * nw) == 0 and length % (POOL * nn) == 0 and series.shape[0] % LANE == 0
 
 

time: 156 us -> 153 us (0.981)
  Pallas kernels: 155 us -> 152 us
    pallas_call x1, Pallas kernels: 148 us -> 146 us  [fast(): pl.pallas_call(functools.partial(whole, c), out_shape=(S((piece, nn * row...]
where the time goes in v5:
time: 153 us
  Pallas kernels  152 us (99%)
    pallas_call x1, Pallas kernels, fast(): pl.pallas_call(functools.partial(whole, c), out_shape=(S((piece, nn * row...  146 us
    pallas_call x1, Pallas kernels, fast(): pl.pallas_call(functools.partial(finish, c), out_shape=tuple((S(x.shape,...  6.64 us

profile of v5, /device:TPU:0, one launch (start us, length us, event | category | flops | bytes accessed | tf_op | source)
XLA Modules:
  0.0 153.1 jit_solution(7069597638255880964)
XLA Ops:
  0.7 145.6 %shard_map.409 = (bf16[900,1536]{1,0:T(8,128)(2,1)}, f32[180,1536]{1,0:T(8,128)}, bf16[3600,384]{1,0:T(8,128)(2,1)}, f32[16,3584]{1,0:T(8,128)}, f32[64,900]{1,0...) custom-call(s32[1536]{0:T(1024)} %refs_0_.1, ...), custom_call_target="tpu_custom_call" | custom-call | tf_op jit(solution)/shard_map/pallas_call | solution.py:991
  146.3 6.6 %shard_map.410 = (bf16[900,1536]{1,0:T(8,128)(2,1)}, f32[180,1536]{1,0:T(8,128)}, bf16[3600,384]{1,0:T(8,128)(2,1)}, f32[16,900]{1,0:T(8,128)}, f32[512]{0:T(512...) custom-call(bf16[900,1536]{1,0:T(8,128)(2,1)} %get-tuple-element.50., ...), custom_call_target="tpu_custom_call" | custom-call | tf_op jit(solution)/shard_map/pallas_call | solution.py:1014

commit v6 on v5

--- a/solution.py
+++ b/solution.py
@@ -673,8 +673,6 @@
         bt[k + 1] = bt[k] + bl[k]
 
     send_bias()
-    pull_rest(n_f3)
-    gk[...] = dot_nt(f3a[...], bg[...]).astype(BF16).reshape(nc, 2, c.hw, piece)
     r_cm.wait_recv()
     for z in range(nc):
         both = wmid[z, core, :, :, outer].astype(F32) + cm[z, :, :, outer].astype(F32)
@@ -696,6 +694,8 @@
         s.start()
     add_bias()
     send_bias()
+    pull_rest(n_f3)
+    gk[...] = dot_nt(f3a[...], bg[...]).astype(BF16).reshape(nc, 2, c.hw, piece)
     exchange_series(1)
     go[...] = dot_nt(f3a[...], fut[...]).astype(BF16).reshape(nc, 2, c.hw, part)
     r_ck = [send(gk.at[:, 1 - core], ck, net.sibling()), send(go.at[:, 1 - core], co, net.sibling())]

time: 153 us -> 152 us (level)
  no operation moved by 1% of the time
where the time goes in v6:
time: 152 us
  Pallas kernels  151 us (99%)
    pallas_call x1, Pallas kernels, fast(): pl.pallas_call(functools.partial(whole, c), out_shape=(S((piece, nn * row...  144 us
    pallas_call x1, Pallas kernels, fast(): pl.pallas_call(functools.partial(finish, c), out_shape=tuple((S(x.shape,...  6.64 us

profile of v6, /device:TPU:0, one launch (start us, length us, event | category | flops | bytes accessed | tf_op | source)
XLA Modules:
  0.0 151.8 jit_solution(5979805362839863564)
XLA Ops:
  0.7 144.3 %shard_map.409 = (bf16[900,1536]{1,0:T(8,128)(2,1)}, f32[180,1536]{1,0:T(8,128)}, bf16[3600,384]{1,0:T(8,128)(2,1)}, f32[16,3584]{1,0:T(8,128)}, f32[64,900]{1,0...) custom-call(s32[1536]{0:T(1024)} %refs_0_.1, ...), custom_call_target="tpu_custom_call" | custom-call | tf_op jit(solution)/shard_map/pallas_call | solution.py:991
  145.0 6.6 %shard_map.410 = (bf16[900,1536]{1,0:T(8,128)(2,1)}, f32[180,1536]{1,0:T(8,128)}, bf16[3600,384]{1,0:T(8,128)(2,1)}, f32[16,900]{1,0:T(8,128)}, f32[512]{0:T(512...) custom-call(bf16[900,1536]{1,0:T(8,128)(2,1)} %get-tuple-element.50., ...), custom_call_target="tpu_custom_call" | custom-call | tf_op jit(solution)/shard_map/pallas_call | solution.py:1014
